TPU v7x, 512 devices: a whole 4x8x8 slice. The times are simulated.
512 devices in a mesh: grp: 32 (over y, x), mlp: 16 (over z, core).
Axes of the slice: x: 4, y: 8, z: 8, core: 2. Of those that a mesh axis runs over, the one named last changes fastest.
Arguments:
- queries: bfloat16 [32, 128, 4096], P('grp'), may hold values from -70 to 70
- fresh_kv: bfloat16 [32, 128, 1024], P('grp', 'mlp'), may hold values from -5 to 5
- kv_pages: bfloat16 [32, 32, 128, 1024], P('grp', 'mlp'), may hold values from -5 to 5
- residual: bfloat16 [32, 128, 4096], P('grp'), may hold values from -3 to 3
- norm_gain: float32 [4096], replicated, may hold values from 0.5 to 1.5
- out_weight: bfloat16 [4096, 4096], P('mlp', 'grp'), may hold values from -0.09375 to 0.09375
- gate_weight: bfloat16 [4096, 6144], P('grp', 'mlp'), may hold values from -0.09375 to 0.09375
- up_weight: bfloat16 [4096, 6144], P('grp', 'mlp'), may hold values from -0.09375 to 0.09375
- down_weight: bfloat16 [6144, 4096], P('mlp', 'grp'), may hold values from -0.078125 to 0.078125
- page_table: int32 [32, 16, 12], P('grp'), may hold values from -1 to 31, as said below
- shared_pages: int32 [32, 4], P('grp'), may hold values from 0 to 31, as said below
- cache_lens: int32 [32, 16], P('grp'), may hold values from 513 to 2048, as said below
- prefill_offsets: int32 [32], P('grp'), may hold values from 1 to 512
Outputs:
- layer_out: bfloat16 [32, 128, 4096], P('grp', 'mlp')
Inputs may be any that keep to these rules, and one draw needn't show every extreme that they name: `page_table`: row d lists the pool pages that hold decode d's tokens after the shared prompt, in order, and -1 after its last page; no page appears twice in a group, and none is also a shared page. `shared_pages`: the pool pages of the group's shared prompt in order; they are the first 4 pages of every request of the group. `cache_lens`: decode d's cached tokens fill exactly its listed pages after the 4 shared pages; in every group one decode has the most.
All inputs are finite; a program needn't handle non-finite values.
Results may differ from a plain program's by a relative error of at most 0.029.
Values may be sent and summed in bfloat16 or wider, within the bound.
No kernel may reach another device: no remote copies, remote signals or barrier semaphores. Data moves between devices by JAX's collectives and lax.ppermute only.
A program may use at most 128 MiB of HBM per device.

v0:
```python
import jax
import jax.numpy as jnp
from jax import lax
from jax.sharding import PartitionSpec as P

HEADS = 32
KV_HEADS = 4
HEAD = 128
PAGE = 128
SHARED_PAGES = 4
PRIVATE_PAGES = 12
DECODES = 16
PREFILL = 112
ROWS = 128


NEG_FILL = -1e30
EPSILON = 1e-05


def merged(shard, axis, combine):
    everything = jax.tree.map(lambda part: lax.all_gather(part, axis), shard)
    leading = jax.tree.map(lambda part: part[0], everything)

    def step(k, so_far):
        return combine(so_far, jax.tree.map(lambda part: part[k], everything))

    return lax.fori_loop(1, lax.axis_size(axis), step, leading)


def page_layout(page_ids, table_group, shared_group):
    shared_match = shared_group[None, :] == page_ids[:, None]
    is_shared = jnp.any(shared_match, axis=1)
    shared_slot = jnp.sum(
        jnp.where(shared_match, jnp.arange(SHARED_PAGES, dtype=jnp.int32)[None, :], 0),
        axis=1,
        dtype=jnp.int32,
    )
    own_match = table_group[None, :, :] == page_ids[:, None, None]
    owner_id = (
        jnp.sum(
            jnp.where(own_match, jnp.arange(DECODES, dtype=jnp.int32)[None, :, None] + 1, 0),
            axis=(1, 2),
            dtype=jnp.int32,
        )
        - 1
    )
    own_slot = jnp.sum(
        jnp.where(own_match, jnp.arange(PRIVATE_PAGES, dtype=jnp.int32)[None, None, :], 0),
        axis=(1, 2),
        dtype=jnp.int32,
    )
    page_base = jnp.where(is_shared, shared_slot * PAGE, (SHARED_PAGES + own_slot) * PAGE)
    key_pos = (page_base[:, None] + jnp.arange(PAGE, dtype=jnp.int32)[None, :]).reshape(-1)
    key_shared = jnp.repeat(is_shared, PAGE)
    key_owner = jnp.repeat(jnp.where(is_shared, -1, owner_id), PAGE)
    return (key_pos, key_shared, key_owner)


def row_layout(lens_group, offset_value):
    row_ids = jnp.arange(ROWS, dtype=jnp.int32)
    is_prefill = row_ids < PREFILL
    decode_id = jnp.where(is_prefill, -2, row_ids - PREFILL)
    picked = decode_id[:, None] == jnp.arange(DECODES, dtype=jnp.int32)[None, :]
    decode_limit = jnp.sum(jnp.where(picked, lens_group[None, :], 0), axis=1, dtype=jnp.int32)
    limit = jnp.where(is_prefill, offset_value, decode_limit)
    return (row_ids, is_prefill, decode_id, limit)


def cache_visible(key_pos, key_shared, key_owner, decode_id, limit):
    belongs = key_shared[None, :] | (key_owner[None, :] == decode_id[:, None])
    return belongs & (key_pos[None, :] < limit[:, None])


def fresh_visible(key_rows, row_ids, is_prefill):
    before = (key_rows[None, :] < PREFILL) & (key_rows[None, :] <= row_ids[:, None])
    return jnp.where(is_prefill[:, None], before, key_rows[None, :] == row_ids[:, None])


def rms_norm(values, norm_gain):
    return (
        values * lax.rsqrt(jnp.mean(values * values, axis=1, keepdims=True) + EPSILON) * norm_gain
    ).astype(jnp.bfloat16)


def combine_parts(earlier_part, later_part):
    peak_one, total_one, mixed_one = earlier_part
    peak_two, total_two, mixed_two = later_part
    row_peak = jnp.maximum(peak_one, peak_two)
    factor_one = jnp.exp(peak_one - row_peak)
    factor_two = jnp.exp(peak_two - row_peak)
    row_total = total_one * factor_one + total_two * factor_two
    row_number, head_number = row_peak.shape
    weighted = (
        mixed_one.reshape(row_number, head_number, -1) * factor_one[:, :, None]
        + mixed_two.reshape(row_number, head_number, -1) * factor_two[:, :, None]
    )
    return (row_peak, row_total, weighted.reshape(row_number, -1))


def local(
    queries,
    fresh_kv,
    kv_pages,
    residual,
    norm_gain,
    out_weight,
    gate_weight,
    up_weight,
    down_weight,
    page_table,
    shared_pages,
    cache_lens,
    prefill_offsets,
):
    out_rows, gate_cols, up_cols, down_rows = (
        lax.all_gather(out_weight, "grp", axis=1, tiled=True),
        lax.all_gather(gate_weight, "grp", axis=0, tiled=True),
        lax.all_gather(up_weight, "grp", axis=0, tiled=True),
        lax.all_gather(down_weight, "grp", axis=1, tiled=True),
    )
    mlp_index = lax.axis_index("mlp")
    pool_pages = kv_pages.shape[1]
    own_count = fresh_kv.shape[1]
    page_ids = mlp_index * pool_pages + jnp.arange(pool_pages, dtype=jnp.int32)
    key_rows = mlp_index * own_count + jnp.arange(own_count, dtype=jnp.int32)
    key_pos, key_shared, key_owner = page_layout(page_ids, page_table[0], shared_pages[0])
    row_ids, is_prefill, decode_id, limit = row_layout(cache_lens[0], prefill_offsets[0])
    cache_seen = cache_visible(key_pos, key_shared, key_owner, decode_id, limit)
    fresh_seen = fresh_visible(key_rows, row_ids, is_prefill)
    cached = kv_pages[0].reshape(pool_pages * PAGE, 2, KV_HEADS, HEAD)
    fresh = fresh_kv[0].reshape(own_count, 2, KV_HEADS, HEAD)
    grouped = HEADS // KV_HEADS
    query_heads = queries[0].reshape(ROWS, KV_HEADS, grouped, HEAD)
    score_scale = HEAD ** (-0.5)
    peak_list = []
    total_list = []
    mixed_list = []
    for head_index in range(KV_HEADS):
        query_block = query_heads[:, head_index]
        cache_scores = (
            jnp.einsum(
                "rgh,kh->rgk",
                query_block,
                cached[:, 0, head_index],
                preferred_element_type=jnp.float32,
            )
            * score_scale
        )
        fresh_scores = (
            jnp.einsum(
                "rgh,kh->rgk",
                query_block,
                fresh[:, 0, head_index],
                preferred_element_type=jnp.float32,
            )
            * score_scale
        )
        cache_scores = jnp.where(cache_seen[:, None, :], cache_scores, NEG_FILL)
        fresh_scores = jnp.where(fresh_seen[:, None, :], fresh_scores, NEG_FILL)
        row_peak = jnp.maximum(jnp.max(cache_scores, axis=2), jnp.max(fresh_scores, axis=2))
        cache_exps = jnp.where(
            cache_seen[:, None, :], jnp.exp(cache_scores - row_peak[:, :, None]), 0.0
        )
        fresh_exps = jnp.where(
            fresh_seen[:, None, :], jnp.exp(fresh_scores - row_peak[:, :, None]), 0.0
        )
        row_total = jnp.sum(cache_exps, axis=2) + jnp.sum(fresh_exps, axis=2)
        weighted = jnp.einsum(
            "rgk,kh->rgh",
            cache_exps.astype(jnp.bfloat16),
            cached[:, 1, head_index],
            preferred_element_type=jnp.float32,
        )
        weighted = weighted + jnp.einsum(
            "rgk,kh->rgh",
            fresh_exps.astype(jnp.bfloat16),
            fresh[:, 1, head_index],
            preferred_element_type=jnp.float32,
        )
        peak_list.append(row_peak)
        total_list.append(row_total)
        mixed_list.append(weighted)
    row_peak = jnp.stack(peak_list, axis=1).reshape(ROWS, HEADS)
    row_total = jnp.stack(total_list, axis=1).reshape(ROWS, HEADS)
    weighted = jnp.stack(mixed_list, axis=1).reshape(ROWS, HEADS * HEAD)
    row_peak, row_total, weighted = merged((row_peak, row_total, weighted), "mlp", combine_parts)
    attended = (
        (weighted.reshape(ROWS, HEADS, HEAD) / row_total[:, :, None])
        .reshape(ROWS, HEADS * HEAD)
        .astype(jnp.bfloat16)
    )
    feature_count = out_rows.shape[0]
    own_features = lax.dynamic_slice_in_dim(attended, mlp_index * feature_count, feature_count, 1)
    row_begin = mlp_index * own_count
    projected = lax.psum(
        jnp.dot(own_features, out_rows, preferred_element_type=jnp.float32).astype(jnp.bfloat16),
        "mlp",
    ).astype(jnp.float32)
    updated = residual[0].astype(jnp.float32) + projected
    normed = rms_norm(updated, norm_gain)
    carried_rows = lax.dynamic_slice_in_dim(updated, row_begin, own_count, 0)
    gate_act = jnp.dot(normed, gate_cols, preferred_element_type=jnp.float32)
    up_act = jnp.dot(normed, up_cols, preferred_element_type=jnp.float32)
    hidden = (jax.nn.silu(gate_act) * up_act).astype(jnp.bfloat16)
    returned = lax.psum_scatter(
        jnp.dot(hidden, down_rows, preferred_element_type=jnp.float32).astype(jnp.bfloat16),
        "mlp",
        scatter_dimension=0,
        tiled=True,
    ).astype(jnp.float32)
    return (carried_rows + returned).astype(jnp.bfloat16)[None]


def solution(mesh):
    placed = (
        P("grp", None, None),
        P("grp", "mlp", None),
        P("grp", "mlp", None, None),
        P("grp", None, None),
        P(),
        P("mlp", "grp"),
        P("grp", "mlp"),
        P("grp", "mlp"),
        P("mlp", "grp"),
        P("grp", None, None),
        P("grp", None),
        P("grp", None),
        P("grp"),
    )
    return jax.shard_map(
        local, mesh=mesh, in_specs=placed, out_specs=P("grp", "mlp", None), check_vma=False
    )
```

profile of v0, /device:TPU:1, one launch (start us, length us, event | category | flops | bytes accessed | tf_op | source)
XLA Modules:
  0.0 784.7 jit_solution(5587190281900795073)
XLA Ops:
  6.6 0.9 compare_reduce_fusion
  7.5 0.8 fusion.85
  8.3 1.6 copy.59
  10.1 0.8 fusion.107
  14.3 1.6 fusion.99
  16.5 1.0 fusion.106
  17.5 1.9 fusion.104
  19.4 1.8 copy.89
  21.2 2.0 fusion.102
  23.2 0.9 copy.90
  24.1 2.9 fusion.100
  28.2 1.0 fusion.10
  29.7 1.0 fusion.9
  31.2 0.9 fusion.8
  32.6 0.9 fusion.7
  33.8 1.8 copy.72
  37.2 2.4 fusion.17
  39.7 25.8 %all_gather.22 = f32[16,128,32]{1,2,0:T(8,128)S(1)} all-gather(f32[1,128,32]{1,2,0:T(8,128)S(1)} %maximum_bitcast_fusion.1), channel_id=1, replica_groups=mesh['grp'=32,'mlp'=16] {'mlp'}, dimensions={0}, use_global_device_ids=true | all-gather | bytes 278528 | tf_op jit(solution)/shard_map/all_gather | solution.py:22
  65.5 16.6 %all_gather.21 = f32[16,128,32]{1,2,0:T(8,128)S(1)} all-gather(f32[1,128,32]{1,2,0:T(8,128)S(1)} %maximum_bitcast_fusion), channel_id=1, replica_groups=mesh['grp'=32,'mlp'=16] {'mlp'}, dimensions={0}, use_global_device_ids=true | all-gather | bytes 278528 | tf_op jit(solution)/shard_map/all_gather | solution.py:22
  82.3 139.0 %all-gather.6.cloned.1.call-done = f32[16,128,4096]{2,1,0:T(8,128)} async-done(((f32[1,128,4096]{2,1,0:T(8,128)}), f32[16,128,4096]{2,1,0:T(8,128)}) %all-gather.6.cloned.1.call-update) | async-done | bytes 33554448 | tf_op jit(solution)/shard_map/all_gather | solution.py:22
  221.3 1.7 slice_bitcast_fusion
  223.1 108.8 %while.19 = (s32[]{:T(128)}, f32[128,32]{1,0:T(8,128)S(1)}, f32[128,32]{1,0:T(8,128)S(1)}, f32[128,4096]{1,0:T(8,128)S(1)}, f32[16,128,32]{1,2,0:T(8,128)S(1)}, ...) while((s32[]{:T(128)}, f32[128,32]{1,0:T(8,128)S(1)}, ...), condition=%wide.region_22.23_spmd, body=%wide.region_21.22_spmd.sunk | while | flops 1597445 | bytes 14975127 | solution.py:28
  224.6 5.7 fusion.115
  231.8 5.7 fusion.115
  239.1 5.7 fusion.115
  246.3 5.7 fusion.115
  253.6 5.7 fusion.115
  260.9 5.7 fusion.115
  268.1 5.7 fusion.115
  275.4 5.7 fusion.115
  282.6 5.7 fusion.115
  289.9 5.7 fusion.115
  297.1 5.7 fusion.115
  304.4 5.7 fusion.115
  311.7 5.7 fusion.115
  318.9 5.7 fusion.115
  326.2 5.7 fusion.115
  332.5 3.0 copy.115
  335.5 3.2 convolution_convert_fusion.1
  340.5 113.4 %all-reduce.2.cloned.1.call-done = bf16[128,4096]{1,0:T(8,128)(2,1)} async-done(((bf16[128,4096]{1,0:T(8,128)(2,1)}), bf16[128,4096]{1,0:T(8,128)(2,1)}) %all-reduce.2.cloned.1.call-update) | async-done | bytes 1048592 | tf_op jit(solution)/shard_map/psum | solution.py:196
  453.9 3.0 convert_add_fusion
  456.9 81.9 %all-gather.10.cloned.1.call-done = bf16[4096,384]{1,0:T(8,128)(2,1)} async-done(((bf16[128,384]{1,0:T(8,128)(2,1)}), bf16[4096,384]{1,0:T(8,128)(2,1)}) %all-gather.10.cloned.1.call-update) | async-done | bytes 3145744 | tf_op jit(solution)/shard_map/all_gather | solution.py:118
  538.8 2.6 fusion.97
  541.5 83.0 %all-gather.12.cloned.1.call-done = bf16[4096,384]{1,0:T(8,128)(2,1)} async-done(((bf16[128,384]{1,0:T(8,128)(2,1)}), bf16[4096,384]{1,0:T(8,128)(2,1)}) %all-gather.12.cloned.1.call-update) | async-done | bytes 3145744 | tf_op jit(solution)/shard_map/all_gather | solution.py:119
  624.4 85.3 %all-gather.14.cloned.1.call-done = bf16[384,4096]{1,0:T(8,128)(2,1)} async-done(((bf16[384,128]{1,0:T(8,128)(2,1)}), bf16[384,4096]{1,0:T(8,128)(2,1)}) %all-gather.14.cloned.1.call-update) | async-done | bytes 3145744 | tf_op jit(solution)/shard_map/all_gather | solution.py:120
  709.7 5.3 convolution_convert_fusion
  715.0 61.2 %reduce-scatter.2.cloned.1.call-done = bf16[8,4096]{1,0:T(8,128)(2,1)} async-done(((bf16[128,4096]{1,0:T(8,128)(2,1)}), bf16[8,4096]{1,0:T(8,128)(2,1)}) %reduce-scatter.2.cloned.1.call-update) | async-done | bytes 65552 | tf_op jit(solution)/shard_map/reduce_scatter | solution.py:206
  776.2 1.6 fusion.51
  (190 shorter events, 32.4 us)
Async XLA Ops:
  6.5 3.5 copy-start.16
  6.5 6.6 copy-start.15
  6.5 7.4 copy-start.8
  6.5 214.8 %all-gather.6.cloned.1.call-start = ((), (), s32[]{:S(2)}) async-start(), calls=%async_computation.1 | async-start | bytes 35651584 | tf_op jit(solution)/shard_map/all_gather | solution.py:22
  10.0 7.5 copy-start.7
  11.7 4.6 copy-start.20
  19.4 9.8 %copy-start.2 = (f32[128,8,256]{2,0,1:T(8,128)}, f32[128,8,256]{2,0,1:T(8,128)S(1)}, u32[]{:S(2)}) copy-start(f32[128,8,256]{2,0,1:T(8,128)S(1)} %get-tuple-element.256) | copy-start | bytes 3145732
  23.2 7.6 copy-start.4
  24.1 5.2 copy-start.10
  27.1 2.1 copy-start.19
  27.8 1.9 copy-start.11
  28.2 2.5 copy-start.18
  28.2 2.6 copy-start.9
  29.3 1.9 copy-start.12
  29.7 2.5 copy-start.17
  29.7 2.5 copy-start.6
  30.8 1.8 copy-start.13
  35.6 1.2 copy-start.3
  35.6 1.5 copy-start.5
  35.7 299.8 %all-gather.8.cloned.1.call-start = ((), (), s32[]{:S(2)}) async-start(), calls=%async_computation.2 | async-start | bytes 2162688 | tf_op jit(solution)/shard_map/all_gather | solution.py:117
  36.4 417.5 %all-reduce.2.cloned.1.call-start = ((), (), s32[]{:S(2)}) async-start(), calls=%async_computation.3 | async-start | bytes 2097152 | tf_op jit(solution)/shard_map/psum | solution.py:196
  335.5 118.4 %copy-start = (bf16[1,128,4096]{2,1,0:T(8,128)(2,1)S(1)}, bf16[1,128,4096]{2,1,0:T(8,128)(2,1)}, u32[]{:S(2)}) copy-start(bf16[1,128,4096]{2,1,0:T(8,128)(2,1)} %param.18) | copy-start | bytes 3145732
  338.7 200.1 %all-gather.10.cloned.1.call-start = ((), (), s32[]{:S(2)}) async-start(), calls=%async_computation.4 | async-start | bytes 3244032 | tf_op jit(solution)/shard_map/all_gather | solution.py:118
  339.3 285.1 %all-gather.12.cloned.1.call-start = ((), (), s32[]{:S(2)}) async-start(), calls=%async_computation.5 | async-start | bytes 3244032 | tf_op jit(solution)/shard_map/all_gather | solution.py:119
  339.9 369.8 %all-gather.14.cloned.1.call-start = ((), (), s32[]{:S(2)}) async-start(), calls=%async_computation.6 | async-start | bytes 3244032 | tf_op jit(solution)/shard_map/all_gather | solution.py:120
  340.5 198.3 %copy-start.14 = (f32[4096]{0:T(1024)S(1)}, f32[4096]{0:T(1024)}, u32[]{:S(2)}) copy-start(f32[4096]{0:T(1024)} %param.19) | copy-start | bytes 49156
  340.5 435.7 %reduce-scatter.2.cloned.1.call-start = ((), (), s32[]{:S(2)}) async-start(), calls=%async_computation.7 | async-start | bytes 1114112 | tf_op jit(solution)/shard_map/reduce_scatter | solution.py:206
  453.9 84.9 %copy-start.1 = (bf16[128,4096]{1,0:T(8,128)(2,1)S(1)}, bf16[128,4096]{1,0:T(8,128)(2,1)}, u32[]{:S(2)}) copy-start(bf16[128,4096]{1,0:T(8,128)(2,1)} %all-reduce.2.cloned.1.call-done) | copy-start | bytes 3145732
Sparse Core Ops, SparseCore 0:
  35.8 185.4 all-gather.5
  224.4 74.5 all-gather.7
  338.9 115.0 all-reduce.1
  457.4 81.3 all-gather.9
  542.3 82.0 all-gather.11
  627.8 81.8 all-gather.13
  715.1 61.0 reduce-scatter.1
where the time goes:
time: 788 us; the launch traced here: 785 us
  waiting for transfers between devices  566 us (72%)
  other arithmetic  97.4 us (12%)
  blocking collectives  42.4 us (5%)
  local copies, waits for them, and re-layouts  35.8 us (5%)
  matrix products  27.6 us (4%)
  between operations  14.6 us (2%)
    all_gather x1, waiting for transfers between devices, merged(): everything = jax.tree.map(lambda part: lax.all_gather(part, axis), shard)  139 us
    psum x1, waiting for transfers between devices, local(): lax.psum(jnp.dot(own_features, out_rows, preferred_element_type=jnp.float...  113 us
    add x15, other arithmetic, combine_parts(): mixed_one.reshape(row_number, head_number, -1) * factor_one[:, :, None]  86.1 us
    all_gather x1, waiting for transfers between devices, local(): lax.all_gather(down_weight, 'grp', axis=1, tiled=True)  85.3 us
    all_gather x1, waiting for transfers between devices, local(): lax.all_gather(up_weight, 'grp', axis=0, tiled=True)  83 us
    all_gather x1, waiting for transfers between devices, local(): lax.all_gather(gate_weight, 'grp', axis=0, tiled=True)  81.9 us
    reduce_scatter x1, waiting for transfers between devices, local(): lax.psum_scatter(jnp.dot(hidden, down_rows, preferred_element_type=jnp.fl...  61.2 us
    all_gather x2, blocking collectives, merged(): everything = jax.tree.map(lambda part: lax.all_gather(part, axis), shard)  42.4 us
  transfers between devices with their start and end apart: 7, of which 6 were waited for; matrix products, arithmetic and copies ran while one was open for 16% of the time, Pallas kernels for 0%

commit v1 on v0

v1 whole, which is shorter than its diff:
```python
import jax
import jax.numpy as jnp
from jax import lax
from jax.experimental import pallas as pl
from jax.experimental.pallas import tpu as pltpu
from jax.sharding import Mesh
from jax.sharding import PartitionSpec as P

HEAD = 128
PAGE = 128
SHARED_PAGES = 4
PRIVATE_PAGES = 12
DECODES = 16
PREFILL = 112
ROWS = 128
OWN_PAGES = 2
FRESH_PAD = 16
KEYS = OWN_PAGES * PAGE + FRESH_PAD
STATS = 16
NEG_FILL = -1e30
EPSILON = 1e-05
LONG = "y", "x", "z", "c"


def pieces(value):
    first = value.astype(jnp.bfloat16).astype(jnp.float32)
    rest = value - first
    second = rest.astype(jnp.bfloat16).astype(jnp.float32)
    return (first, second, rest - second)


def attention_kernel(
    place_ref, limit_ref, query_one, query_two, own_key, own_value, far_key, far_value, out_ref
):
    query = jnp.concatenate(
        [query_one[:, :HEAD], query_one[:, HEAD:], query_two[:, :HEAD], query_two[:, HEAD:]], axis=0
    )
    keys = jnp.concatenate([own_key[...], far_key[...]], axis=0)
    values = jnp.concatenate([own_value[...], far_value[...]], axis=0)
    scores = lax.dot_general(
        keys, query, (((1,), (1,)), ((), ())), preferred_element_type=jnp.float32
    ) * (HEAD ** (-0.5))
    token = lax.broadcasted_iota(jnp.int32, (PAGE, ROWS), 0)
    fresh = lax.broadcasted_iota(jnp.int32, (FRESH_PAD, ROWS), 0)
    row = lax.broadcasted_iota(jnp.int32, (FRESH_PAD, ROWS), 1)
    own_count = place_ref[3]
    seen = []
    for side in range(2):
        for page in range(OWN_PAGES):
            limit = limit_ref[pl.ds(side * OWN_PAGES + page, 1), :]
            seen.append((token < limit).astype(jnp.int32))
        key_row = place_ref[1 + side] + fresh
        before = jnp.where((key_row < PREFILL) & (key_row <= row), 1, 0)
        same = jnp.where(key_row == row, 1, 0)
        visible = jnp.where(row < PREFILL, before, same)
        seen.append(jnp.where(fresh < own_count, visible, 0))
    seen = jnp.concatenate(seen, axis=0)
    seen = jnp.concatenate([seen] * 4, axis=1) > 0
    scores = jnp.where(seen, scores, NEG_FILL)
    peak = jnp.max(scores, axis=0, keepdims=True)
    exps = jnp.where(seen, jnp.exp(scores - peak), 0.0)
    total = jnp.sum(exps, axis=0, keepdims=True)
    mixed = lax.dot_general(
        values,
        exps.astype(jnp.bfloat16),
        (((0,), (0,)), ((), ())),
        preferred_element_type=jnp.float32,
    )
    line = lax.broadcasted_iota(jnp.int32, (STATS, ROWS), 0)
    for half in range(2):
        stats = jnp.zeros((STATS, ROWS), jnp.float32)
        for head in range(2):
            column = (2 * half + head) * ROWS
            out_ref[half, pl.ds(head * HEAD, HEAD), :] = mixed[:, column : column + ROWS].astype(
                jnp.bfloat16
            )
            sent = pieces(peak[:, column : column + ROWS]) + pieces(
                total[:, column : column + ROWS]
            )
            for index, value in enumerate(sent):
                stats = jnp.where(line == 6 * head + index, value, stats)
        out_ref[half, pl.ds(2 * HEAD, STATS), :] = stats.astype(jnp.bfloat16)


def attention(place, limits, queries, own_kv, far_kv):
    kv_heads = own_kv.shape[1] // (2 * HEAD)
    chips = 2 * kv_heads

    def kv_spec(offset):
        return pl.BlockSpec((KEYS, HEAD), lambda j, place: (0, offset + j))

    return pl.pallas_call(
        attention_kernel,
        grid_spec=pltpu.PrefetchScalarGridSpec(
            num_scalar_prefetch=1,
            grid=(kv_heads,),
            in_specs=[
                pl.BlockSpec((2 * OWN_PAGES, ROWS), lambda j, place: (0, 0)),
                pl.BlockSpec((ROWS, 2 * HEAD), lambda j, place: (0, 4 * j + place[0])),
                pl.BlockSpec((ROWS, 2 * HEAD), lambda j, place: (0, 4 * j + 2 + place[0])),
                kv_spec(0),
                kv_spec(kv_heads),
                kv_spec(0),
                kv_spec(kv_heads),
            ],
            out_specs=pl.BlockSpec((2, 2 * HEAD + STATS, ROWS), lambda j, place: (j, 0, 0)),
        ),
        out_shape=jax.ShapeDtypeStruct((chips, 2 * HEAD + STATS, ROWS), jnp.bfloat16),
        compiler_params=pltpu.CompilerParams(vmem_limit_bytes=32 * 1024 * 1024),
        name="attention",
    )(place, limits, queries, queries, own_kv, own_kv, far_kv, far_kv)


def combine_kernel(parts_ref, out_ref):
    chips = parts_ref.shape[0]
    for head in range(2):
        peaks = []
        totals = []
        for source in range(chips):
            stats = parts_ref[source, pl.ds(2 * HEAD, STATS), :].astype(jnp.float32)
            base = 6 * head
            peaks.append(stats[base : base + 1] + stats[base + 1 : base + 2] + stats[base + 2 : base + 3])
            totals.append(
                stats[base + 3 : base + 4] + stats[base + 4 : base + 5] + stats[base + 5 : base + 6]
            )
        peak = peaks[0]
        for other in peaks[1:]:
            peak = jnp.maximum(peak, other)
        total = jnp.zeros_like(peak)
        mixed = jnp.zeros((HEAD, ROWS), jnp.float32)
        for source in range(chips):
            factor = jnp.exp(peaks[source] - peak)
            total = total + totals[source] * factor
            mixed = mixed + parts_ref[source, pl.ds(head * HEAD, HEAD), :].astype(jnp.float32) * factor
        attended = (mixed / total).astype(jnp.bfloat16)
        for copy in range(out_ref.shape[0]):
            out_ref[copy, pl.ds(head * HEAD, HEAD), :] = attended


def combine(parts, copies):
    return pl.pallas_call(
        combine_kernel,
        out_shape=jax.ShapeDtypeStruct((copies, 2 * HEAD, ROWS), jnp.bfloat16),
        compiler_params=pltpu.CompilerParams(vmem_limit_bytes=32 * 1024 * 1024),
        name="combine",
    )(parts)


def page_limits(page_ids, table, shared, lens, offset):
    shared_match = shared[None, :] == page_ids[:, None]
    is_shared = jnp.any(shared_match, axis=1)
    shared_slot = jnp.sum(
        jnp.where(shared_match, jnp.arange(SHARED_PAGES, dtype=jnp.int32)[None, :], 0), axis=1
    )
    own_match = table[None, :, :] == page_ids[:, None, None]
    decode = jnp.arange(DECODES, dtype=jnp.int32)[None, :, None] + 1
    owner = jnp.sum(jnp.where(own_match, decode, 0), axis=(1, 2)) - 1
    slot = jnp.arange(PRIVATE_PAGES, dtype=jnp.int32)[None, None, :]
    own_slot = jnp.sum(jnp.where(own_match, slot, 0), axis=(1, 2))
    base = jnp.where(is_shared, shared_slot, SHARED_PAGES + own_slot) * PAGE
    limit = jnp.concatenate([jnp.broadcast_to(offset, (PREFILL,)), lens])
    decode_id = jnp.arange(ROWS, dtype=jnp.int32) - PREFILL
    belongs = is_shared[:, None] | (
        (owner[:, None] == decode_id[None, :]) & (decode_id >= 0)[None, :]
    )
    return jnp.where(belongs, limit[None, :] - base[:, None], 0)


def swap(value):
    return lax.ppermute(value, "c", [(0, 1), (1, 0)])


def sum_to_rows(left, weights, core, contract):
    x_size, z_size = lax.axis_size("x"), lax.axis_size("z")
    half = weights.shape[0] // 2

    def product(which):
        piece = lax.dynamic_slice_in_dim(weights, which * half, half, 0)
        return lax.dot_general(
            left, piece, (((contract,), (1,)), ((), ())), preferred_element_type=jnp.float32
        ).reshape(x_size * ROWS, -1)

    far = swap(product(1 - core).astype(jnp.bfloat16))
    near = (product(core) + far.astype(jnp.float32)).astype(jnp.bfloat16)
    parts = lax.all_to_all(near, ("x", "z", "c"), 0, 0, tiled=True)
    rows = ROWS // (2 * z_size)
    parts = parts.reshape(x_size, z_size, 2, rows, half // HEAD, HEAD).astype(jnp.float32)
    summed = jnp.sum(parts, axis=1)
    return jnp.transpose(summed, (2, 1, 3, 0, 4)).reshape(rows, -1)


def local(
    queries,
    fresh_kv,
    kv_pages,
    residual,
    norm_gain,
    out_weight,
    gate_weight,
    up_weight,
    down_weight,
    page_table,
    shared_pages,
    cache_lens,
    prefill_offsets,
):
    y_size, x_size, z_size = lax.axis_size("y"), lax.axis_size("x"), lax.axis_size("z")
    core = lax.axis_index("c")
    mine = lax.axis_index("z") * 2 + core
    other = mine + 1 - 2 * core
    features = out_weight.shape[0]
    hidden_units = gate_weight.shape[1]
    own_rows = fresh_kv.shape[1]

    wide = lax.all_gather(
        jnp.concatenate([gate_weight, up_weight, out_weight.T, down_weight.T], axis=1),
        "y",
        axis=0,
        tiled=True,
    )
    joint = 2 * hidden_units

    own_kv = jnp.concatenate(
        [
            kv_pages.reshape(OWN_PAGES * PAGE, -1),
            fresh_kv[0],
            jnp.zeros((FRESH_PAD - own_rows, fresh_kv.shape[2]), jnp.bfloat16),
        ],
        axis=0,
    )
    far_kv = swap(own_kv)
    ids = jnp.arange(OWN_PAGES, dtype=jnp.int32)
    limits = page_limits(
        jnp.concatenate([mine * OWN_PAGES + ids, other * OWN_PAGES + ids]),
        page_table[0],
        shared_pages[0],
        cache_lens[0],
        prefill_offsets[0],
    )
    place = jnp.stack([core, mine * own_rows, other * own_rows, jnp.int32(own_rows)])
    parts = attention(place, limits, queries[0], own_kv, far_kv)
    parts = lax.all_to_all(parts, "z", 0, 0, tiled=True)
    attended = lax.all_to_all(combine(parts, x_size), "x", 0, 0, tiled=True)

    projected = sum_to_rows(attended, wide[:, joint : joint + features], core, 1)
    carried = lax.dynamic_slice_in_dim(residual[0], mine * own_rows, own_rows, 0)
    updated = carried.astype(jnp.float32) + projected
    normed = (
        updated
        * lax.rsqrt(jnp.mean(updated * updated, axis=1, keepdims=True) + EPSILON)
        * norm_gain
    ).astype(jnp.bfloat16)

    half = y_size // 2
    sent = jnp.transpose(normed.reshape(own_rows, 2, half, x_size, HEAD), (3, 1, 0, 2, 4))
    sent = jnp.broadcast_to(
        sent.reshape(x_size, 1, 2, own_rows, half * HEAD),
        (x_size, z_size, 2, own_rows, half * HEAD),
    ).reshape(x_size * ROWS, half * HEAD)
    near_rows = lax.all_to_all(sent, ("x", "z", "c"), 0, 0, tiled=True)
    far_rows = swap(near_rows)

    def partial(rows, which):
        piece = lax.dynamic_slice_in_dim(wide[:, :joint], which * half * HEAD, half * HEAD, 0)
        return jnp.dot(rows, piece, preferred_element_type=jnp.float32)

    gated = partial(near_rows, core) + partial(far_rows, 1 - core)
    gated = lax.all_to_all(gated.astype(jnp.bfloat16), "x", 0, 0, tiled=True)
    gated = jnp.sum(gated.reshape(x_size, ROWS, 2 * hidden_units).astype(jnp.float32), axis=0)
    gate_act, up_act = gated[:, :hidden_units], gated[:, hidden_units:]
    hidden = (jax.nn.silu(gate_act) * up_act).astype(jnp.bfloat16)
    hidden = jnp.broadcast_to(hidden[None], (x_size, ROWS, hidden_units))
    hidden = lax.all_to_all(hidden.reshape(x_size * ROWS, hidden_units), "x", 0, 0, tiled=True)

    returned = sum_to_rows(hidden, wide[:, joint + features :], core, 1)
    return (updated + returned).astype(jnp.bfloat16)[None]


def solution(mesh):
    cores = 2
    chips = mesh.shape["mlp"] // cores
    along = 4 if mesh.shape["grp"] % 16 == 0 else 2
    long_mesh = Mesh(
        mesh.devices.reshape(mesh.shape["grp"] // along, along, chips, cores), LONG
    )
    grp, mlp = ("y", "x"), ("z", "c")
    placed = (
        P(grp, None, None),
        P(grp, mlp, None),
        P(grp, mlp, None, None),
        P(grp, None, None),
        P(),
        P(mlp, grp),
        P(grp, mlp),
        P(grp, mlp),
        P(mlp, grp),
        P(grp, None, None),
        P(grp, None),
        P(grp, None),
        P(grp),
    )
    return jax.shard_map(
        local, mesh=long_mesh, in_specs=placed, out_specs=P(grp, mlp, None), check_vma=False
    )
```

time: 788 us -> 193 us (0.24)
  waiting for transfers between devices: 566 us -> 48.6 us
  other arithmetic: 97.4 us -> 9.94 us
  starting transfers between devices: 0.24 us -> 42.7 us
  local copies, waits for them, and re-layouts: 35.8 us -> 5.49 us
  matrix products: 27.6 us -> 3.57 us
  blocking collectives: 42.4 us -> 61.6 us
    all_gather x5 -> x1, waiting for transfers between devices: 389 us -> 6.77 us  [local(): lax.all_gather(jnp.concatenate([gate_weight, up_weight, out_weight.T, dow...]
    psum x1 -> x0, waiting for transfers between devices: 113 us -> none  [local(): lax.psum(jnp.dot(own_features, out_rows, preferred_element_type=jnp.float...]
    add x39 -> x2, other arithmetic: 90.1 us -> 0.01 us  [the longest x1 0.01 us: local(): other * OWN_PAGES + ids]
    all_to_all x0 -> x3, blocking collectives: none -> 61.6 us  [the longest x1 23.4 us: local(): near_rows = lax.all_to_all(sent, ('x', 'z', 'c'), 0, 0, tiled=True)]
    reduce_scatter x1 -> x0, waiting for transfers between devices: 61.2 us -> none  [local(): lax.psum_scatter(jnp.dot(hidden, down_rows, preferred_element_type=jnp.fl...]
    all_gather x2 -> x0, blocking collectives: 42.4 us -> none  [merged(): everything = jax.tree.map(lambda part: lax.all_gather(part, axis), shard)]
    all_to_all x0 -> x4, waiting for transfers between devices: none -> 38.2 us  [the longest x2 33 us: sum_to_rows(): parts = lax.all_to_all(near, ('x', 'z', 'c'), 0, 0, tiled=True)]
    dot_general x19 -> x6, matrix products: 27.6 us -> 3.57 us  [the longest x4 2.41 us: product(): lax.dot_general(left, piece, (((contract,), (1,)), ((), ())), preferred_e...]
  transfers between devices with their start and end apart: 7 -> 9, of which waited for: 6 -> 7; matrix products, arithmetic and copies ran while one was open for 16% -> 4% of each run, Pallas kernels for 0% -> 3%
where the time goes in v1:
time: 193 us; the launch traced here: 192 us
  blocking collectives  61.6 us (32%)
  waiting for transfers between devices  48.6 us (25%)
  starting transfers between devices  42.7 us (22%)
  between operations  14.4 us (7%)
  other arithmetic  9.94 us (5%)
  local copies, waits for them, and re-layouts  5.49 us (3%)
  Pallas kernels  5.31 us (3%)
  matrix products  3.57 us (2%)
    all_to_all x2, waiting for transfers between devices, sum_to_rows(): parts = lax.all_to_all(near, ('x', 'z', 'c'), 0, 0, tiled=True)  33 us
    all_to_all x1, blocking collectives, local(): near_rows = lax.all_to_all(sent, ('x', 'z', 'c'), 0, 0, tiled=True)  23.4 us
    all_to_all x1, blocking collectives, local(): parts = lax.all_to_all(parts, 'z', 0, 0, tiled=True)  22.3 us
    ppermute x4, starting transfers between devices, swap(): return lax.ppermute(value, 'c', [(0, 1), (1, 0)])  20.1 us
    all_to_all x1, blocking collectives, local(): gated = lax.all_to_all(gated.astype(jnp.bfloat16), 'x', 0, 0, tiled=True)  15.9 us
    all_to_all x2, starting transfers between devices, sum_to_rows(): parts = lax.all_to_all(near, ('x', 'z', 'c'), 0, 0, tiled=True)  15.2 us
    all_gather x1, waiting for transfers between devices, local(): lax.all_gather(jnp.concatenate([gate_weight, up_weight, out_weight.T, dow...  6.77 us
    all_to_all x1, waiting for transfers between devices, local(): lax.all_to_all(hidden.reshape(x_size * ROWS, hidden_units), 'x', 0, 0, ti...  5.29 us
  transfers between devices with their start and end apart: 9, of which 7 were waited for; matrix products, arithmetic and copies ran while one was open for 4% of the time, Pallas kernels for 3%

profile of v1, /device:TPU:1, one launch (start us, length us, event | category | flops | bytes accessed | tf_op | source)
XLA Modules:
  0.0 191.6 jit_solution(481906825547367110)
XLA Ops:
  6.6 1.0 copy.47
  7.6 1.0 copy.48
  8.7 1.7 pad_maximum_fusion
  10.4 0.1 pad.7.clone
  10.5 0.9 maximum_maximum_fusion.own_key.own_value
  11.4 8.8 %collective-permute-start = (bf16[272,1024]{1,0:T(8,128)(2,1)S(1)}, bf16[272,1024]{1,0:T(8,128)(2,1)S(1)}, u32[]{:S(2)}, u32[]{:S(2)}) collective-permute-start(bf16[272,1024]{1,0:T(8,128)(2,1)S(1)} %maximum_maximum_fusion.own_key.own_value), channel_id=1, source_target_pairs={{0,1},{1,0},{2,3},{3,2},{4,5},{5,4},{6,7},{7,6},{8,9},{9,8},{10,11... | collective-permute-start | bytes 1671176 | tf_op jit(solution)/shard_map/ppermute | solution.py:170
  20.9 0.1 concatenate.13
  21.0 0.1 pad_add_fusion.1
  21.0 0.2 compare_reduce_fusion
  21.2 0.2 fusion.19
  21.4 0.2 fusion.17
  21.6 0.1 pad_add_fusion.place_ref
  21.7 0.1 subtract_select_fusion.limit_ref
  21.8 4.5 %attention.1 = bf16[8,272,128]{2,1,0:T(8,128)(2,1)S(1)} custom-call(s32[4]{0:T(128)S(1)} %pad_add_fusion.place_ref, s32[4,128]{1,0:T(4,128)S(1)} %subtract_select_fusion.limit_ref, bf16[128,4096]{1,0:T(8,128)(2,1)S(1)} %bitcast.56, bf16[128,4096]{1,0:T(8,128)(2,1)S(1)} %bitcast.57, bf16[272,1024]{1,0:T(8,128)(2,1)S(1)} %maximum_maximum_fusion.own_key.own_value, ...), custom_call_target="tpu_custom_call" | custom-call | tf_op jit(solution)/shard_map/attention/pallas_call | solution.py:92
  26.3 22.3 %all_to_all.58.parts_ref = bf16[8,272,128]{2,1,0:T(8,128)(2,1)S(1)} all-to-all(bf16[8,272,128]{2,1,0:T(8,128)(2,1)S(1)} %attention.1), channel_id=1, replica_groups=mesh['y'=8,'x'=4,'z'=8,'c'=2] {'z'}, dimensions={0} | all-to-all | bytes 1114112 | tf_op jit(solution)/shard_map/all_to_all | solution.py:242
  48.6 0.9 combine.1
  49.5 4.0 %all-to-all-start.1 = ((bf16[4,256,128]{2,1,0:T(8,128)(2,1)}), bf16[4,256,128]{2,1,0:T(8,128)(2,1)S(1)}, u32[]{:S(2)}, u32[]{:S(2)}) async-start(bf16[4,256,128]{2,1,0:T(8,128)(2,1)} %combine.1), calls=%async_computation.1 | async-start | bytes 524288 | tf_op jit(solution)/shard_map/all_to_all | solution.py:243
  53.5 6.8 %all-gather.2.cloned.1.call-done = bf16[1024,1408]{1,0:T(8,128)(2,1)} async-done(((bf16[128,1408]{1,0:T(8,128)(2,1)}), bf16[1024,1408]{1,0:T(8,128)(2,1)}) %all-gather.2.cloned.1.call-update) | async-done | bytes 2883600 | tf_op jit(solution)/shard_map/all_gather | solution.py:215
  60.3 1.1 slice.21
  61.3 0.4 convolution_convert_fusion.1
  61.7 4.7 %collective-permute-start.1 = (bf16[512,512]{1,0:T(8,128)(2,1)S(1)}, bf16[512,512]{1,0:T(8,128)(2,1)S(1)}, u32[]{:S(2)}, u32[]{:S(2)}) collective-permute-start(bf16[512,512]{1,0:T(8,128)(2,1)S(1)} %bitcast.72), channel_id=1, source_target_pairs={{0,1},{1,0},{2,3},{3,2},{4,5},{5,4},{6,7},{7,6},{8,9},{9,8},{10,11... | collective-permute-start | bytes 1572872 | tf_op jit(solution)/shard_map/ppermute | solution.py:170
  66.4 0.3 fusion.11
  66.7 1.1 collective-permute-done.1
  67.9 1.0 fusion
  68.9 10.7 %all-to-all-start.2 = ((bf16[64,8,512]{2,1,0:T(8,128)(2,1)}), bf16[64,8,512]{2,1,0:T(8,128)(2,1)S(1)}, u32[]{:S(2)}, u32[]{:S(2)}) async-start(bf16[64,8,512]{2,1,0:T(8,128)(2,1)} %bitcast.15), calls=%async_computation.2 | async-start | bytes 1048576 | tf_op jit(solution)/shard_map/all_to_all | solution.py:185
  79.6 1.7 dynamic-slice_convert_fusion
  81.3 15.6 %all-to-all-done.2 = bf16[64,8,512]{2,1,0:T(8,128)(2,1)S(1)} async-done(((bf16[64,8,512]{2,1,0:T(8,128)(2,1)}), bf16[64,8,512]{2,1,0:T(8,128)(2,1)S(1)}, u32[]{:S(2)}, u32[]{:S(2)}) %all-to-all-start.2) | async-done | bytes 524320 | tf_op jit(solution)/shard_map/all_to_all | solution.py:185
  97.0 1.1 multiply_reduce_fusion
  98.0 1.0 fusion.16
  99.1 23.4 %all_to_all.59 = bf16[64,8,512]{2,1,0:T(8,128)(2,1)S(1)} all-to-all(bf16[64,8,512]{2,1,0:T(8,128)(2,1)S(1)} %bitcast.64), channel_id=1, replica_groups=mesh['y'=8,'x'=4,'z'=8,'c'=2] {'x','z','c'}, dimensions={0} | all-to-all | bytes 1048576 | tf_op jit(solution)/shard_map/all_to_all | solution.py:260
  122.5 2.2 %collective-permute-start.2 = (bf16[512,512]{1,0:T(8,128)(2,1)S(1)}, bf16[512,512]{1,0:T(8,128)(2,1)S(1)}, u32[]{:S(2)}, u32[]{:S(2)}) collective-permute-start(bf16[512,512]{1,0:T(8,128)(2,1)S(1)} %bitcast.65), channel_id=1, source_target_pairs={{0,1},{1,0},{2,3},{3,2},{4,5},{5,4},{6,7},{7,6},{8,9},{9,8},{10,11... | collective-permute-start | bytes 1572872 | tf_op jit(solution)/shard_map/ppermute | solution.py:170
  124.7 0.1 slice.22
  124.8 0.6 fusion.2
  125.4 0.9 collective-permute-done.2
  126.3 0.6 add_convert_fusion
  126.9 15.9 %all_to_all.60 = bf16[4,128,768]{2,1,0:T(8,128)(2,1)S(1)} all-to-all(bf16[4,128,768]{2,1,0:T(8,128)(2,1)S(1)} %bitcast.60), channel_id=1, replica_groups=mesh['y'=8,'x'=4,'z'=8,'c'=2] {'x'}, dimensions={0} | all-to-all | bytes 1572864 | tf_op jit(solution)/shard_map/all_to_all | solution.py:268
  142.8 0.1 convert_reduce_fusion
  142.9 0.8 broadcast_in_dim.78
  143.7 3.5 %all-to-all-start.5 = ((bf16[4,128,384]{2,1,0:T(8,128)(2,1)}), bf16[4,128,384]{2,1,0:T(8,128)(2,1)S(1)}, u32[]{:S(2)}, u32[]{:S(2)}) async-start(bf16[4,128,384]{2,1,0:T(8,128)(2,1)} %broadcast_in_dim.78), calls=%async_computation.5 | async-start | bytes 786432 | tf_op jit(solution)/shard_map/all_to_all | solution.py:273
  147.2 1.2 slice.25
  148.4 5.3 %all-to-all-done.5 = bf16[4,128,384]{2,1,0:T(8,128)(2,1)S(1)} async-done(((bf16[4,128,384]{2,1,0:T(8,128)(2,1)}), bf16[4,128,384]{2,1,0:T(8,128)(2,1)S(1)}, u32[]{:S(2)}, u32[]{:S(2)}) %all-to-all-start.5) | async-done | bytes 393248 | tf_op jit(solution)/shard_map/all_to_all | solution.py:273
  153.7 0.5 convolution_convert_fusion
  154.2 4.4 %collective-permute-start.3 = (bf16[512,512]{1,0:T(8,128)(2,1)S(1)}, bf16[512,512]{1,0:T(8,128)(2,1)S(1)}, u32[]{:S(2)}, u32[]{:S(2)}) collective-permute-start(bf16[512,512]{1,0:T(8,128)(2,1)S(1)} %convolution_convert_fusion), channel_id=1, source_target_pairs={{0,1},{1,0},{2,3},{3,2},{4,5},{5,4},{6,7},{7,6},{8,9},{9,8},{10,11... | collective-permute-start | bytes 1572872 | tf_op jit(solution)/shard_map/ppermute | solution.py:170
  158.6 1.5 collective-permute-done.3
  160.1 1.3 fusion.4
  161.3 4.4 %all-to-all-start.6 = ((bf16[64,8,512]{2,1,0:T(8,128)(2,1)}), bf16[64,8,512]{2,1,0:T(8,128)(2,1)S(1)}, u32[]{:S(2)}, u32[]{:S(2)}) async-start(bf16[64,8,512]{2,1,0:T(8,128)(2,1)} %fusion.4), calls=%async_computation.6 | async-start | bytes 1048576 | tf_op jit(solution)/shard_map/all_to_all | solution.py:185
  165.8 17.3 %all-to-all-done.6 = bf16[64,8,512]{2,1,0:T(8,128)(2,1)S(1)} async-done(((bf16[64,8,512]{2,1,0:T(8,128)(2,1)}), bf16[64,8,512]{2,1,0:T(8,128)(2,1)S(1)}, u32[]{:S(2)}, u32[]{:S(2)}) %all-to-all-start.6) | async-done | bytes 524320 | tf_op jit(solution)/shard_map/all_to_all | solution.py:185
  183.2 1.5 add_convert_fusion.2
  (34 shorter events, 0.4 us)
Async XLA Ops:
  6.5 4.0 %copy-start.2 = (bf16[1,2,128,1024]{3,2,1,0:T(8,128)(2,1)S(1)}, bf16[1,2,128,1024]{3,2,1,0:T(8,128)(2,1)}, u32[]{:S(2)}) copy-start(bf16[1,2,128,1024]{3,2,1,0:T(8,128)(2,1)} %param.15) | copy-start | bytes 1572868
  6.5 14.3 %copy-start.4 = (s32[1,16,12]{1,0,2:T(1,128)S(1)}, s32[1,16,12]{1,0,2:T(1,128)}, u32[]{:S(2)}) copy-start(s32[1,16,12]{1,0,2:T(1,128)} %param.22) | copy-start | bytes 2308
  6.5 14.3 %copy-start.5 = (s32[1,16]{1,0:T(1,128)S(1)}, s32[1,16]{1,0:T(1,128)}, u32[]{:S(2)}) copy-start(s32[1,16]{1,0:T(1,128)} %param.24) | copy-start | bytes 196
  6.5 14.5 %copy-start.6 = (s32[1,4]{1,0:T(1,128)S(1)}, s32[1,4]{1,0:T(1,128)}, u32[]{:S(2)}) copy-start(s32[1,4]{1,0:T(1,128)} %param.23) | copy-start | bytes 52
  6.5 15.2 %copy-start = (bf16[1,128,4096]{2,1,0:T(8,128)(2,1)S(1)}, bf16[1,128,4096]{2,1,0:T(8,128)(2,1)}, u32[]{:S(2)}) copy-start(bf16[1,128,4096]{2,1,0:T(8,128)(2,1)} %param.13) | copy-start | bytes 3145732
  6.5 53.7 %all-gather.2.cloned.1.call-start = ((), (), s32[]{:S(2)}) async-start(), calls=%async_computation.7 | async-start | bytes 3244032 | tf_op jit(solution)/shard_map/all_gather | solution.py:215
  11.4 10.4 %collective-permute-start = (bf16[272,1024]{1,0:T(8,128)(2,1)S(1)}, bf16[272,1024]{1,0:T(8,128)(2,1)S(1)}, u32[]{:S(2)}, u32[]{:S(2)}) collective-permute-start(bf16[272,1024]{1,0:T(8,128)(2,1)S(1)} %maximum_maximum_fusion.own_key.own_value), channel_id=1, source_target_pairs={{0,1},{1,0},{2,3},{3,2},{4,5},{5,4},{6,7},{7,6},{8,9},{9,8},{10,11... | collective-permute-start | bytes 1671176 | tf_op jit(solution)/shard_map/ppermute | solution.py:170
  49.5 11.9 %all-to-all-start.1 = ((bf16[4,256,128]{2,1,0:T(8,128)(2,1)}), bf16[4,256,128]{2,1,0:T(8,128)(2,1)S(1)}, u32[]{:S(2)}, u32[]{:S(2)}) async-start(bf16[4,256,128]{2,1,0:T(8,128)(2,1)} %combine.1), calls=%async_computation.1 | async-start | bytes 524288 | tf_op jit(solution)/shard_map/all_to_all | solution.py:243
  61.7 6.2 %collective-permute-start.1 = (bf16[512,512]{1,0:T(8,128)(2,1)S(1)}, bf16[512,512]{1,0:T(8,128)(2,1)S(1)}, u32[]{:S(2)}, u32[]{:S(2)}) collective-permute-start(bf16[512,512]{1,0:T(8,128)(2,1)S(1)} %bitcast.72), channel_id=1, source_target_pairs={{0,1},{1,0},{2,3},{3,2},{4,5},{5,4},{6,7},{7,6},{8,9},{9,8},{10,11... | collective-permute-start | bytes 1572872 | tf_op jit(solution)/shard_map/ppermute | solution.py:170
  66.7 12.9 %copy-start.3 = (f32[4096]{0:T(1024)S(1)}, f32[4096]{0:T(1024)}, u32[]{:S(2)}) copy-start(f32[4096]{0:T(1024)} %param.17) | copy-start | bytes 49156
  68.9 28.0 %all-to-all-start.2 = ((bf16[64,8,512]{2,1,0:T(8,128)(2,1)}), bf16[64,8,512]{2,1,0:T(8,128)(2,1)S(1)}, u32[]{:S(2)}, u32[]{:S(2)}) async-start(bf16[64,8,512]{2,1,0:T(8,128)(2,1)} %bitcast.15), calls=%async_computation.2 | async-start | bytes 1048576 | tf_op jit(solution)/shard_map/all_to_all | solution.py:185
  79.6 45.1 %copy-start.1 = (bf16[1024,1408]{1,0:T(8,128)(2,1)S(1)}, bf16[1024,1408]{1,0:T(8,128)(2,1)}, u32[]{:S(2)}) copy-start(bf16[1024,1408]{1,0:T(8,128)(2,1)} %all-gather.2.cloned.1.call-done) | copy-start | bytes 8650756
  122.5 3.8 %collective-permute-start.2 = (bf16[512,512]{1,0:T(8,128)(2,1)S(1)}, bf16[512,512]{1,0:T(8,128)(2,1)S(1)}, u32[]{:S(2)}, u32[]{:S(2)}) collective-permute-start(bf16[512,512]{1,0:T(8,128)(2,1)S(1)} %bitcast.65), channel_id=1, source_target_pairs={{0,1},{1,0},{2,3},{3,2},{4,5},{5,4},{6,7},{7,6},{8,9},{9,8},{10,11... | collective-permute-start | bytes 1572872 | tf_op jit(solution)/shard_map/ppermute | solution.py:170
  143.7 10.0 %all-to-all-start.5 = ((bf16[4,128,384]{2,1,0:T(8,128)(2,1)}), bf16[4,128,384]{2,1,0:T(8,128)(2,1)S(1)}, u32[]{:S(2)}, u32[]{:S(2)}) async-start(bf16[4,128,384]{2,1,0:T(8,128)(2,1)} %broadcast_in_dim.78), calls=%async_computation.5 | async-start | bytes 786432 | tf_op jit(solution)/shard_map/all_to_all | solution.py:273
  154.2 5.9 %collective-permute-start.3 = (bf16[512,512]{1,0:T(8,128)(2,1)S(1)}, bf16[512,512]{1,0:T(8,128)(2,1)S(1)}, u32[]{:S(2)}, u32[]{:S(2)}) collective-permute-start(bf16[512,512]{1,0:T(8,128)(2,1)S(1)} %convolution_convert_fusion), channel_id=1, source_target_pairs={{0,1},{1,0},{2,3},{3,2},{4,5},{5,4},{6,7},{7,6},{8,9},{9,8},{10,11... | collective-permute-start | bytes 1572872 | tf_op jit(solution)/shard_map/ppermute | solution.py:170
  161.3 21.8 %all-to-all-start.6 = ((bf16[64,8,512]{2,1,0:T(8,128)(2,1)}), bf16[64,8,512]{2,1,0:T(8,128)(2,1)S(1)}, u32[]{:S(2)}, u32[]{:S(2)}) async-start(bf16[64,8,512]{2,1,0:T(8,128)(2,1)} %fusion.4), calls=%async_computation.6 | async-start | bytes 1048576 | tf_op jit(solution)/shard_map/all_to_all | solution.py:185
Sparse Core Ops, SparseCore 0:
  10.5 49.6 all-gather.1

commit v2 on v1

v2 whole, which is shorter than its diff:
```python
import functools

import jax
import jax.numpy as jnp
from jax import lax
from jax.experimental import pallas as pl
from jax.experimental.pallas import tpu as pltpu
from jax.sharding import Mesh
from jax.sharding import PartitionSpec as P

HEAD = 128
PAGE = 128
SHARED_PAGES = 4
PRIVATE_PAGES = 12
DECODES = 16
PREFILL = 112
ROWS = 128
OWN_PAGES = 2
FRESH_PAD = 16
KEYS = OWN_PAGES * PAGE + FRESH_PAD
STATS = 16
NEG_FILL = -1e30
EPSILON = 1e-05
LONG = "y", "x", "z", "c"
LIMIT = pltpu.CompilerParams(vmem_limit_bytes=32 * 1024 * 1024)
WIDE_LIMIT = pltpu.CompilerParams(vmem_limit_bytes=60 * 1024 * 1024)


def pieces(value):
    first = value.astype(jnp.bfloat16).astype(jnp.float32)
    rest = value - first
    second = rest.astype(jnp.bfloat16).astype(jnp.float32)
    return (first, second, rest - second)


def fill_limits(page_ids, lens_ref, offset_ref, table_ref, shared_ref, limit_ref):
    row = lax.broadcasted_iota(jnp.int32, (1, ROWS), 1)
    bound = jnp.full((1, ROWS), offset_ref[0], jnp.int32)
    for decode in range(DECODES):
        bound = jnp.where(row == PREFILL + decode, lens_ref[0, decode], bound)
    table, shared = table_ref[...], shared_ref[...]
    slot = lax.broadcasted_iota(jnp.int32, table.shape, 0)
    decode = lax.broadcasted_iota(jnp.int32, table.shape, 2) + 1
    shared_slot = lax.broadcasted_iota(jnp.int32, shared.shape, 1) + 1

    def whole(values):
        return jnp.sum(jnp.sum(values, axis=0), axis=1, keepdims=True)

    for index, page_id in enumerate(page_ids):
        listed = table == page_id
        owner = whole(jnp.where(listed, decode, 0)) - 1
        own_slot = whole(jnp.where(listed, slot, 0))
        prompt_slot = jnp.sum(
            jnp.where(shared == page_id, shared_slot, 0), axis=1, keepdims=True
        ) - 1
        prompt = jnp.broadcast_to(prompt_slot, row.shape) >= 0
        base = jnp.where(prompt_slot >= 0, prompt_slot, SHARED_PAGES + own_slot) * PAGE
        mine = (row >= PREFILL) & (row - PREFILL == owner)
        limit_ref[index : index + 1, :] = jnp.where(prompt | mine, bound - base, 0)


def attention_kernel(
    own_rows,
    core_ref,
    lens_ref,
    offset_ref,
    table_ref,
    shared_ref,
    query_one,
    query_two,
    own_key,
    own_value,
    far_key,
    far_value,
    out_ref,
    limit_ref,
):
    core = lax.axis_index("c")
    mine = 2 * lax.axis_index("z") + core
    sides = (mine, mine + 1 - 2 * core)

    @pl.when(pl.program_id(0) == 0)
    def _():
        page_ids = [side * OWN_PAGES + page for side in sides for page in range(OWN_PAGES)]
        fill_limits(page_ids, lens_ref, offset_ref, table_ref, shared_ref, limit_ref)

    query = jnp.concatenate(
        [query_one[:, :HEAD], query_one[:, HEAD:], query_two[:, :HEAD], query_two[:, HEAD:]], axis=0
    )
    keys = jnp.concatenate([own_key[...], far_key[...]], axis=0)
    values = jnp.concatenate([own_value[...], far_value[...]], axis=0)
    scores = lax.dot_general(
        keys, query, (((1,), (1,)), ((), ())), preferred_element_type=jnp.float32
    ) * (HEAD ** (-0.5))
    token = lax.broadcasted_iota(jnp.int32, (PAGE, ROWS), 0)
    fresh = lax.broadcasted_iota(jnp.int32, (FRESH_PAD, ROWS), 0)
    row = lax.broadcasted_iota(jnp.int32, (FRESH_PAD, ROWS), 1)
    seen = []
    for side in range(2):
        for page in range(OWN_PAGES):
            limit = limit_ref[pl.ds(side * OWN_PAGES + page, 1), :]
            seen.append((token < limit).astype(jnp.int32))
        key_row = sides[side] * own_rows + fresh
        before = jnp.where((key_row < PREFILL) & (key_row <= row), 1, 0)
        same = jnp.where(key_row == row, 1, 0)
        visible = jnp.where(row < PREFILL, before, same)
        seen.append(jnp.where(fresh < own_rows, visible, 0))
    seen = jnp.concatenate(seen, axis=0)
    seen = jnp.concatenate([seen] * 4, axis=1) > 0
    scores = jnp.where(seen, scores, NEG_FILL)
    peak = jnp.max(scores, axis=0, keepdims=True)
    exps = jnp.where(seen, jnp.exp(scores - peak), 0.0)
    total = jnp.sum(exps, axis=0, keepdims=True)
    mixed = lax.dot_general(
        values,
        exps.astype(jnp.bfloat16),
        (((0,), (0,)), ((), ())),
        preferred_element_type=jnp.float32,
    )
    line = lax.broadcasted_iota(jnp.int32, (STATS, ROWS), 0)
    for half in range(2):
        stats = jnp.zeros((STATS, ROWS), jnp.float32)
        for head in range(2):
            column = (2 * half + head) * ROWS
            out_ref[half, pl.ds(head * HEAD, HEAD), :] = mixed[:, column : column + ROWS].astype(
                jnp.bfloat16
            )
            sent = pieces(peak[:, column : column + ROWS]) + pieces(
                total[:, column : column + ROWS]
            )
            for index, value in enumerate(sent):
                stats = jnp.where(line == 6 * head + index, value, stats)
        out_ref[half, pl.ds(2 * HEAD, STATS), :] = stats.astype(jnp.bfloat16)


def attention(core, own_rows, lens, offset, table, shared, queries, own_kv, far_kv):
    kv_heads = own_kv.shape[1] // (2 * HEAD)
    chips = 2 * kv_heads
    smem = pl.BlockSpec(memory_space=pltpu.SMEM)

    def kv_spec(offset):
        return pl.BlockSpec((KEYS, HEAD), lambda j, core: (0, offset + j))

    return pl.pallas_call(
        functools.partial(attention_kernel, own_rows),
        grid_spec=pltpu.PrefetchScalarGridSpec(
            num_scalar_prefetch=1,
            grid=(kv_heads,),
            in_specs=[
                smem,
                smem,
                pl.BlockSpec(table.shape, lambda j, core: (0, 0, 0)),
                pl.BlockSpec(shared.shape, lambda j, core: (0, 0)),
                pl.BlockSpec((ROWS, 2 * HEAD), lambda j, core: (0, 4 * j + core[0])),
                pl.BlockSpec((ROWS, 2 * HEAD), lambda j, core: (0, 4 * j + 2 + core[0])),
                kv_spec(0),
                kv_spec(kv_heads),
                kv_spec(0),
                kv_spec(kv_heads),
            ],
            out_specs=pl.BlockSpec((2, 2 * HEAD + STATS, ROWS), lambda j, core: (j, 0, 0)),
            scratch_shapes=[pltpu.VMEM((2 * OWN_PAGES, ROWS), jnp.int32)],
        ),
        out_shape=jax.ShapeDtypeStruct((chips, 2 * HEAD + STATS, ROWS), jnp.bfloat16),
        compiler_params=LIMIT,
        name="attention",
    )(core, lens, offset, table, shared, queries, queries, own_kv, own_kv, far_kv, far_kv)


def combine_kernel(parts_ref, out_ref):
    chips = parts_ref.shape[0]
    for head in range(2):
        peaks = []
        totals = []
        for source in range(chips):
            stats = parts_ref[source, pl.ds(2 * HEAD, STATS), :].astype(jnp.float32)
            lines = [stats[6 * head + k : 6 * head + k + 1] for k in range(6)]
            peaks.append(lines[0] + lines[1] + lines[2])
            totals.append(lines[3] + lines[4] + lines[5])
        peak = peaks[0]
        for other in peaks[1:]:
            peak = jnp.maximum(peak, other)
        total = jnp.zeros_like(peak)
        mixed = jnp.zeros((HEAD, ROWS), jnp.float32)
        for source in range(chips):
            factor = jnp.exp(peaks[source] - peak)
            total = total + totals[source] * factor
            mixed = mixed + parts_ref[source, pl.ds(head * HEAD, HEAD), :].astype(jnp.float32) * factor
        attended = (mixed / total).T.astype(jnp.bfloat16)
        for copy in range(out_ref.shape[0]):
            out_ref[copy, :, head * HEAD : (head + 1) * HEAD] = attended


def combine(parts, copies):
    return pl.pallas_call(
        combine_kernel,
        out_shape=jax.ShapeDtypeStruct((copies, ROWS, 2 * HEAD), jnp.bfloat16),
        compiler_params=LIMIT,
        name="combine",
    )(parts)


def pack_kernel(
    out_ref, gate_ref, up_ref, down_ref, pages_ref, fresh_ref, weights_ref, kv_ref, spread_ref
):
    units = gate_ref.shape[1]
    weights_ref[:, :HEAD] = out_ref[:HEAD, :]
    weights_ref[:, HEAD : 2 * HEAD] = out_ref[HEAD:, :]
    weights_ref[:, 2 * HEAD : 2 * HEAD + units] = gate_ref[...]
    weights_ref[:, 2 * HEAD + units :] = up_ref[...]
    for page in range(OWN_PAGES):
        kv_ref[page * PAGE : (page + 1) * PAGE, :] = pages_ref[page]
    rest = FRESH_PAD - fresh_ref.shape[0]
    fresh = fresh_ref[...]
    if rest:
        fresh = jnp.concatenate([fresh, jnp.zeros((rest, fresh.shape[1]), jnp.bfloat16)], axis=0)
    kv_ref[OWN_PAGES * PAGE :, :] = fresh
    for copy in range(spread_ref.shape[0]):
        spread_ref[copy] = down_ref[...]


def pack(out_weight, gate_weight, up_weight, down_weight, pages, fresh, copies):
    width = 2 * HEAD + 2 * gate_weight.shape[1]
    return pl.pallas_call(
        pack_kernel,
        out_shape=(
            jax.ShapeDtypeStruct((HEAD, width), jnp.bfloat16),
            jax.ShapeDtypeStruct((KEYS, fresh.shape[1]), jnp.bfloat16),
            jax.ShapeDtypeStruct((copies,) + down_weight.shape, jnp.bfloat16),
        ),
        compiler_params=WIDE_LIMIT,
        name="pack",
    )(out_weight, gate_weight, up_weight, down_weight, pages, fresh)


def out_kernel(place_ref, attended_ref, weights_ref, *rest):
    result_ref = rest[-1]
    weights = jnp.concatenate([weights_ref[:, :HEAD], weights_ref[:, HEAD:]], axis=0)
    product = jnp.dot(attended_ref[...], weights, preferred_element_type=jnp.float32)
    if len(rest) == 2:
        product = product + rest[0][...].astype(jnp.float32)
    result_ref[...] = product.astype(jnp.bfloat16)


def out_product(half, attended, weights, far=None):
    rows = attended.shape[0]
    steps = weights.shape[0] // (2 * HEAD)
    column = pl.BlockSpec((rows, HEAD), lambda i, half: (0, i))
    return pl.pallas_call(
        out_kernel,
        grid_spec=pltpu.PrefetchScalarGridSpec(
            num_scalar_prefetch=1,
            grid=(steps,),
            in_specs=[
                pl.BlockSpec((rows, 2 * HEAD), lambda i, half: (0, 0)),
                pl.BlockSpec((HEAD, 2 * HEAD), lambda i, half: (half[0] * steps + i, 0)),
            ]
            + ([] if far is None else [column]),
            out_specs=column,
        ),
        out_shape=jax.ShapeDtypeStruct((rows, steps * HEAD), jnp.bfloat16),
        compiler_params=LIMIT,
        name="out_product",
    )(half, attended, weights, *(() if far is None else (far,)))


def norm_kernel(place_ref, parts_ref, residual_ref, gain_ref, updated_ref, sent_ref):
    x_size, z_size = parts_ref.shape[:2]
    blocks = parts_ref.shape[4] // HEAD
    square = jnp.zeros((parts_ref.shape[3], 1), jnp.float32)
    for x in range(x_size):
        for core in range(2):
            summed = parts_ref[x, 0, core].astype(jnp.float32)
            for z in range(1, z_size):
                summed = summed + parts_ref[x, z, core].astype(jnp.float32)
            for block in range(blocks):
                column = ((core * blocks + block) * x_size + x) * HEAD
                value = summed[:, block * HEAD : (block + 1) * HEAD]
                value = value + residual_ref[0, :, column : column + HEAD].astype(jnp.float32)
                square = square + jnp.sum(value * value, axis=1, keepdims=True)
                updated_ref[:, column : column + HEAD] = value
    scale = lax.rsqrt(square / (2 * x_size * blocks * HEAD) + EPSILON)
    for x in range(x_size):
        for core in range(2):
            normed = []
            for block in range(blocks):
                column = ((core * blocks + block) * x_size + x) * HEAD
                value = updated_ref[:, column : column + HEAD] * scale
                normed.append(value * gain_ref[:, column : column + HEAD])
            normed = jnp.concatenate(normed, axis=1).astype(jnp.bfloat16)
            for z in range(z_size):
                sent_ref[x, z, core] = normed


def add_and_norm(place, parts, residual, gain):
    rows, width = parts.shape[3], residual.shape[2]
    return pl.pallas_call(
        norm_kernel,
        grid_spec=pltpu.PrefetchScalarGridSpec(
            num_scalar_prefetch=1,
            grid=(1,),
            in_specs=[
                pl.BlockSpec(parts.shape, lambda i, place: (0,) * 5),
                pl.BlockSpec((1, rows, width), lambda i, place: (0, place[0], 0)),
                pl.BlockSpec((1, width), lambda i, place: (0, 0)),
            ],
            out_specs=[
                pl.BlockSpec((rows, width), lambda i, place: (0, 0)),
                pl.BlockSpec(parts.shape, lambda i, place: (0,) * 5),
            ],
        ),
        out_shape=(
            jax.ShapeDtypeStruct((rows, width), jnp.float32),
            jax.ShapeDtypeStruct(parts.shape, jnp.bfloat16),
        ),
        compiler_params=LIMIT,
        name="add_and_norm",
    )(place, parts, residual, gain.reshape(1, -1))


def times_down(hidden, down_ref):
    return jnp.concatenate(
        [
            jnp.dot(hidden, down_ref[block], preferred_element_type=jnp.float32)
            for block in range(down_ref.shape[0])
        ],
        axis=1,
    )


def hidden_kernel(half_ref, parts_ref, down_ref, hidden_ref, far_ref):
    @pl.when(pl.program_id(0) == 0)
    def _():
        summed = parts_ref[0].astype(jnp.float32)
        for source in range(1, parts_ref.shape[0]):
            summed = summed + parts_ref[source].astype(jnp.float32)
        units = summed.shape[1] // 2
        gate = summed[:, :units]
        hidden_ref[...] = (gate / (1.0 + jnp.exp(-gate)) * summed[:, units:]).astype(jnp.bfloat16)

    far_ref[...] = times_down(hidden_ref[...], down_ref).astype(jnp.bfloat16)


def down_spec(down, steps):
    blocks = down.shape[0] // (2 * steps)
    return pl.BlockSpec((blocks,) + down.shape[1:], lambda i, half: (half[0] * steps + i, 0, 0))


def hidden_product(half, parts, down):
    units = down.shape[1]
    steps = 4 if down.shape[0] % 8 == 0 else 1
    width = down.shape[0] // 2 * HEAD
    return pl.pallas_call(
        hidden_kernel,
        grid_spec=pltpu.PrefetchScalarGridSpec(
            num_scalar_prefetch=1,
            grid=(steps,),
            in_specs=[
                pl.BlockSpec(parts.shape, lambda i, half: (0, 0, 0)),
                down_spec(down, steps),
            ],
            out_specs=[
                pl.BlockSpec((ROWS, units), lambda i, half: (0, 0)),
                pl.BlockSpec((ROWS, width // steps), lambda i, half: (0, i)),
            ],
        ),
        out_shape=(
            jax.ShapeDtypeStruct((ROWS, units), jnp.bfloat16),
            jax.ShapeDtypeStruct((ROWS, width), jnp.bfloat16),
        ),
        compiler_params=LIMIT,
        name="hidden_product",
    )(half, parts, down)


def down_kernel(half_ref, hidden_ref, down_ref, far_ref, near_ref):
    product = times_down(hidden_ref[...], down_ref) + far_ref[...].astype(jnp.float32)
    near_ref[...] = product.astype(jnp.bfloat16)


def down_product(half, hidden, down, far):
    steps = 4 if down.shape[0] % 8 == 0 else 1
    column = pl.BlockSpec((ROWS, far.shape[1] // steps), lambda i, half: (0, i))
    return pl.pallas_call(
        down_kernel,
        grid_spec=pltpu.PrefetchScalarGridSpec(
            num_scalar_prefetch=1,
            grid=(steps,),
            in_specs=[
                pl.BlockSpec(hidden.shape, lambda i, half: (0, 0)),
                down_spec(down, steps),
                column,
            ],
            out_specs=column,
        ),
        out_shape=jax.ShapeDtypeStruct(far.shape, jnp.bfloat16),
        compiler_params=LIMIT,
        name="down_product",
    )(half, hidden, down, far)


def swap(value):
    return lax.ppermute(value, "c", [(0, 1), (1, 0)])


def local(
    queries,
    fresh_kv,
    kv_pages,
    residual,
    norm_gain,
    out_weight,
    gate_weight,
    up_weight,
    down_weight,
    page_table,
    shared_pages,
    cache_lens,
    prefill_offsets,
):
    y_size, x_size, z_size = lax.axis_size("y"), lax.axis_size("x"), lax.axis_size("z")
    core = lax.axis_index("c")
    mine = lax.axis_index("z") * 2 + core
    near_half, far_half = core.reshape(1), (1 - core).reshape(1)
    own_rows = fresh_kv.shape[1]
    half = y_size // 2

    packed, own_kv, spread = pack(
        out_weight, gate_weight, up_weight, down_weight, kv_pages[0], fresh_kv[0], x_size
    )
    weights = lax.all_gather(packed, "y", axis=0, tiled=True)
    far_kv = swap(own_kv)
    down = lax.all_to_all(spread, "x", 0, 0, tiled=True)
    parts = attention(
        near_half,
        own_rows,
        cache_lens,
        prefill_offsets,
        jnp.transpose(page_table, (2, 0, 1)),
        shared_pages,
        queries[0],
        own_kv,
        far_kv,
    )
    parts, down = lax.optimization_barrier((parts, down))
    down = lax.all_gather(down, "y", axis=0, tiled=True)
    parts = lax.all_to_all(parts, "z", 0, 0, tiled=True)
    attended = lax.all_to_all(combine(parts, x_size), "x", 0, 0, tiled=True)
    attended = attended.reshape(x_size * ROWS, 2 * HEAD)

    far = swap(out_product(far_half, attended, weights))
    parts = out_product(near_half, attended, weights, far)
    parts = lax.all_to_all(parts, ("x", "z", "c"), 0, 0, tiled=True)
    parts = parts.reshape(x_size, z_size, 2, own_rows, half * HEAD)
    updated, sent = add_and_norm(mine.reshape(1), parts, residual, norm_gain)
    near_rows = lax.all_to_all(
        sent.reshape(x_size * ROWS, half * HEAD), ("x", "z", "c"), 0, 0, tiled=True
    )
    far_rows = swap(near_rows)

    def partial(rows, which):
        piece = lax.dynamic_slice_in_dim(weights, which * half * HEAD, half * HEAD, 0)
        return jnp.dot(rows, piece[:, 2 * HEAD :], preferred_element_type=jnp.float32)

    gated = partial(near_rows, core) + partial(far_rows, 1 - core)
    gated = lax.all_to_all(gated.astype(jnp.bfloat16), "x", 0, 0, tiled=True)
    gated = gated.reshape(x_size, ROWS, gated.shape[1])
    hidden, far = hidden_product(far_half, gated, down)
    parts = down_product(near_half, hidden, down, swap(far))
    parts = lax.all_to_all(parts, ("z", "c"), 0, 0, tiled=True)
    parts = parts.reshape(z_size, 2, own_rows, parts.shape[1])
    returned = jnp.transpose(jnp.sum(parts.astype(jnp.float32), axis=0), (1, 0, 2))
    return (updated + returned.reshape(own_rows, -1)).astype(jnp.bfloat16)[None]


def solution(mesh):
    cores = 2
    chips = mesh.shape["mlp"] // cores
    along = 4 if mesh.shape["grp"] % 16 == 0 else 2
    long_mesh = Mesh(
        mesh.devices.reshape(mesh.shape["grp"] // along, along, chips, cores), LONG
    )
    grp, mlp = ("y", "x"), ("z", "c")
    placed = (
        P(grp, None, None),
        P(grp, mlp, None),
        P(grp, mlp, None, None),
        P(grp, None, None),
        P(),
        P(mlp, grp),
        P(grp, mlp),
        P(grp, mlp),
        P(mlp, grp),
        P(grp, None, None),
        P(grp, None),
        P(grp, None),
        P(grp),
    )
    return jax.shard_map(
        local, mesh=long_mesh, in_specs=placed, out_specs=P(grp, mlp, None), check_vma=False
    )
```

time: 193 us -> 182 us (0.943)
  waiting for transfers between devices: 48.6 us -> 38.9 us
  other arithmetic: 9.94 us -> 0.72 us
  Pallas kernels: 5.31 us -> 13.9 us
  starting transfers between devices: 42.7 us -> 36.6 us
  blocking collectives: 61.6 us -> 66 us
  local copies, waits for them, and re-layouts: 5.49 us -> 8.54 us
    all_to_all x3, waiting for transfers between devices: 38.2 us -> 29.3 us  [the longest x1 17.4 us: local(): parts = lax.all_to_all(parts, ('x', 'z', 'c'), 0, 0, tiled=True)]
    pallas_call x2 -> x8, Pallas kernels: 5.31 us -> 13.9 us  [the longest x1 4.61 us: attention(): pl.pallas_call(functools.partial(attention_kernel, own_rows), grid_spec=p...]
    all_gather x1 -> x2, waiting for transfers between devices: 6.77 us -> 0.01 us  [the longest x1 0.01 us: local(): weights = lax.all_gather(packed, 'y', axis=0, tiled=True)]
    all_to_all x3, starting transfers between devices: 18.6 us -> 12.1 us  [the longest x1 4.57 us: local(): parts = lax.all_to_all(parts, ('x', 'z', 'c'), 0, 0, tiled=True)]
    unnamed x17 -> x24, local copies, waits for them, and re-layouts: 2.08 us -> 8.54 us
    all_to_all x1, waiting for transfers between devices: 0.01 us -> 5.53 us  [local(): attended = lax.all_to_all(combine(parts, x_size), 'x', 0, 0, tiled=True)]
    all_to_all x2, blocking collectives: 39.3 us -> 44.6 us  [the longest x1 23.5 us: local(): lax.all_to_all(sent.reshape(x_size * ROWS, half * HEAD), ('x', 'z', 'c'),...]
    convert_element_type x4 -> x0, other arithmetic: 4.22 us -> none  [the longest x1 1.67 us: local(): updated = carried.astype(jnp.float32) + projected]
  transfers between devices with their start and end apart: 9 -> 10, of which waited for: 7 -> 6; matrix products, arithmetic and copies ran while one was open for 4% -> 1% of each run, Pallas kernels for 3% -> 5%
where the time goes in v2:
time: 182 us; the launch traced here: 181 us
  blocking collectives  66 us (36%)
  waiting for transfers between devices  38.9 us (21%)
  starting transfers between devices  36.6 us (20%)
  between operations  14.2 us (8%)
  Pallas kernels  13.9 us (8%)
  local copies, waits for them, and re-layouts  8.54 us (5%)
  matrix products  2.06 us (1%)
    all_to_all x1, blocking collectives, local(): lax.all_to_all(sent.reshape(x_size * ROWS, half * HEAD), ('x', 'z', 'c'),...  23.5 us
    all_to_all x1, blocking collectives, local(): parts = lax.all_to_all(parts, 'z', 0, 0, tiled=True)  21.4 us
    all_to_all x1, blocking collectives, local(): parts = lax.all_to_all(parts, ('z', 'c'), 0, 0, tiled=True)  21.1 us
    ppermute x4, starting transfers between devices, swap(): return lax.ppermute(value, 'c', [(0, 1), (1, 0)])  19.9 us
    all_to_all x1, waiting for transfers between devices, local(): parts = lax.all_to_all(parts, ('x', 'z', 'c'), 0, 0, tiled=True)  17.4 us
    all_to_all x1, waiting for transfers between devices, local(): gated = lax.all_to_all(gated.astype(jnp.bfloat16), 'x', 0, 0, tiled=True)  12 us
    unnamed x24, local copies, waits for them, and re-layouts  8.54 us
    all_to_all x1, waiting for transfers between devices, local(): attended = lax.all_to_all(combine(parts, x_size), 'x', 0, 0, tiled=True)  5.53 us
  transfers between devices with their start and end apart: 10, of which 6 were waited for; matrix products, arithmetic and copies ran while one was open for 1% of the time, Pallas kernels for 5%

profile of v2, /device:TPU:1, one launch (start us, length us, event | category | flops | bytes accessed | tf_op | source)
XLA Modules:
  0.0 181.0 jit_solution(11838704092186364302)
XLA Ops:
  6.5 0.0 all-gather.3.cloned.1.call-start
  6.5 2.4 %pack.1 = (bf16[128,1024]{1,0:T(8,128)(2,1)}, bf16[272,1024]{1,0:T(8,128)(2,1)}, bf16[4,384,128]{2,1,0:T(8,128)(2,1)}) custom-call(bf16[256,128]{1,0:T(8,128)(2,1)} %out_ref.1, bf16[128,384]{1,0:T(8,128)(2,1)} %gate_ref.1, bf16[128,384]{1,0:T(8,128)(2,1)} %up_ref.1, bf16[384,128]{1,0:T(8,128)(2,1)} %down_ref.1, bf16[2,128,1024]{2,1,0:T(8,128)(2,1)} %bitcast.36, ...), custom_call_target="tpu_custom_call" | custom-call | tf_op jit(solution)/shard_map/pack/pallas_call | solution.py:224
  9.0 0.0 all-gather.3.cloned.1.call-update
  9.0 8.8 %collective-permute-start = (bf16[272,1024]{1,0:T(8,128)(2,1)}, bf16[272,1024]{1,0:T(8,128)(2,1)S(1)}, u32[]{:S(2)}, u32[]{:S(2)}) collective-permute-start(bf16[272,1024]{1,0:T(8,128)(2,1)} %get-tuple-element.14.own_key.own_value), channel_id=1, source_target_pairs={{0,1},{1,0},{2,3},{3,2},{4,5},{5,4},{6,7},{7,6},{8,9},{9,8},{10,11... | collective-permute-start | bytes 1671176 | tf_op jit(solution)/shard_map/ppermute | solution.py:403
  17.8 3.5 %all-to-all-start = ((bf16[4,384,128]{2,1,0:T(8,128)(2,1)}), bf16[4,384,128]{2,1,0:T(8,128)(2,1)S(1)}, u32[]{:S(2)}, u32[]{:S(2)}) async-start(bf16[4,384,128]{2,1,0:T(8,128)(2,1)} %get-tuple-element.15), calls=%async_computation | async-start | bytes 786432 | tf_op jit(solution)/shard_map/all_to_all | solution.py:433
  21.3 0.0 all-gather.5.cloned.1.call-start
  22.0 0.0 collective-permute-done.far_key.far_value
  22.0 0.0 copy-done.4
  22.0 0.0 copy-start.5
  22.0 1.0 copy-done.5
  23.0 0.7 copy-done.8
  23.7 0.7 copy-done.9
  24.4 0.7 copy-done.10
  25.0 4.6 %attention.1 = bf16[8,272,128]{2,1,0:T(8,128)(2,1)S(1)} custom-call(s32[1]{0:T(128)} %bitcast.1.core_ref.place_ref.half_ref, s32[1,16]{1,0:T(1,128)S(1)} %copy-done.9, s32[1]{0:T(128)S(6)} %copy.14.offset_ref, s32[12,1,16]{2,1,0:T(1,128)S(1)} %bitcast.33, s32[1,4]{1,0:T(1,128)S(1)} %copy-done.10, bf16[128,4096]{1,0:T(8,128)(2,1)S(1)} %bitcast.25, ...), custom_call_target="tpu_custom_call" | custom-call | tf_op jit(solution)/shard_map/attention/pallas_call | solution.py:144
  29.7 0.0 all-to-all-done
  29.7 0.0 copy-start.11
  29.7 0.7 copy-done.11
  30.4 0.0 all-gather.5.cloned.1.call-update
  30.5 21.4 %all_to_all.54.parts_ref = bf16[8,272,128]{2,1,0:T(8,128)(2,1)S(1)} all-to-all(bf16[8,272,128]{2,1,0:T(8,128)(2,1)S(1)} %attention.1), channel_id=1, replica_groups=mesh['y'=8,'x'=4,'z'=8,'c'=2] {'z'}, dimensions={0} | all-to-all | bytes 1114112 | tf_op jit(solution)/shard_map/all_to_all | solution.py:447
  51.9 0.9 combine.1
  52.8 4.5 %all-to-all-start.2 = ((bf16[4,128,256]{2,1,0:T(8,128)(2,1)}), bf16[4,128,256]{2,1,0:T(8,128)(2,1)S(1)}, u32[]{:S(2)}, u32[]{:S(2)}) async-start(bf16[4,128,256]{2,1,0:T(8,128)(2,1)} %combine.1), calls=%async_computation.2 | async-start | bytes 524288 | tf_op jit(solution)/shard_map/all_to_all | solution.py:448
  57.3 5.5 %all-to-all-done.2 = bf16[4,128,256]{2,1,0:T(8,128)(2,1)S(1)} async-done(((bf16[4,128,256]{2,1,0:T(8,128)(2,1)}), bf16[4,128,256]{2,1,0:T(8,128)(2,1)S(1)}, u32[]{:S(2)}, u32[]{:S(2)}) %all-to-all-start.2) | async-done | bytes 262176 | tf_op jit(solution)/shard_map/all_to_all | solution.py:448
  62.9 1.6 copy-done
  64.5 1.1 out_product.2
  65.6 0.0 copy-start.7
  65.6 5.7 %collective-permute-start.1 = (bf16[512,512]{1,0:T(8,128)(2,1)S(1)}, bf16[512,512]{1,0:T(8,128)(2,1)S(1)}, u32[]{:S(2)}, u32[]{:S(2)}) collective-permute-start(bf16[512,512]{1,0:T(8,128)(2,1)S(1)} %out_product.2), channel_id=1, source_target_pairs={{0,1},{1,0},{2,3},{3,2},{4,5},{5,4},{6,7},{7,6},{8,9},{9,8},{10,11... | collective-permute-start | bytes 1572872 | tf_op jit(solution)/shard_map/ppermute | solution.py:403
  71.3 1.5 collective-permute-done.1.rest_0_
  72.8 2.2 %out_product.3 = bf16[512,512]{1,0:T(8,128)(2,1)} custom-call(s32[1]{0:T(128)} %bitcast.1.core_ref.place_ref.half_ref, bf16[512,256]{1,0:T(8,128)(2,1)S(1)} %bitcast.28, bf16[1024,1024]{1,0:T(8,128)(2,1)S(1)} %copy-done, bf16[512,512]{1,0:T(8,128)(2,1)S(1)} %collective-permute-done.1.rest_0_), custom_call_target="tpu_custom_call" | custom-call | tf_op jit(solution)/shard_map/out_product/pallas_call | solution.py:249
  75.0 4.6 %all-to-all-start.3 = ((bf16[64,8,512]{2,1,0:T(8,128)(2,1)}), bf16[64,8,512]{2,1,0:T(8,128)(2,1)S(1)}, u32[]{:S(2)}, u32[]{:S(2)}) async-start(bf16[64,8,512]{2,1,0:T(8,128)(2,1)} %bitcast.8), calls=%async_computation.3 | async-start | bytes 1048576 | tf_op jit(solution)/shard_map/all_to_all | solution.py:453
  79.6 17.4 %all-to-all-done.3 = bf16[64,8,512]{2,1,0:T(8,128)(2,1)S(1)} async-done(((bf16[64,8,512]{2,1,0:T(8,128)(2,1)}), bf16[64,8,512]{2,1,0:T(8,128)(2,1)S(1)}, u32[]{:S(2)}, u32[]{:S(2)}) %all-to-all-start.3) | async-done | bytes 524320 | tf_op jit(solution)/shard_map/all_to_all | solution.py:453
  96.9 0.0 copy-done.7
  96.9 1.2 copy-done.6
  98.2 0.2 add_and_norm.1
  98.4 23.5 %all_to_all.55 = bf16[64,8,512]{2,1,0:T(8,128)(2,1)S(1)} all-to-all(bf16[64,8,512]{2,1,0:T(8,128)(2,1)S(1)} %bitcast.31), channel_id=1, replica_groups=mesh['y'=8,'x'=4,'z'=8,'c'=2] {'x','z','c'}, dimensions={0} | all-to-all | bytes 1048576 | tf_op jit(solution)/shard_map/all_to_all | solution.py:456
  121.8 2.2 %collective-permute-start.2 = (bf16[512,512]{1,0:T(8,128)(2,1)S(1)}, bf16[512,512]{1,0:T(8,128)(2,1)S(1)}, u32[]{:S(2)}, u32[]{:S(2)}) collective-permute-start(bf16[512,512]{1,0:T(8,128)(2,1)S(1)} %bitcast.34), channel_id=1, source_target_pairs={{0,1},{1,0},{2,3},{3,2},{4,5},{5,4},{6,7},{7,6},{8,9},{9,8},{10,11... | collective-permute-start | bytes 1572872 | tf_op jit(solution)/shard_map/ppermute | solution.py:403
  124.1 0.6 fusion.1
  124.7 1.0 collective-permute-done.2
  125.6 1.5 add_convert_fusion
  127.1 4.1 %all-to-all-start.5 = ((bf16[4,128,768]{2,1,0:T(8,128)(2,1)}), bf16[4,128,768]{2,1,0:T(8,128)(2,1)S(1)}, u32[]{:S(2)}, u32[]{:S(2)}) async-start(bf16[4,128,768]{2,1,0:T(8,128)(2,1)} %bitcast.13), calls=%async_computation.5 | async-start | bytes 1572864 | tf_op jit(solution)/shard_map/all_to_all | solution.py:466
  131.2 12.0 %all-to-all-done.5.parts_ref = bf16[4,128,768]{2,1,0:T(8,128)(2,1)S(1)} async-done(((bf16[4,128,768]{2,1,0:T(8,128)(2,1)}), bf16[4,128,768]{2,1,0:T(8,128)(2,1)S(1)}, u32[]{:S(2)}, u32[]{:S(2)}) %all-to-all-start.5) | async-done | bytes 786464 | tf_op jit(solution)/shard_map/all_to_all | solution.py:466
  143.2 1.9 %copy-done.2 = bf16[32,384,128]{2,1,0:T(8,128)(2,1)S(1)} copy-done((bf16[32,384,128]{2,1,0:T(8,128)(2,1)S(1)}, bf16[32,384,128]{2,1,0:T(8,128)(2,1)}, u32[]{:S(2)}) %copy-start.2) | copy-done | bytes 3145752
  145.1 1.3 hidden_product.1
  146.4 3.2 %collective-permute-start.3 = (bf16[128,2048]{1,0:T(8,128)(2,1)S(1)}, bf16[128,2048]{1,0:T(8,128)(2,1)S(1)}, u32[]{:S(2)}, u32[]{:S(2)}) collective-permute-start(bf16[128,2048]{1,0:T(8,128)(2,1)S(1)} %get-tuple-element.22), channel_id=1, source_target_pairs={{0,1},{1,0},{2,3},{3,2},{4,5},{5,4},{6,7},{7,6},{8,9},{9,8},{10,11... | collective-permute-start | bytes 1572872 | tf_op jit(solution)/shard_map/ppermute | solution.py:403
  149.6 1.5 collective-permute-done.3.far_ref
  151.1 1.2 down_product.1
  152.3 21.1 %all_to_all.56 = bf16[16,8,2048]{2,1,0:T(8,128)(2,1)S(1)} all-to-all(bf16[16,8,2048]{2,1,0:T(8,128)(2,1)S(1)} %bitcast.29), channel_id=1, replica_groups=mesh['y'=8,'x'=4,'z'=8,'c'=2] {'z','c'}, dimensions={0} | all-to-all | bytes 1048576 | tf_op jit(solution)/shard_map/all_to_all | solution.py:470
  173.4 0.1 convert_reduce_fusion
  173.5 0.7 fusion.3
  (13 shorter events, 0.0 us)
Async XLA Ops:
  6.5 15.4 %copy-start.4 = (bf16[1,128,4096]{2,1,0:T(8,128)(2,1)S(1)}, bf16[1,128,4096]{2,1,0:T(8,128)(2,1)}, u32[]{:S(2)}) copy-start(bf16[1,128,4096]{2,1,0:T(8,128)(2,1)} %param.13) | copy-start | bytes 3145732
  6.5 56.3 %all-gather.3.cloned.1.call-start = ((), (), s32[]{:S(2)}) async-start(), calls=%async_computation.7 | async-start | bytes 2359296 | tf_op jit(solution)/shard_map/all_gather | solution.py:431
  9.0 13.0 %collective-permute-start = (bf16[272,1024]{1,0:T(8,128)(2,1)}, bf16[272,1024]{1,0:T(8,128)(2,1)S(1)}, u32[]{:S(2)}, u32[]{:S(2)}) collective-permute-start(bf16[272,1024]{1,0:T(8,128)(2,1)} %get-tuple-element.14.own_key.own_value), channel_id=1, source_target_pairs={{0,1},{1,0},{2,3},{3,2},{4,5},{5,4},{6,7},{7,6},{8,9},{9,8},{10,11... | collective-permute-start | bytes 1671176 | tf_op jit(solution)/shard_map/ppermute | solution.py:403
  17.8 11.9 %all-to-all-start = ((bf16[4,384,128]{2,1,0:T(8,128)(2,1)}), bf16[4,384,128]{2,1,0:T(8,128)(2,1)S(1)}, u32[]{:S(2)}, u32[]{:S(2)}) async-start(bf16[4,384,128]{2,1,0:T(8,128)(2,1)} %get-tuple-element.15), calls=%async_computation | async-start | bytes 786432 | tf_op jit(solution)/shard_map/all_to_all | solution.py:433
  21.3 110.0 %all-gather.5.cloned.1.call-start = ((), (), s32[]{:S(2)}) async-start(), calls=%async_computation.8 | async-start | bytes 3538944 | tf_op jit(solution)/shard_map/all_gather | solution.py:446
  22.0 1.1 copy-start.5
  23.0 0.7 copy-start.8
  23.7 0.7 copy-start.9
  24.4 0.7 copy-start.10
  29.7 0.8 copy-start.11
  52.8 10.1 %all-to-all-start.2 = ((bf16[4,128,256]{2,1,0:T(8,128)(2,1)}), bf16[4,128,256]{2,1,0:T(8,128)(2,1)S(1)}, u32[]{:S(2)}, u32[]{:S(2)}) async-start(bf16[4,128,256]{2,1,0:T(8,128)(2,1)} %combine.1), calls=%async_computation.2 | async-start | bytes 524288 | tf_op jit(solution)/shard_map/all_to_all | solution.py:448
  62.9 1.6 copy-start
  65.6 31.4 %copy-start.7 = (f32[4096]{0:T(1024)S(1)}, f32[4096]{0:T(1024)}, u32[]{:S(2)}) copy-start(f32[4096]{0:T(1024)} %param.17) | copy-start | bytes 49156
  65.6 7.2 %collective-permute-start.1 = (bf16[512,512]{1,0:T(8,128)(2,1)S(1)}, bf16[512,512]{1,0:T(8,128)(2,1)S(1)}, u32[]{:S(2)}, u32[]{:S(2)}) collective-permute-start(bf16[512,512]{1,0:T(8,128)(2,1)S(1)} %out_product.2), channel_id=1, source_target_pairs={{0,1},{1,0},{2,3},{3,2},{4,5},{5,4},{6,7},{7,6},{8,9},{9,8},{10,11... | collective-permute-start | bytes 1572872 | tf_op jit(solution)/shard_map/ppermute | solution.py:403
  75.0 49.1 %copy-start.1 = (bf16[1024,1024]{1,0:T(8,128)(2,1)S(1)}, bf16[1024,1024]{1,0:T(8,128)(2,1)}, u32[]{:S(2)}) copy-start(bf16[1024,1024]{1,0:T(8,128)(2,1)} %all-gather.3.cloned.1.call-done.weights_ref) | copy-start | bytes 6291460
  75.0 21.9 %all-to-all-start.3 = ((bf16[64,8,512]{2,1,0:T(8,128)(2,1)}), bf16[64,8,512]{2,1,0:T(8,128)(2,1)S(1)}, u32[]{:S(2)}, u32[]{:S(2)}) async-start(bf16[64,8,512]{2,1,0:T(8,128)(2,1)} %bitcast.8), calls=%async_computation.3 | async-start | bytes 1048576 | tf_op jit(solution)/shard_map/all_to_all | solution.py:453
  96.9 1.2 copy-start.6
  121.8 3.8 %collective-permute-start.2 = (bf16[512,512]{1,0:T(8,128)(2,1)S(1)}, bf16[512,512]{1,0:T(8,128)(2,1)S(1)}, u32[]{:S(2)}, u32[]{:S(2)}) collective-permute-start(bf16[512,512]{1,0:T(8,128)(2,1)S(1)} %bitcast.34), channel_id=1, source_target_pairs={{0,1},{1,0},{2,3},{3,2},{4,5},{5,4},{6,7},{7,6},{8,9},{9,8},{10,11... | collective-permute-start | bytes 1572872 | tf_op jit(solution)/shard_map/ppermute | solution.py:403
  127.1 16.1 %all-to-all-start.5 = ((bf16[4,128,768]{2,1,0:T(8,128)(2,1)}), bf16[4,128,768]{2,1,0:T(8,128)(2,1)S(1)}, u32[]{:S(2)}, u32[]{:S(2)}) async-start(bf16[4,128,768]{2,1,0:T(8,128)(2,1)} %bitcast.13), calls=%async_computation.5 | async-start | bytes 1572864 | tf_op jit(solution)/shard_map/all_to_all | solution.py:466
  143.2 1.9 %copy-start.2 = (bf16[32,384,128]{2,1,0:T(8,128)(2,1)S(1)}, bf16[32,384,128]{2,1,0:T(8,128)(2,1)}, u32[]{:S(2)}) copy-start(bf16[32,384,128]{2,1,0:T(8,128)(2,1)} %all-gather.5.cloned.1.call-done.down_ref) | copy-start | bytes 9437188
  145.1 6.0 %copy-start.3 = (bf16[32,384,128]{2,1,0:T(8,128)(2,1)S(1)}, bf16[32,384,128]{2,1,0:T(8,128)(2,1)}, u32[]{:S(2)}) copy-start(bf16[32,384,128]{2,1,0:T(8,128)(2,1)} %all-gather.5.cloned.1.call-done.down_ref) | copy-start | bytes 9437188
  146.4 4.7 %collective-permute-start.3 = (bf16[128,2048]{1,0:T(8,128)(2,1)S(1)}, bf16[128,2048]{1,0:T(8,128)(2,1)S(1)}, u32[]{:S(2)}, u32[]{:S(2)}) collective-permute-start(bf16[128,2048]{1,0:T(8,128)(2,1)S(1)} %get-tuple-element.22), channel_id=1, source_target_pairs={{0,1},{1,0},{2,3},{3,2},{4,5},{5,4},{6,7},{7,6},{8,9},{9,8},{10,11... | collective-permute-start | bytes 1572872 | tf_op jit(solution)/shard_map/ppermute | solution.py:403
Sparse Core Ops, SparseCore 0:
  9.4 45.3 all-gather.2
  56.9 49.6 all-gather.4

commit v3 on v2

--- a/solution.py
+++ b/solution.py
@@ -62,10 +62,9 @@
 def attention_kernel(
     own_rows,
     core_ref,
-    lens_ref,
-    offset_ref,
-    table_ref,
-    shared_ref,
+    mine_ref,
+    limit_ref,
+    residual_ref,
     query_one,
     query_two,
     own_key,
@@ -73,17 +72,15 @@
     far_key,
     far_value,
     out_ref,
-    limit_ref,
+    carried_ref,
 ):
+    @pl.when(pl.program_id(0) == 0)
+    def _():
+        carried_ref[...] = residual_ref[0].astype(jnp.float32)
+
     core = lax.axis_index("c")
     mine = 2 * lax.axis_index("z") + core
     sides = (mine, mine + 1 - 2 * core)
-
-    @pl.when(pl.program_id(0) == 0)
-    def _():
-        page_ids = [side * OWN_PAGES + page for side in sides for page in range(OWN_PAGES)]
-        fill_limits(page_ids, lens_ref, offset_ref, table_ref, shared_ref, limit_ref)
-
     query = jnp.concatenate(
         [query_one[:, :HEAD], query_one[:, HEAD:], query_two[:, :HEAD], query_two[:, HEAD:]], axis=0
     )
@@ -133,38 +130,41 @@
         out_ref[half, pl.ds(2 * HEAD, STATS), :] = stats.astype(jnp.bfloat16)
 
 
-def attention(core, own_rows, lens, offset, table, shared, queries, own_kv, far_kv):
+def attention(core, mine, own_rows, limits, residual, queries, own_kv, far_kv):
     kv_heads = own_kv.shape[1] // (2 * HEAD)
     chips = 2 * kv_heads
-    smem = pl.BlockSpec(memory_space=pltpu.SMEM)
+    width = residual.shape[2]
 
     def kv_spec(offset):
-        return pl.BlockSpec((KEYS, HEAD), lambda j, core: (0, offset + j))
+        return pl.BlockSpec((KEYS, HEAD), lambda j, core, mine: (0, offset + j))
 
     return pl.pallas_call(
         functools.partial(attention_kernel, own_rows),
         grid_spec=pltpu.PrefetchScalarGridSpec(
-            num_scalar_prefetch=1,
+            num_scalar_prefetch=2,
             grid=(kv_heads,),
             in_specs=[
-                smem,
-                smem,
-                pl.BlockSpec(table.shape, lambda j, core: (0, 0, 0)),
-                pl.BlockSpec(shared.shape, lambda j, core: (0, 0)),
-                pl.BlockSpec((ROWS, 2 * HEAD), lambda j, core: (0, 4 * j + core[0])),
-                pl.BlockSpec((ROWS, 2 * HEAD), lambda j, core: (0, 4 * j + 2 + core[0])),
+                pl.BlockSpec(limits.shape, lambda j, core, mine: (0, 0)),
+                pl.BlockSpec((1, own_rows, width), lambda j, core, mine: (0, mine[0], 0)),
+                pl.BlockSpec((ROWS, 2 * HEAD), lambda j, core, mine: (0, 4 * j + core[0])),
+                pl.BlockSpec((ROWS, 2 * HEAD), lambda j, core, mine: (0, 4 * j + 2 + core[0])),
                 kv_spec(0),
                 kv_spec(kv_heads),
                 kv_spec(0),
                 kv_spec(kv_heads),
             ],
-            out_specs=pl.BlockSpec((2, 2 * HEAD + STATS, ROWS), lambda j, core: (j, 0, 0)),
-            scratch_shapes=[pltpu.VMEM((2 * OWN_PAGES, ROWS), jnp.int32)],
-        ),
-        out_shape=jax.ShapeDtypeStruct((chips, 2 * HEAD + STATS, ROWS), jnp.bfloat16),
-        compiler_params=LIMIT,
+            out_specs=[
+                pl.BlockSpec((2, 2 * HEAD + STATS, ROWS), lambda j, core, mine: (j, 0, 0)),
+                pl.BlockSpec((own_rows, width), lambda j, core, mine: (0, 0)),
+            ],
+        ),
+        out_shape=(
+            jax.ShapeDtypeStruct((chips, 2 * HEAD + STATS, ROWS), jnp.bfloat16),
+            jax.ShapeDtypeStruct((own_rows, width), jnp.float32),
+        ),
+        compiler_params=WIDE_LIMIT,
         name="attention",
-    )(core, lens, offset, table, shared, queries, queries, own_kv, own_kv, far_kv, far_kv)
+    )(core, mine, limits, residual, queries, queries, own_kv, own_kv, far_kv, far_kv)
 
 
 def combine_kernel(parts_ref, out_ref):
@@ -201,36 +201,60 @@
 
 
 def pack_kernel(
-    out_ref, gate_ref, up_ref, down_ref, pages_ref, fresh_ref, weights_ref, kv_ref, spread_ref
+    lens_ref,
+    offset_ref,
+    table_ref,
+    shared_ref,
+    out_ref,
+    gate_ref,
+    up_ref,
+    down_ref,
+    pages_ref,
+    fresh_ref,
+    weights_ref,
+    kv_ref,
+    spread_ref,
+    limit_ref,
 ):
-    units = gate_ref.shape[1]
-    weights_ref[:, :HEAD] = out_ref[:HEAD, :]
-    weights_ref[:, HEAD : 2 * HEAD] = out_ref[HEAD:, :]
-    weights_ref[:, 2 * HEAD : 2 * HEAD + units] = gate_ref[...]
-    weights_ref[:, 2 * HEAD + units :] = up_ref[...]
+    column = 0
+    for source in (out_ref, gate_ref, up_ref):
+        for row in range(0, source.shape[0], HEAD):
+            width = source.shape[1]
+            weights_ref[:, column : column + width] = source[row : row + HEAD, :]
+            column += width
+    for copy in range(spread_ref.shape[0]):
+        spread_ref[copy] = down_ref[...]
     for page in range(OWN_PAGES):
         kv_ref[page * PAGE : (page + 1) * PAGE, :] = pages_ref[page]
-    rest = FRESH_PAD - fresh_ref.shape[0]
+    own_rows = fresh_ref.shape[0]
+    rest = FRESH_PAD - own_rows
     fresh = fresh_ref[...]
     if rest:
         fresh = jnp.concatenate([fresh, jnp.zeros((rest, fresh.shape[1]), jnp.bfloat16)], axis=0)
     kv_ref[OWN_PAGES * PAGE :, :] = fresh
-    for copy in range(spread_ref.shape[0]):
-        spread_ref[copy] = down_ref[...]
-
-
-def pack(out_weight, gate_weight, up_weight, down_weight, pages, fresh, copies):
-    width = 2 * HEAD + 2 * gate_weight.shape[1]
+    core = lax.axis_index("c")
+    mine = 2 * lax.axis_index("z") + core
+    sides = (mine, mine + 1 - 2 * core)
+    page_ids = [side * OWN_PAGES + page for side in sides for page in range(OWN_PAGES)]
+    fill_limits(page_ids, lens_ref, offset_ref, table_ref, shared_ref, limit_ref)
+
+
+def pack(copies, lens, offset, table, shared, weights, down_weight, pages, fresh):
+    width = sum((piece.shape[0] // HEAD) * piece.shape[1] for piece in weights)
+    smem = pl.BlockSpec(memory_space=pltpu.SMEM)
+    vmem = pl.BlockSpec(memory_space=pltpu.VMEM)
     return pl.pallas_call(
         pack_kernel,
+        in_specs=[smem] * 2 + [vmem] * 8,
         out_shape=(
             jax.ShapeDtypeStruct((HEAD, width), jnp.bfloat16),
             jax.ShapeDtypeStruct((KEYS, fresh.shape[1]), jnp.bfloat16),
             jax.ShapeDtypeStruct((copies,) + down_weight.shape, jnp.bfloat16),
+            jax.ShapeDtypeStruct((2 * OWN_PAGES, ROWS), jnp.int32),
         ),
         compiler_params=WIDE_LIMIT,
         name="pack",
-    )(out_weight, gate_weight, up_weight, down_weight, pages, fresh)
+    )(lens, offset, table, shared, *weights, down_weight, pages, fresh)
 
 
 def out_kernel(place_ref, attended_ref, weights_ref, *rest):
@@ -264,7 +288,7 @@
     )(half, attended, weights, *(() if far is None else (far,)))
 
 
-def norm_kernel(place_ref, parts_ref, residual_ref, gain_ref, updated_ref, sent_ref):
+def norm_kernel(parts_ref, residual_ref, gain_ref, updated_ref, sent_ref):
     x_size, z_size = parts_ref.shape[:2]
     blocks = parts_ref.shape[4] // HEAD
     square = jnp.zeros((parts_ref.shape[3], 1), jnp.float32)
@@ -276,7 +300,7 @@
             for block in range(blocks):
                 column = ((core * blocks + block) * x_size + x) * HEAD
                 value = summed[:, block * HEAD : (block + 1) * HEAD]
-                value = value + residual_ref[0, :, column : column + HEAD].astype(jnp.float32)
+                value = value + residual_ref[:, column : column + HEAD]
                 square = square + jnp.sum(value * value, axis=1, keepdims=True)
                 updated_ref[:, column : column + HEAD] = value
     scale = lax.rsqrt(square / (2 * x_size * blocks * HEAD) + EPSILON)
@@ -292,30 +316,16 @@
                 sent_ref[x, z, core] = normed
 
 
-def add_and_norm(place, parts, residual, gain):
-    rows, width = parts.shape[3], residual.shape[2]
+def add_and_norm(parts, residual, gain):
     return pl.pallas_call(
         norm_kernel,
-        grid_spec=pltpu.PrefetchScalarGridSpec(
-            num_scalar_prefetch=1,
-            grid=(1,),
-            in_specs=[
-                pl.BlockSpec(parts.shape, lambda i, place: (0,) * 5),
-                pl.BlockSpec((1, rows, width), lambda i, place: (0, place[0], 0)),
-                pl.BlockSpec((1, width), lambda i, place: (0, 0)),
-            ],
-            out_specs=[
-                pl.BlockSpec((rows, width), lambda i, place: (0, 0)),
-                pl.BlockSpec(parts.shape, lambda i, place: (0,) * 5),
-            ],
-        ),
         out_shape=(
-            jax.ShapeDtypeStruct((rows, width), jnp.float32),
+            jax.ShapeDtypeStruct(residual.shape, jnp.float32),
             jax.ShapeDtypeStruct(parts.shape, jnp.bfloat16),
         ),
         compiler_params=LIMIT,
         name="add_and_norm",
-    )(place, parts, residual, gain.reshape(1, -1))
+    )(parts, residual, gain.reshape(1, -1))
 
 
 def times_down(hidden, down_ref):
@@ -425,22 +435,22 @@
     own_rows = fresh_kv.shape[1]
     half = y_size // 2
 
-    packed, own_kv, spread = pack(
-        out_weight, gate_weight, up_weight, down_weight, kv_pages[0], fresh_kv[0], x_size
-    )
-    weights = lax.all_gather(packed, "y", axis=0, tiled=True)
-    far_kv = swap(own_kv)
-    down = lax.all_to_all(spread, "x", 0, 0, tiled=True)
-    parts = attention(
-        near_half,
-        own_rows,
+    packed, own_kv, spread, limits = pack(
+        x_size,
         cache_lens,
         prefill_offsets,
         jnp.transpose(page_table, (2, 0, 1)),
         shared_pages,
-        queries[0],
-        own_kv,
-        far_kv,
+        (out_weight, gate_weight, up_weight),
+        down_weight,
+        kv_pages[0],
+        fresh_kv[0],
+    )
+    weights = lax.all_gather(packed, "y", axis=0, tiled=True)
+    far_kv = swap(own_kv)
+    down = lax.all_to_all(spread, "x", 0, 0, tiled=True)
+    parts, carried = attention(
+        near_half, mine.reshape(1), own_rows, limits, residual, queries[0], own_kv, far_kv
     )
     parts, down = lax.optimization_barrier((parts, down))
     down = lax.all_gather(down, "y", axis=0, tiled=True)
@@ -452,7 +462,7 @@
     parts = out_product(near_half, attended, weights, far)
     parts = lax.all_to_all(parts, ("x", "z", "c"), 0, 0, tiled=True)
     parts = parts.reshape(x_size, z_size, 2, own_rows, half * HEAD)
-    updated, sent = add_and_norm(mine.reshape(1), parts, residual, norm_gain)
+    updated, sent = add_and_norm(parts, carried, norm_gain)
     near_rows = lax.all_to_all(
         sent.reshape(x_size * ROWS, half * HEAD), ("x", "z", "c"), 0, 0, tiled=True
     )
@@ -463,7 +473,8 @@
         return jnp.dot(rows, piece[:, 2 * HEAD :], preferred_element_type=jnp.float32)
 
     gated = partial(near_rows, core) + partial(far_rows, 1 - core)
-    gated = lax.all_to_all(gated.astype(jnp.bfloat16), "x", 0, 0, tiled=True)
+    gated, down = lax.optimization_barrier((gated.astype(jnp.bfloat16), down))
+    gated = lax.all_to_all(gated, "x", 0, 0, tiled=True)
     gated = gated.reshape(x_size, ROWS, gated.shape[1])
     hidden, far = hidden_product(far_half, gated, down)
     parts = down_product(near_half, hidden, down, swap(far))

time: 182 us -> 177 us (0.973)
  blocking collectives: 66 us -> 102 us
  waiting for transfers between devices: 38.9 us -> 11.3 us
  starting transfers between devices: 36.6 us -> 27.3 us
  local copies, waits for them, and re-layouts: 8.54 us -> 5.07 us
    all_to_all x0 -> x2, blocking collectives: none -> 37.4 us  [the longest x1 21.5 us: local(): parts = lax.all_to_all(parts, ('x', 'z', 'c'), 0, 0, tiled=True)]
    all_to_all x2 -> x0, waiting for transfers between devices: 29.3 us -> none  [the longest x1 17.4 us: local(): parts = lax.all_to_all(parts, ('x', 'z', 'c'), 0, 0, tiled=True)]
    all_to_all x2 -> x0, starting transfers between devices: 8.67 us -> none  [the longest x1 4.57 us: local(): parts = lax.all_to_all(parts, ('x', 'z', 'c'), 0, 0, tiled=True)]
    unnamed x24 -> x16, local copies, waits for them, and re-layouts: 8.54 us -> 5.07 us
  transfers between devices with their start and end apart: 10 -> 8, of which waited for: 6 -> 5; matrix products, arithmetic and copies ran while one was open for 1% -> 1% of each run, Pallas kernels for 5% -> 5%
where the time goes in v3:
time: 177 us; the launch traced here: 176 us
  blocking collectives  102 us (58%)
  starting transfers between devices  27.3 us (15%)
  between operations  14.2 us (8%)
  Pallas kernels  13.9 us (8%)
  waiting for transfers between devices  11.3 us (6%)
  local copies, waits for them, and re-layouts  5.07 us (3%)
    all_to_all x1, blocking collectives, local(): lax.all_to_all(sent.reshape(x_size * ROWS, half * HEAD), ('x', 'z', 'c'),...  23.4 us
    all_to_all x1, blocking collectives, local(): parts = lax.all_to_all(parts, ('x', 'z', 'c'), 0, 0, tiled=True)  21.5 us
    all_to_all x1, blocking collectives, local(): parts = lax.all_to_all(parts, 'z', 0, 0, tiled=True)  21.1 us
    ppermute x4, starting transfers between devices, swap(): return lax.ppermute(value, 'c', [(0, 1), (1, 0)])  20.4 us
    all_to_all x1, blocking collectives, local(): parts = lax.all_to_all(parts, ('z', 'c'), 0, 0, tiled=True)  20.3 us
    all_to_all x1, blocking collectives, local(): gated = lax.all_to_all(gated, 'x', 0, 0, tiled=True)  15.9 us
    pallas_call x1, Pallas kernels, attention(): pl.pallas_call(functools.partial(attention_kernel, own_rows), grid_spec=p...  5.58 us
    all_to_all x1, waiting for transfers between devices, local(): attended = lax.all_to_all(combine(parts, x_size), 'x', 0, 0, tiled=True)  5.49 us
  transfers between devices with their start and end apart: 8, of which 5 were waited for; matrix products, arithmetic and copies ran while one was open for 1% of the time, Pallas kernels for 5%

profile of v3, /device:TPU:1, one launch (start us, length us, event | category | flops | bytes accessed | tf_op | source)
XLA Modules:
  0.0 175.8 jit_solution(12971068524536758964)
XLA Ops:
  6.5 0.0 all-gather.3.cloned.1.call-start
  7.2 2.4 %pack.1 = (bf16[128,1024]{1,0:T(8,128)(2,1)}, bf16[272,1024]{1,0:T(8,128)(2,1)}, bf16[4,384,128]{2,1,0:T(8,128)(2,1)}, s32[4,128]{1,0:T(4,128)}) custom-call(s32[1,16]{1,0:T(1,128)} %lens_ref.1, s32[1]{0:T(128)S(6)} %copy.14.offset_ref, s32[12,1,16]{2,1,0:T(1,128)} %bitcast.40, s32[1,4]{1,0:T(1,128)} %shared_ref.1, bf16[256,128]{1,0:T(8,128)(2,1)} %out_ref.1, ...), custom_call_target="tpu_custom_call" | custom-call | tf_op jit(solution)/shard_map/pack/pallas_call | solution.py:246
  9.6 0.0 all-gather.3.cloned.1.call-update
  9.6 8.8 %collective-permute-start = (bf16[272,1024]{1,0:T(8,128)(2,1)}, bf16[272,1024]{1,0:T(8,128)(2,1)S(1)}, u32[]{:S(2)}, u32[]{:S(2)}) collective-permute-start(bf16[272,1024]{1,0:T(8,128)(2,1)} %get-tuple-element.20.own_key.own_value), channel_id=1, source_target_pairs={{0,1},{1,0},{2,3},{3,2},{4,5},{5,4},{6,7},{7,6},{8,9},{9,8},{10,11... | collective-permute-start | bytes 1671176 | tf_op jit(solution)/shard_map/ppermute | solution.py:413
  18.4 3.5 %all-to-all-start = ((bf16[4,384,128]{2,1,0:T(8,128)(2,1)}), bf16[4,384,128]{2,1,0:T(8,128)(2,1)S(1)}, u32[]{:S(2)}, u32[]{:S(2)}) async-start(bf16[4,384,128]{2,1,0:T(8,128)(2,1)} %get-tuple-element.22), calls=%async_computation | async-start | bytes 786432 | tf_op jit(solution)/shard_map/all_to_all | solution.py:451
  21.9 0.0 all-gather.5.cloned.1.call-start
  22.0 0.0 collective-permute-done.far_key.far_value
  22.0 0.0 copy-start.6
  22.0 0.8 copy-done.6
  22.8 5.6 %attention.1 = (bf16[8,272,128]{2,1,0:T(8,128)(2,1)}, f32[8,4096]{1,0:T(8,128)}) custom-call(s32[1]{0:T(128)} %bitcast.core_ref.place_ref.half_ref, s32[1]{0:T(128)} %bitcast.1.mine_ref, s32[4,128]{1,0:T(4,128)} %get-tuple-element.19.limit_ref, bf16[1,128,4096]{2,1,0:T(8,128)(2,1)} %residual_ref.1, bf16[128,4096]{1,0:T(8,128)(2,1)} %bitcast.32, ...), custom_call_target="tpu_custom_call" | custom-call | tf_op jit(solution)/shard_map/attention/pallas_call | solution.py:141
  28.4 1.7 all-to-all-done
  30.1 0.0 copy-start.7
  30.1 0.8 copy-done.7
  30.9 0.0 all-gather.5.cloned.1.call-update
  30.9 21.1 %all_to_all.54.parts_ref = bf16[8,272,128]{2,1,0:T(8,128)(2,1)S(1)} all-to-all(bf16[8,272,128]{2,1,0:T(8,128)(2,1)} %get-tuple-element.23), channel_id=1, replica_groups=mesh['y'=8,'x'=4,'z'=8,'c'=2] {'z'}, dimensions={0} | all-to-all | bytes 1114112 | tf_op jit(solution)/shard_map/all_to_all | solution.py:457
  52.0 0.9 combine.1
  52.9 3.4 %all-to-all-start.2 = ((bf16[4,128,256]{2,1,0:T(8,128)(2,1)}), bf16[4,128,256]{2,1,0:T(8,128)(2,1)S(1)}, u32[]{:S(2)}, u32[]{:S(2)}) async-start(bf16[4,128,256]{2,1,0:T(8,128)(2,1)} %combine.1), calls=%async_computation.2 | async-start | bytes 524288 | tf_op jit(solution)/shard_map/all_to_all | solution.py:458
  56.3 5.5 %all-to-all-done.2 = bf16[4,128,256]{2,1,0:T(8,128)(2,1)S(1)} async-done(((bf16[4,128,256]{2,1,0:T(8,128)(2,1)}), bf16[4,128,256]{2,1,0:T(8,128)(2,1)S(1)}, u32[]{:S(2)}, u32[]{:S(2)}) %all-to-all-start.2) | async-done | bytes 262176 | tf_op jit(solution)/shard_map/all_to_all | solution.py:458
  61.8 0.0 all-gather.3.cloned.1.call-done.weights_ref
  61.8 1.6 copy-done
  63.4 1.1 out_product.2
  64.5 0.0 copy-start.4
  64.5 0.0 copy-start.5
  64.5 6.2 %collective-permute-start.1 = (bf16[512,512]{1,0:T(8,128)(2,1)S(1)}, bf16[512,512]{1,0:T(8,128)(2,1)S(1)}, u32[]{:S(2)}, u32[]{:S(2)}) collective-permute-start(bf16[512,512]{1,0:T(8,128)(2,1)S(1)} %out_product.2), channel_id=1, source_target_pairs={{0,1},{1,0},{2,3},{3,2},{4,5},{5,4},{6,7},{7,6},{8,9},{9,8},{10,11... | collective-permute-start | bytes 1572872 | tf_op jit(solution)/shard_map/ppermute | solution.py:413
  70.7 1.5 collective-permute-done.1.rest_0_
  72.2 1.2 out_product.3
  73.4 0.0 copy-start.1
  73.4 21.5 %all_to_all.55 = bf16[64,8,512]{2,1,0:T(8,128)(2,1)S(1)} all-to-all(bf16[64,8,512]{2,1,0:T(8,128)(2,1)S(1)} %bitcast.29), channel_id=1, replica_groups=mesh['y'=8,'x'=4,'z'=8,'c'=2] {'x','z','c'}, dimensions={0} | all-to-all | bytes 1048576 | tf_op jit(solution)/shard_map/all_to_all | solution.py:463
  94.9 0.0 copy-done.4
  94.9 0.0 copy-done.5
  94.9 0.2 add_and_norm.1
  95.1 23.4 %all_to_all.56 = bf16[64,8,512]{2,1,0:T(8,128)(2,1)S(1)} all-to-all(bf16[64,8,512]{2,1,0:T(8,128)(2,1)S(1)} %bitcast.30), channel_id=1, replica_groups=mesh['y'=8,'x'=4,'z'=8,'c'=2] {'x','z','c'}, dimensions={0} | all-to-all | bytes 1048576 | tf_op jit(solution)/shard_map/all_to_all | solution.py:466
  118.5 2.2 %collective-permute-start.2 = (bf16[512,512]{1,0:T(8,128)(2,1)S(1)}, bf16[512,512]{1,0:T(8,128)(2,1)S(1)}, u32[]{:S(2)}, u32[]{:S(2)}) collective-permute-start(bf16[512,512]{1,0:T(8,128)(2,1)S(1)} %bitcast.34), channel_id=1, source_target_pairs={{0,1},{1,0},{2,3},{3,2},{4,5},{5,4},{6,7},{7,6},{8,9},{9,8},{10,11... | collective-permute-start | bytes 1572872 | tf_op jit(solution)/shard_map/ppermute | solution.py:413
  120.7 0.0 copy-done.1
  120.7 0.6 fusion.1
  121.3 1.0 collective-permute-done.2
  122.3 0.6 add_convert_fusion
  122.9 0.0 all-gather.5.cloned.1.call-done.down_ref
  122.9 15.9 %all_to_all.57.parts_ref = bf16[4,128,768]{2,1,0:T(8,128)(2,1)S(1)} all-to-all(bf16[4,128,768]{2,1,0:T(8,128)(2,1)S(1)} %bitcast.35), channel_id=1, replica_groups=mesh['y'=8,'x'=4,'z'=8,'c'=2] {'x'}, dimensions={0} | all-to-all | bytes 1572864 | tf_op jit(solution)/shard_map/all_to_all | solution.py:477
  138.8 1.9 %copy-done.2 = bf16[32,384,128]{2,1,0:T(8,128)(2,1)S(1)} copy-done((bf16[32,384,128]{2,1,0:T(8,128)(2,1)S(1)}, bf16[32,384,128]{2,1,0:T(8,128)(2,1)}, u32[]{:S(2)}) %copy-start.2) | copy-done | bytes 3145752
  140.7 1.3 hidden_product.1
  142.0 3.2 %collective-permute-start.3 = (bf16[128,2048]{1,0:T(8,128)(2,1)S(1)}, bf16[128,2048]{1,0:T(8,128)(2,1)S(1)}, u32[]{:S(2)}, u32[]{:S(2)}) collective-permute-start(bf16[128,2048]{1,0:T(8,128)(2,1)S(1)} %get-tuple-element.32), channel_id=1, source_target_pairs={{0,1},{1,0},{2,3},{3,2},{4,5},{5,4},{6,7},{7,6},{8,9},{9,8},{10,11... | collective-permute-start | bytes 1572872 | tf_op jit(solution)/shard_map/ppermute | solution.py:413
  145.2 1.5 collective-permute-done.3.far_ref
  146.7 0.0 copy-done.3
  146.7 1.2 down_product.1
  147.9 20.3 %all_to_all.58 = bf16[16,8,2048]{2,1,0:T(8,128)(2,1)S(1)} all-to-all(bf16[16,8,2048]{2,1,0:T(8,128)(2,1)S(1)} %bitcast.27), channel_id=1, replica_groups=mesh['y'=8,'x'=4,'z'=8,'c'=2] {'z','c'}, dimensions={0} | all-to-all | bytes 1048576 | tf_op jit(solution)/shard_map/all_to_all | solution.py:481
  168.2 0.1 convert_reduce_fusion
  168.3 0.7 fusion.3
  (3 shorter events, 0.0 us)
Async XLA Ops:
  6.5 55.2 %all-gather.3.cloned.1.call-start = ((), (), s32[]{:S(2)}) async-start(), calls=%async_computation.7 | async-start | bytes 2359296 | tf_op jit(solution)/shard_map/all_gather | solution.py:449
  9.6 12.3 %collective-permute-start = (bf16[272,1024]{1,0:T(8,128)(2,1)}, bf16[272,1024]{1,0:T(8,128)(2,1)S(1)}, u32[]{:S(2)}, u32[]{:S(2)}) collective-permute-start(bf16[272,1024]{1,0:T(8,128)(2,1)} %get-tuple-element.20.own_key.own_value), channel_id=1, source_target_pairs={{0,1},{1,0},{2,3},{3,2},{4,5},{5,4},{6,7},{7,6},{8,9},{9,8},{10,11... | collective-permute-start | bytes 1671176 | tf_op jit(solution)/shard_map/ppermute | solution.py:413
  18.4 11.7 %all-to-all-start = ((bf16[4,384,128]{2,1,0:T(8,128)(2,1)}), bf16[4,384,128]{2,1,0:T(8,128)(2,1)S(1)}, u32[]{:S(2)}, u32[]{:S(2)}) async-start(bf16[4,384,128]{2,1,0:T(8,128)(2,1)} %get-tuple-element.22), calls=%async_computation | async-start | bytes 786432 | tf_op jit(solution)/shard_map/all_to_all | solution.py:451
  21.9 101.0 %all-gather.5.cloned.1.call-start = ((), (), s32[]{:S(2)}) async-start(), calls=%async_computation.8 | async-start | bytes 3538944 | tf_op jit(solution)/shard_map/all_gather | solution.py:456
  22.0 0.8 copy-start.6
  30.1 0.8 copy-start.7
  52.9 8.9 %all-to-all-start.2 = ((bf16[4,128,256]{2,1,0:T(8,128)(2,1)}), bf16[4,128,256]{2,1,0:T(8,128)(2,1)S(1)}, u32[]{:S(2)}, u32[]{:S(2)}) async-start(bf16[4,128,256]{2,1,0:T(8,128)(2,1)} %combine.1), calls=%async_computation.2 | async-start | bytes 524288 | tf_op jit(solution)/shard_map/all_to_all | solution.py:458
  61.8 1.6 copy-start
  64.5 30.4 %copy-start.4 = (f32[8,4096]{1,0:T(8,128)S(1)}, f32[8,4096]{1,0:T(8,128)}, u32[]{:S(2)}) copy-start(f32[8,4096]{1,0:T(8,128)} %get-tuple-element.25.residual_ref) | copy-start | bytes 393220
  64.5 30.4 %copy-start.5 = (f32[4096]{0:T(1024)S(1)}, f32[4096]{0:T(1024)}, u32[]{:S(2)}) copy-start(f32[4096]{0:T(1024)} %param.17) | copy-start | bytes 49156
  64.5 7.7 %collective-permute-start.1 = (bf16[512,512]{1,0:T(8,128)(2,1)S(1)}, bf16[512,512]{1,0:T(8,128)(2,1)S(1)}, u32[]{:S(2)}, u32[]{:S(2)}) collective-permute-start(bf16[512,512]{1,0:T(8,128)(2,1)S(1)} %out_product.2), channel_id=1, source_target_pairs={{0,1},{1,0},{2,3},{3,2},{4,5},{5,4},{6,7},{7,6},{8,9},{9,8},{10,11... | collective-permute-start | bytes 1572872 | tf_op jit(solution)/shard_map/ppermute | solution.py:413
  73.4 47.3 %copy-start.1 = (bf16[1024,1024]{1,0:T(8,128)(2,1)S(1)}, bf16[1024,1024]{1,0:T(8,128)(2,1)}, u32[]{:S(2)}) copy-start(bf16[1024,1024]{1,0:T(8,128)(2,1)} %all-gather.3.cloned.1.call-done.weights_ref) | copy-start | bytes 6291460
  118.5 3.8 %collective-permute-start.2 = (bf16[512,512]{1,0:T(8,128)(2,1)S(1)}, bf16[512,512]{1,0:T(8,128)(2,1)S(1)}, u32[]{:S(2)}, u32[]{:S(2)}) collective-permute-start(bf16[512,512]{1,0:T(8,128)(2,1)S(1)} %bitcast.34), channel_id=1, source_target_pairs={{0,1},{1,0},{2,3},{3,2},{4,5},{5,4},{6,7},{7,6},{8,9},{9,8},{10,11... | collective-permute-start | bytes 1572872 | tf_op jit(solution)/shard_map/ppermute | solution.py:413
  138.8 1.9 %copy-start.2 = (bf16[32,384,128]{2,1,0:T(8,128)(2,1)S(1)}, bf16[32,384,128]{2,1,0:T(8,128)(2,1)}, u32[]{:S(2)}) copy-start(bf16[32,384,128]{2,1,0:T(8,128)(2,1)} %all-gather.5.cloned.1.call-done.down_ref) | copy-start | bytes 9437188
  140.7 6.0 %copy-start.3 = (bf16[32,384,128]{2,1,0:T(8,128)(2,1)S(1)}, bf16[32,384,128]{2,1,0:T(8,128)(2,1)}, u32[]{:S(2)}) copy-start(bf16[32,384,128]{2,1,0:T(8,128)(2,1)} %all-gather.5.cloned.1.call-done.down_ref) | copy-start | bytes 9437188
  142.0 4.7 %collective-permute-start.3 = (bf16[128,2048]{1,0:T(8,128)(2,1)S(1)}, bf16[128,2048]{1,0:T(8,128)(2,1)S(1)}, u32[]{:S(2)}, u32[]{:S(2)}) collective-permute-start(bf16[128,2048]{1,0:T(8,128)(2,1)S(1)} %get-tuple-element.32), channel_id=1, source_target_pairs={{0,1},{1,0},{2,3},{3,2},{4,5},{5,4},{6,7},{7,6},{8,9},{9,8},{10,11... | collective-permute-start | bytes 1572872 | tf_op jit(solution)/shard_map/ppermute | solution.py:413
Sparse Core Ops, SparseCore 0:
  9.8 45.3 all-gather.2
  57.3 49.7 all-gather.4

commit v4 on v3

--- a/solution.py
+++ b/solution.py
@@ -328,6 +328,38 @@
     )(parts, residual, gain.reshape(1, -1))
 
 
+def gate_kernel(near_ref, far_ref, near_rows, far_rows, near_weights, far_weights, gated_ref):
+    product = jnp.dot(near_rows[...], near_weights[...], preferred_element_type=jnp.float32)
+    product = product + jnp.dot(
+        far_rows[...], far_weights[...], preferred_element_type=jnp.float32
+    )
+    gated_ref[...] = product.astype(jnp.bfloat16)
+
+
+def gate_product(near_half, far_half, near_rows, far_rows, weights):
+    rows, depth = near_rows.shape
+    tile = 2 * HEAD
+    steps = weights.shape[1] // tile - 1
+    whole = pl.BlockSpec((rows, depth), lambda i, near, far: (0, 0))
+    return pl.pallas_call(
+        gate_kernel,
+        grid_spec=pltpu.PrefetchScalarGridSpec(
+            num_scalar_prefetch=2,
+            grid=(steps,),
+            in_specs=[
+                whole,
+                whole,
+                pl.BlockSpec((depth, tile), lambda i, near, far: (near[0], 1 + i)),
+                pl.BlockSpec((depth, tile), lambda i, near, far: (far[0], 1 + i)),
+            ],
+            out_specs=pl.BlockSpec((rows, tile), lambda i, near, far: (0, i)),
+        ),
+        out_shape=jax.ShapeDtypeStruct((rows, steps * tile), jnp.bfloat16),
+        compiler_params=LIMIT,
+        name="gate_product",
+    )(near_half, far_half, near_rows, far_rows, weights, weights)
+
+
 def times_down(hidden, down_ref):
     return jnp.concatenate(
         [
@@ -458,22 +490,18 @@
     attended = lax.all_to_all(combine(parts, x_size), "x", 0, 0, tiled=True)
     attended = attended.reshape(x_size * ROWS, 2 * HEAD)
 
-    far = swap(out_product(far_half, attended, weights))
-    parts = out_product(near_half, attended, weights, far)
+    columns = weights[:, : 2 * HEAD]
+    far = swap(out_product(far_half, attended, columns))
+    parts = out_product(near_half, attended, columns, far)
     parts = lax.all_to_all(parts, ("x", "z", "c"), 0, 0, tiled=True)
     parts = parts.reshape(x_size, z_size, 2, own_rows, half * HEAD)
     updated, sent = add_and_norm(parts, carried, norm_gain)
     near_rows = lax.all_to_all(
         sent.reshape(x_size * ROWS, half * HEAD), ("x", "z", "c"), 0, 0, tiled=True
     )
-    far_rows = swap(near_rows)
-
-    def partial(rows, which):
-        piece = lax.dynamic_slice_in_dim(weights, which * half * HEAD, half * HEAD, 0)
-        return jnp.dot(rows, piece[:, 2 * HEAD :], preferred_element_type=jnp.float32)
-
-    gated = partial(near_rows, core) + partial(far_rows, 1 - core)
-    gated, down = lax.optimization_barrier((gated.astype(jnp.bfloat16), down))
+    far_rows, down = lax.optimization_barrier((swap(near_rows), down))
+
+    gated = gate_product(near_half, far_half, near_rows, far_rows, weights)
     gated = lax.all_to_all(gated, "x", 0, 0, tiled=True)
     gated = gated.reshape(x_size, ROWS, gated.shape[1])
     hidden, far = hidden_product(far_half, gated, down)

time: 177 us -> 175 us (0.989)
  local copies, waits for them, and re-layouts: 5.07 us -> 2.64 us
    unnamed x16 -> x12, local copies, waits for them, and re-layouts: 5.07 us -> 1.57 us
where the time goes in v4:
time: 175 us; the launch traced here: 174 us
  blocking collectives  103 us (59%)
  starting transfers between devices  27.2 us (16%)
  Pallas kernels  15.4 us (9%)
  between operations  14.2 us (8%)
  waiting for transfers between devices  10.7 us (6%)
  local copies, waits for them, and re-layouts  2.64 us (2%)
    all_to_all x1, blocking collectives, local(): lax.all_to_all(sent.reshape(x_size * ROWS, half * HEAD), ('x', 'z', 'c'),...  23.4 us
    all_to_all x1, blocking collectives, local(): parts = lax.all_to_all(parts, ('x', 'z', 'c'), 0, 0, tiled=True)  22.4 us
    all_to_all x1, blocking collectives, local(): parts = lax.all_to_all(parts, 'z', 0, 0, tiled=True)  21.1 us
    all_to_all x1, blocking collectives, local(): parts = lax.all_to_all(parts, ('z', 'c'), 0, 0, tiled=True)  20.3 us
    ppermute x4, starting transfers between devices, swap(): return lax.ppermute(value, 'c', [(0, 1), (1, 0)])  20.2 us
    all_to_all x1, blocking collectives, local(): gated = lax.all_to_all(gated, 'x', 0, 0, tiled=True)  15.9 us
    pallas_call x1, Pallas kernels, attention(): pl.pallas_call(functools.partial(attention_kernel, own_rows), grid_spec=p...  5.57 us
    ppermute x4, waiting for transfers between devices, swap(): return lax.ppermute(value, 'c', [(0, 1), (1, 0)])  4.56 us
  transfers between devices with their start and end apart: 8, of which 5 were waited for; matrix products, arithmetic and copies ran while one was open for 1% of the time, Pallas kernels for 5%

profile of v4, /device:TPU:1, one launch (start us, length us, event | category | flops | bytes accessed | tf_op | source)
XLA Modules:
  0.0 174.0 jit_solution(10838155270956896687)
XLA Ops:
  6.5 0.0 all-gather.3.cloned.1.call-start
  7.2 2.4 %pack.1 = (bf16[128,1024]{1,0:T(8,128)(2,1)}, bf16[272,1024]{1,0:T(8,128)(2,1)}, bf16[4,384,128]{2,1,0:T(8,128)(2,1)}, s32[4,128]{1,0:T(4,128)}) custom-call(s32[1,16]{1,0:T(1,128)} %lens_ref.1, s32[1]{0:T(128)S(6)} %copy.14.offset_ref, s32[12,1,16]{2,1,0:T(1,128)} %bitcast.38, s32[1,4]{1,0:T(1,128)} %shared_ref.1, bf16[256,128]{1,0:T(8,128)(2,1)} %out_ref.1, ...), custom_call_target="tpu_custom_call" | custom-call | tf_op jit(solution)/shard_map/pack/pallas_call | solution.py:246
  9.6 0.0 all-gather.3.cloned.1.call-update
  9.6 8.8 %collective-permute-start = (bf16[272,1024]{1,0:T(8,128)(2,1)}, bf16[272,1024]{1,0:T(8,128)(2,1)S(1)}, u32[]{:S(2)}, u32[]{:S(2)}) collective-permute-start(bf16[272,1024]{1,0:T(8,128)(2,1)} %get-tuple-element.20.own_key.own_value), channel_id=1, source_target_pairs={{0,1},{1,0},{2,3},{3,2},{4,5},{5,4},{6,7},{7,6},{8,9},{9,8},{10,11... | collective-permute-start | bytes 1671176 | tf_op jit(solution)/shard_map/ppermute | solution.py:445
  18.4 3.5 %all-to-all-start = ((bf16[4,384,128]{2,1,0:T(8,128)(2,1)}), bf16[4,384,128]{2,1,0:T(8,128)(2,1)S(1)}, u32[]{:S(2)}, u32[]{:S(2)}) async-start(bf16[4,384,128]{2,1,0:T(8,128)(2,1)} %get-tuple-element.22), calls=%async_computation | async-start | bytes 786432 | tf_op jit(solution)/shard_map/all_to_all | solution.py:483
  21.9 0.0 all-gather.5.cloned.1.call-start
  22.0 0.0 collective-permute-done.far_key.far_value
  22.0 0.0 copy-start.4
  22.0 0.8 copy-done.4
  22.8 5.6 %attention.1 = (bf16[8,272,128]{2,1,0:T(8,128)(2,1)}, f32[8,4096]{1,0:T(8,128)}) custom-call(s32[1]{0:T(128)} %bitcast.core_ref.place_ref.near_ref.half_ref, s32[1]{0:T(128)} %bitcast.1.mine_ref, s32[4,128]{1,0:T(4,128)} %get-tuple-element.19.limit_ref, bf16[1,128,4096]{2,1,0:T(8,128)(2,1)} %residual_ref.1, bf16[128,4096]{1,0:T(8,128)(2,1)} %bitcast.32, ...), custom_call_target="tpu_custom_call" | custom-call | tf_op jit(solution)/shard_map/attention/pallas_call | solution.py:141
  28.3 1.7 %all-to-all-done = bf16[4,384,128]{2,1,0:T(8,128)(2,1)S(1)} async-done(((bf16[4,384,128]{2,1,0:T(8,128)(2,1)}), bf16[4,384,128]{2,1,0:T(8,128)(2,1)S(1)}, u32[]{:S(2)}, u32[]{:S(2)}) %all-to-all-start) | async-done | bytes 393248 | tf_op jit(solution)/shard_map/all_to_all | solution.py:483
  30.1 0.0 copy-start.5
  30.1 0.7 copy-done.5
  30.8 0.0 all-gather.5.cloned.1.call-update
  30.9 21.1 %all_to_all.53.parts_ref = bf16[8,272,128]{2,1,0:T(8,128)(2,1)S(1)} all-to-all(bf16[8,272,128]{2,1,0:T(8,128)(2,1)} %get-tuple-element.23), channel_id=1, replica_groups=mesh['y'=8,'x'=4,'z'=8,'c'=2] {'z'}, dimensions={0} | all-to-all | bytes 1114112 | tf_op jit(solution)/shard_map/all_to_all | solution.py:489
  51.9 0.0 copy-start.2
  51.9 0.0 copy-start.3
  51.9 0.9 combine.1
  52.9 3.4 %all-to-all-start.2 = ((bf16[4,128,256]{2,1,0:T(8,128)(2,1)}), bf16[4,128,256]{2,1,0:T(8,128)(2,1)S(1)}, u32[]{:S(2)}, u32[]{:S(2)}) async-start(bf16[4,128,256]{2,1,0:T(8,128)(2,1)} %combine.1), calls=%async_computation.2 | async-start | bytes 524288 | tf_op jit(solution)/shard_map/all_to_all | solution.py:490
  56.3 0.0 all-gather.3.cloned.1.call-done.near_weights.far_weights
  56.3 1.1 slice.4.weights_ref
  57.4 0.0 copy-start.1
  57.4 4.4 %all-to-all-done.2 = bf16[4,128,256]{2,1,0:T(8,128)(2,1)S(1)} async-done(((bf16[4,128,256]{2,1,0:T(8,128)(2,1)}), bf16[4,128,256]{2,1,0:T(8,128)(2,1)S(1)}, u32[]{:S(2)}, u32[]{:S(2)}) %all-to-all-start.2) | async-done | bytes 262176 | tf_op jit(solution)/shard_map/all_to_all | solution.py:490
  61.8 1.0 out_product.2
  62.8 6.0 %collective-permute-start.1 = (bf16[512,512]{1,0:T(8,128)(2,1)S(1)}, bf16[512,512]{1,0:T(8,128)(2,1)S(1)}, u32[]{:S(2)}, u32[]{:S(2)}) collective-permute-start(bf16[512,512]{1,0:T(8,128)(2,1)S(1)} %out_product.2), channel_id=1, source_target_pairs={{0,1},{1,0},{2,3},{3,2},{4,5},{5,4},{6,7},{7,6},{8,9},{9,8},{10,11... | collective-permute-start | bytes 1572872 | tf_op jit(solution)/shard_map/ppermute | solution.py:445
  68.9 1.5 collective-permute-done.1.rest_0_
  70.4 1.2 out_product.3
  71.5 22.4 %all_to_all.54 = bf16[64,8,512]{2,1,0:T(8,128)(2,1)S(1)} all-to-all(bf16[64,8,512]{2,1,0:T(8,128)(2,1)S(1)} %bitcast.29), channel_id=1, replica_groups=mesh['y'=8,'x'=4,'z'=8,'c'=2] {'x','z','c'}, dimensions={0} | all-to-all | bytes 1048576 | tf_op jit(solution)/shard_map/all_to_all | solution.py:496
  94.0 0.0 copy-done.2
  94.0 0.0 copy-done.3
  94.0 0.2 add_and_norm.1
  94.2 23.4 %all_to_all.55 = bf16[64,8,512]{2,1,0:T(8,128)(2,1)S(1)} all-to-all(bf16[64,8,512]{2,1,0:T(8,128)(2,1)S(1)} %bitcast.30), channel_id=1, replica_groups=mesh['y'=8,'x'=4,'z'=8,'c'=2] {'x','z','c'}, dimensions={0} | all-to-all | bytes 1048576 | tf_op jit(solution)/shard_map/all_to_all | solution.py:499
  117.6 2.2 %collective-permute-start.2 = (bf16[512,512]{1,0:T(8,128)(2,1)S(1)}, bf16[512,512]{1,0:T(8,128)(2,1)S(1)}, u32[]{:S(2)}, u32[]{:S(2)}) collective-permute-start(bf16[512,512]{1,0:T(8,128)(2,1)S(1)} %bitcast.25), channel_id=1, source_target_pairs={{0,1},{1,0},{2,3},{3,2},{4,5},{5,4},{6,7},{7,6},{8,9},{9,8},{10,11... | collective-permute-start | bytes 1572872 | tf_op jit(solution)/shard_map/ppermute | solution.py:445
  119.8 0.0 all-gather.5.cloned.1.call-done.down_ref
  119.9 0.0 copy-start
  119.9 1.5 collective-permute-done.2.far_rows
  121.4 0.0 copy-done.1
  121.4 1.6 gate_product.1
  123.0 15.9 %all_to_all.56.parts_ref = bf16[4,128,768]{2,1,0:T(8,128)(2,1)S(1)} all-to-all(bf16[4,128,768]{2,1,0:T(8,128)(2,1)S(1)} %bitcast.22), channel_id=1, replica_groups=mesh['y'=8,'x'=4,'z'=8,'c'=2] {'x'}, dimensions={0} | all-to-all | bytes 1572864 | tf_op jit(solution)/shard_map/all_to_all | solution.py:505
  138.9 0.0 copy-done
  138.9 1.3 hidden_product.1
  140.2 3.2 %collective-permute-start.3 = (bf16[128,2048]{1,0:T(8,128)(2,1)S(1)}, bf16[128,2048]{1,0:T(8,128)(2,1)S(1)}, u32[]{:S(2)}, u32[]{:S(2)}) collective-permute-start(bf16[128,2048]{1,0:T(8,128)(2,1)S(1)} %get-tuple-element.32), channel_id=1, source_target_pairs={{0,1},{1,0},{2,3},{3,2},{4,5},{5,4},{6,7},{7,6},{8,9},{9,8},{10,11... | collective-permute-start | bytes 1572872 | tf_op jit(solution)/shard_map/ppermute | solution.py:445
  143.4 1.5 collective-permute-done.3.far_ref
  144.9 1.2 down_product.1
  146.1 20.3 %all_to_all.57 = bf16[16,8,2048]{2,1,0:T(8,128)(2,1)S(1)} all-to-all(bf16[16,8,2048]{2,1,0:T(8,128)(2,1)S(1)} %bitcast.27), channel_id=1, replica_groups=mesh['y'=8,'x'=4,'z'=8,'c'=2] {'z','c'}, dimensions={0} | all-to-all | bytes 1048576 | tf_op jit(solution)/shard_map/all_to_all | solution.py:509
  166.4 0.1 convert_reduce_fusion
  166.5 0.7 fusion
Async XLA Ops:
  6.5 49.8 %all-gather.3.cloned.1.call-start = ((), (), s32[]{:S(2)}) async-start(), calls=%async_computation.7 | async-start | bytes 2359296 | tf_op jit(solution)/shard_map/all_gather | solution.py:481
  9.6 12.3 %collective-permute-start = (bf16[272,1024]{1,0:T(8,128)(2,1)}, bf16[272,1024]{1,0:T(8,128)(2,1)S(1)}, u32[]{:S(2)}, u32[]{:S(2)}) collective-permute-start(bf16[272,1024]{1,0:T(8,128)(2,1)} %get-tuple-element.20.own_key.own_value), channel_id=1, source_target_pairs={{0,1},{1,0},{2,3},{3,2},{4,5},{5,4},{6,7},{7,6},{8,9},{9,8},{10,11... | collective-permute-start | bytes 1671176 | tf_op jit(solution)/shard_map/ppermute | solution.py:445
  18.4 11.7 %all-to-all-start = ((bf16[4,384,128]{2,1,0:T(8,128)(2,1)}), bf16[4,384,128]{2,1,0:T(8,128)(2,1)S(1)}, u32[]{:S(2)}, u32[]{:S(2)}) async-start(bf16[4,384,128]{2,1,0:T(8,128)(2,1)} %get-tuple-element.22), calls=%async_computation | async-start | bytes 786432 | tf_op jit(solution)/shard_map/all_to_all | solution.py:483
  21.9 97.9 %all-gather.5.cloned.1.call-start = ((), (), s32[]{:S(2)}) async-start(), calls=%async_computation.8 | async-start | bytes 3538944 | tf_op jit(solution)/shard_map/all_gather | solution.py:488
  22.0 0.8 copy-start.4
  30.1 0.7 copy-start.5
  51.9 42.0 %copy-start.2 = (f32[8,4096]{1,0:T(8,128)S(1)}, f32[8,4096]{1,0:T(8,128)}, u32[]{:S(2)}) copy-start(f32[8,4096]{1,0:T(8,128)} %get-tuple-element.25.residual_ref) | copy-start | bytes 393220
  51.9 42.0 %copy-start.3 = (f32[4096]{0:T(1024)S(1)}, f32[4096]{0:T(1024)}, u32[]{:S(2)}) copy-start(f32[4096]{0:T(1024)} %param.17) | copy-start | bytes 49156
  52.9 8.9 %all-to-all-start.2 = ((bf16[4,128,256]{2,1,0:T(8,128)(2,1)}), bf16[4,128,256]{2,1,0:T(8,128)(2,1)S(1)}, u32[]{:S(2)}, u32[]{:S(2)}) async-start(bf16[4,128,256]{2,1,0:T(8,128)(2,1)} %combine.1), calls=%async_computation.2 | async-start | bytes 524288 | tf_op jit(solution)/shard_map/all_to_all | solution.py:490
  57.4 64.0 %copy-start.1 = (bf16[1024,1024]{1,0:T(8,128)(2,1)S(1)}, bf16[1024,1024]{1,0:T(8,128)(2,1)}, u32[]{:S(2)}) copy-start(bf16[1024,1024]{1,0:T(8,128)(2,1)} %all-gather.3.cloned.1.call-done.near_weights.far_weights) | copy-start | bytes 6291460
  62.8 7.6 %collective-permute-start.1 = (bf16[512,512]{1,0:T(8,128)(2,1)S(1)}, bf16[512,512]{1,0:T(8,128)(2,1)S(1)}, u32[]{:S(2)}, u32[]{:S(2)}) collective-permute-start(bf16[512,512]{1,0:T(8,128)(2,1)S(1)} %out_product.2), channel_id=1, source_target_pairs={{0,1},{1,0},{2,3},{3,2},{4,5},{5,4},{6,7},{7,6},{8,9},{9,8},{10,11... | collective-permute-start | bytes 1572872 | tf_op jit(solution)/shard_map/ppermute | solution.py:445
  117.6 3.8 %collective-permute-start.2 = (bf16[512,512]{1,0:T(8,128)(2,1)S(1)}, bf16[512,512]{1,0:T(8,128)(2,1)S(1)}, u32[]{:S(2)}, u32[]{:S(2)}) collective-permute-start(bf16[512,512]{1,0:T(8,128)(2,1)S(1)} %bitcast.25), channel_id=1, source_target_pairs={{0,1},{1,0},{2,3},{3,2},{4,5},{5,4},{6,7},{7,6},{8,9},{9,8},{10,11... | collective-permute-start | bytes 1572872 | tf_op jit(solution)/shard_map/ppermute | solution.py:445
  119.9 19.1 %copy-start = (bf16[32,384,128]{2,1,0:T(8,128)(2,1)S(1)}, bf16[32,384,128]{2,1,0:T(8,128)(2,1)}, u32[]{:S(2)}) copy-start(bf16[32,384,128]{2,1,0:T(8,128)(2,1)} %all-gather.5.cloned.1.call-done.down_ref) | copy-start | bytes 9437188
  140.2 4.7 %collective-permute-start.3 = (bf16[128,2048]{1,0:T(8,128)(2,1)S(1)}, bf16[128,2048]{1,0:T(8,128)(2,1)S(1)}, u32[]{:S(2)}, u32[]{:S(2)}) collective-permute-start(bf16[128,2048]{1,0:T(8,128)(2,1)S(1)} %get-tuple-element.32), channel_id=1, source_target_pairs={{0,1},{1,0},{2,3},{3,2},{4,5},{5,4},{6,7},{7,6},{8,9},{9,8},{10,11... | collective-permute-start | bytes 1572872 | tf_op jit(solution)/shard_map/ppermute | solution.py:445
Sparse Core Ops, SparseCore 0:
  9.7 45.3 all-gather.2
  57.3 49.6 all-gather.4

commit v5 on v4

--- a/solution.py
+++ b/solution.py
@@ -485,9 +485,11 @@
         near_half, mine.reshape(1), own_rows, limits, residual, queries[0], own_kv, far_kv
     )
     parts, down = lax.optimization_barrier((parts, down))
+    parts = lax.all_to_all(parts, "z", 0, 0, tiled=True)
+    combined = combine(parts, x_size)
+    down, _ = lax.optimization_barrier((down, combined))
     down = lax.all_gather(down, "y", axis=0, tiled=True)
-    parts = lax.all_to_all(parts, "z", 0, 0, tiled=True)
-    attended = lax.all_to_all(combine(parts, x_size), "x", 0, 0, tiled=True)
+    attended = lax.all_to_all(combined, "x", 0, 0, tiled=True)
     attended = attended.reshape(x_size * ROWS, 2 * HEAD)
 
     columns = weights[:, : 2 * HEAD]

time: 175 us -> 175 us (level)
  no operation moved by 1% of the time
where the time goes in v5:
time: 175 us; the launch traced here: 174 us
  blocking collectives  104 us (59%)
  starting transfers between devices  27.3 us (16%)
  Pallas kernels  15.4 us (9%)
  between operations  14.2 us (8%)
  waiting for transfers between devices  10.8 us (6%)
  local copies, waits for them, and re-layouts  1.91 us (1%)
    all_to_all x1, blocking collectives, local(): lax.all_to_all(sent.reshape(x_size * ROWS, half * HEAD), ('x', 'z', 'c'),...  23.4 us
    all_to_all x1, blocking collectives, local(): parts = lax.all_to_all(parts, ('x', 'z', 'c'), 0, 0, tiled=True)  23.1 us
    all_to_all x1, blocking collectives, local(): parts = lax.all_to_all(parts, 'z', 0, 0, tiled=True)  21.1 us
    all_to_all x1, blocking collectives, local(): parts = lax.all_to_all(parts, ('z', 'c'), 0, 0, tiled=True)  20.3 us
    ppermute x4, starting transfers between devices, swap(): return lax.ppermute(value, 'c', [(0, 1), (1, 0)])  20.2 us
    all_to_all x1, blocking collectives, local(): gated = lax.all_to_all(gated, 'x', 0, 0, tiled=True)  15.9 us
    pallas_call x1, Pallas kernels, attention(): pl.pallas_call(functools.partial(attention_kernel, own_rows), grid_spec=p...  5.57 us
    ppermute x4, waiting for transfers between devices, swap(): return lax.ppermute(value, 'c', [(0, 1), (1, 0)])  4.6 us
  transfers between devices with their start and end apart: 8, of which 5 were waited for; matrix products, arithmetic and copies ran while one was open for 1% of the time, Pallas kernels for 5%

profile of v5, /device:TPU:1, one launch (start us, length us, event | category | flops | bytes accessed | tf_op | source)
XLA Modules:
  0.0 174.0 jit_solution(2517491737407756286)
XLA Ops:
  6.5 0.0 all-gather.3.cloned.1.call-start
  7.2 2.4 %pack.1 = (bf16[128,1024]{1,0:T(8,128)(2,1)}, bf16[272,1024]{1,0:T(8,128)(2,1)}, bf16[4,384,128]{2,1,0:T(8,128)(2,1)}, s32[4,128]{1,0:T(4,128)}) custom-call(s32[1,16]{1,0:T(1,128)} %lens_ref.1, s32[1]{0:T(128)S(6)} %copy.14.offset_ref, s32[12,1,16]{2,1,0:T(1,128)} %bitcast.38, s32[1,4]{1,0:T(1,128)} %shared_ref.1, bf16[256,128]{1,0:T(8,128)(2,1)} %out_ref.1, ...), custom_call_target="tpu_custom_call" | custom-call | tf_op jit(solution)/shard_map/pack/pallas_call | solution.py:246
  9.6 0.0 all-gather.3.cloned.1.call-update
  9.6 8.8 %collective-permute-start = (bf16[272,1024]{1,0:T(8,128)(2,1)}, bf16[272,1024]{1,0:T(8,128)(2,1)S(1)}, u32[]{:S(2)}, u32[]{:S(2)}) collective-permute-start(bf16[272,1024]{1,0:T(8,128)(2,1)} %get-tuple-element.21.own_key.own_value), channel_id=1, source_target_pairs={{0,1},{1,0},{2,3},{3,2},{4,5},{5,4},{6,7},{7,6},{8,9},{9,8},{10,11... | collective-permute-start | bytes 1671176 | tf_op jit(solution)/shard_map/ppermute | solution.py:445
  18.4 3.5 %all-to-all-start = ((bf16[4,384,128]{2,1,0:T(8,128)(2,1)}), bf16[4,384,128]{2,1,0:T(8,128)(2,1)S(1)}, u32[]{:S(2)}, u32[]{:S(2)}) async-start(bf16[4,384,128]{2,1,0:T(8,128)(2,1)} %get-tuple-element.23), calls=%async_computation | async-start | bytes 786432 | tf_op jit(solution)/shard_map/all_to_all | solution.py:483
  21.9 0.0 all-gather.5.cloned.1.call-start
  22.0 0.0 collective-permute-done.far_key.far_value
  22.0 0.0 copy-start.4
  22.0 0.8 copy-done.4
  22.8 5.6 %attention.1 = (bf16[8,272,128]{2,1,0:T(8,128)(2,1)}, f32[8,4096]{1,0:T(8,128)}) custom-call(s32[1]{0:T(128)} %bitcast.core_ref.place_ref.near_ref.half_ref, s32[1]{0:T(128)} %bitcast.1.mine_ref, s32[4,128]{1,0:T(4,128)} %get-tuple-element.20.limit_ref, bf16[1,128,4096]{2,1,0:T(8,128)(2,1)} %residual_ref.1, bf16[128,4096]{1,0:T(8,128)(2,1)} %bitcast.32, ...), custom_call_target="tpu_custom_call" | custom-call | tf_op jit(solution)/shard_map/attention/pallas_call | solution.py:141
  28.4 1.7 all-to-all-done
  30.1 0.0 copy-start.5
  30.1 21.1 %all_to_all.53.parts_ref = bf16[8,272,128]{2,1,0:T(8,128)(2,1)S(1)} all-to-all(bf16[8,272,128]{2,1,0:T(8,128)(2,1)} %get-tuple-element.24), channel_id=1, replica_groups=mesh['y'=8,'x'=4,'z'=8,'c'=2] {'z'}, dimensions={0} | all-to-all | bytes 1114112 | tf_op jit(solution)/shard_map/all_to_all | solution.py:488
  51.2 0.9 combine.1
  52.1 0.0 copy-start.2
  52.1 0.0 copy-start.3
  52.1 0.0 copy-done.5
  52.1 0.0 all-gather.5.cloned.1.call-update
  52.1 3.5 %all-to-all-start.2 = ((bf16[4,128,256]{2,1,0:T(8,128)(2,1)}), bf16[4,128,256]{2,1,0:T(8,128)(2,1)S(1)}, u32[]{:S(2)}, u32[]{:S(2)}) async-start(bf16[4,128,256]{2,1,0:T(8,128)(2,1)} %combine.1), calls=%async_computation.2 | async-start | bytes 524288 | tf_op jit(solution)/shard_map/all_to_all | solution.py:492
  55.7 0.0 all-gather.3.cloned.1.call-done.near_weights.far_weights
  55.7 1.1 slice.4.weights_ref
  56.8 0.0 copy-start.1
  56.8 4.4 %all-to-all-done.2 = bf16[4,128,256]{2,1,0:T(8,128)(2,1)S(1)} async-done(((bf16[4,128,256]{2,1,0:T(8,128)(2,1)}), bf16[4,128,256]{2,1,0:T(8,128)(2,1)S(1)}, u32[]{:S(2)}, u32[]{:S(2)}) %all-to-all-start.2) | async-done | bytes 262176 | tf_op jit(solution)/shard_map/all_to_all | solution.py:492
  61.2 1.0 out_product.2
  62.2 6.1 %collective-permute-start.1 = (bf16[512,512]{1,0:T(8,128)(2,1)S(1)}, bf16[512,512]{1,0:T(8,128)(2,1)S(1)}, u32[]{:S(2)}, u32[]{:S(2)}) collective-permute-start(bf16[512,512]{1,0:T(8,128)(2,1)S(1)} %out_product.2), channel_id=1, source_target_pairs={{0,1},{1,0},{2,3},{3,2},{4,5},{5,4},{6,7},{7,6},{8,9},{9,8},{10,11... | collective-permute-start | bytes 1572872 | tf_op jit(solution)/shard_map/ppermute | solution.py:445
  68.3 1.5 collective-permute-done.1.rest_0_
  69.8 1.2 out_product.3
  70.9 23.1 %all_to_all.54 = bf16[64,8,512]{2,1,0:T(8,128)(2,1)S(1)} all-to-all(bf16[64,8,512]{2,1,0:T(8,128)(2,1)S(1)} %bitcast.29), channel_id=1, replica_groups=mesh['y'=8,'x'=4,'z'=8,'c'=2] {'x','z','c'}, dimensions={0} | all-to-all | bytes 1048576 | tf_op jit(solution)/shard_map/all_to_all | solution.py:498
  94.0 0.0 copy-done.2
  94.0 0.0 copy-done.3
  94.0 0.2 add_and_norm.1
  94.2 23.4 %all_to_all.55 = bf16[64,8,512]{2,1,0:T(8,128)(2,1)S(1)} all-to-all(bf16[64,8,512]{2,1,0:T(8,128)(2,1)S(1)} %bitcast.30), channel_id=1, replica_groups=mesh['y'=8,'x'=4,'z'=8,'c'=2] {'x','z','c'}, dimensions={0} | all-to-all | bytes 1048576 | tf_op jit(solution)/shard_map/all_to_all | solution.py:501
  117.6 2.2 %collective-permute-start.2 = (bf16[512,512]{1,0:T(8,128)(2,1)S(1)}, bf16[512,512]{1,0:T(8,128)(2,1)S(1)}, u32[]{:S(2)}, u32[]{:S(2)}) collective-permute-start(bf16[512,512]{1,0:T(8,128)(2,1)S(1)} %bitcast.25), channel_id=1, source_target_pairs={{0,1},{1,0},{2,3},{3,2},{4,5},{5,4},{6,7},{7,6},{8,9},{9,8},{10,11... | collective-permute-start | bytes 1572872 | tf_op jit(solution)/shard_map/ppermute | solution.py:445
  119.8 1.6 collective-permute-done.2.far_rows
  121.4 0.0 all-gather.5.cloned.1.call-done.down_ref
  121.4 0.0 copy-done.1
  121.4 0.0 copy-start
  121.4 1.6 gate_product.1
  123.1 15.9 %all_to_all.56.parts_ref = bf16[4,128,768]{2,1,0:T(8,128)(2,1)S(1)} all-to-all(bf16[4,128,768]{2,1,0:T(8,128)(2,1)S(1)} %bitcast.22), channel_id=1, replica_groups=mesh['y'=8,'x'=4,'z'=8,'c'=2] {'x'}, dimensions={0} | all-to-all | bytes 1572864 | tf_op jit(solution)/shard_map/all_to_all | solution.py:507
  138.9 0.0 copy-done
  138.9 1.3 hidden_product.1
  140.2 3.2 %collective-permute-start.3 = (bf16[128,2048]{1,0:T(8,128)(2,1)S(1)}, bf16[128,2048]{1,0:T(8,128)(2,1)S(1)}, u32[]{:S(2)}, u32[]{:S(2)}) collective-permute-start(bf16[128,2048]{1,0:T(8,128)(2,1)S(1)} %get-tuple-element.34), channel_id=1, source_target_pairs={{0,1},{1,0},{2,3},{3,2},{4,5},{5,4},{6,7},{7,6},{8,9},{9,8},{10,11... | collective-permute-start | bytes 1572872 | tf_op jit(solution)/shard_map/ppermute | solution.py:445
  143.4 1.5 collective-permute-done.3.far_ref
  144.9 1.2 down_product.1
  146.1 20.3 %all_to_all.57 = bf16[16,8,2048]{2,1,0:T(8,128)(2,1)S(1)} all-to-all(bf16[16,8,2048]{2,1,0:T(8,128)(2,1)S(1)} %bitcast.27), channel_id=1, replica_groups=mesh['y'=8,'x'=4,'z'=8,'c'=2] {'z','c'}, dimensions={0} | all-to-all | bytes 1048576 | tf_op jit(solution)/shard_map/all_to_all | solution.py:511
  166.4 0.1 convert_reduce_fusion
  166.5 0.7 fusion
Async XLA Ops:
  6.5 49.2 %all-gather.3.cloned.1.call-start = ((), (), s32[]{:S(2)}) async-start(), calls=%async_computation.7 | async-start | bytes 2359296 | tf_op jit(solution)/shard_map/all_gather | solution.py:481
  9.6 12.3 %collective-permute-start = (bf16[272,1024]{1,0:T(8,128)(2,1)}, bf16[272,1024]{1,0:T(8,128)(2,1)S(1)}, u32[]{:S(2)}, u32[]{:S(2)}) collective-permute-start(bf16[272,1024]{1,0:T(8,128)(2,1)} %get-tuple-element.21.own_key.own_value), channel_id=1, source_target_pairs={{0,1},{1,0},{2,3},{3,2},{4,5},{5,4},{6,7},{7,6},{8,9},{9,8},{10,11... | collective-permute-start | bytes 1671176 | tf_op jit(solution)/shard_map/ppermute | solution.py:445
  18.4 11.7 %all-to-all-start = ((bf16[4,384,128]{2,1,0:T(8,128)(2,1)}), bf16[4,384,128]{2,1,0:T(8,128)(2,1)S(1)}, u32[]{:S(2)}, u32[]{:S(2)}) async-start(bf16[4,384,128]{2,1,0:T(8,128)(2,1)} %get-tuple-element.23), calls=%async_computation | async-start | bytes 786432 | tf_op jit(solution)/shard_map/all_to_all | solution.py:483
  21.9 99.5 %all-gather.5.cloned.1.call-start = ((), (), s32[]{:S(2)}) async-start(), calls=%async_computation.8 | async-start | bytes 3538944 | tf_op jit(solution)/shard_map/all_gather | solution.py:491
  22.0 0.8 copy-start.4
  30.1 22.0 %copy-start.5 = (bf16[4,384,128]{2,1,0:T(8,128)(2,1)}, bf16[4,384,128]{2,1,0:T(8,128)(2,1)S(1)}, u32[]{:S(2)}) copy-start(bf16[4,384,128]{2,1,0:T(8,128)(2,1)S(1)} %all-to-all-done) | copy-start | bytes 1179652
  52.1 41.9 %copy-start.2 = (f32[8,4096]{1,0:T(8,128)S(1)}, f32[8,4096]{1,0:T(8,128)}, u32[]{:S(2)}) copy-start(f32[8,4096]{1,0:T(8,128)} %get-tuple-element.26.residual_ref) | copy-start | bytes 393220
  52.1 41.9 %copy-start.3 = (f32[4096]{0:T(1024)S(1)}, f32[4096]{0:T(1024)}, u32[]{:S(2)}) copy-start(f32[4096]{0:T(1024)} %param.17) | copy-start | bytes 49156
  52.1 9.0 %all-to-all-start.2 = ((bf16[4,128,256]{2,1,0:T(8,128)(2,1)}), bf16[4,128,256]{2,1,0:T(8,128)(2,1)S(1)}, u32[]{:S(2)}, u32[]{:S(2)}) async-start(bf16[4,128,256]{2,1,0:T(8,128)(2,1)} %combine.1), calls=%async_computation.2 | async-start | bytes 524288 | tf_op jit(solution)/shard_map/all_to_all | solution.py:492
  56.8 64.6 %copy-start.1 = (bf16[1024,1024]{1,0:T(8,128)(2,1)S(1)}, bf16[1024,1024]{1,0:T(8,128)(2,1)}, u32[]{:S(2)}) copy-start(bf16[1024,1024]{1,0:T(8,128)(2,1)} %all-gather.3.cloned.1.call-done.near_weights.far_weights) | copy-start | bytes 6291460
  62.2 7.6 %collective-permute-start.1 = (bf16[512,512]{1,0:T(8,128)(2,1)S(1)}, bf16[512,512]{1,0:T(8,128)(2,1)S(1)}, u32[]{:S(2)}, u32[]{:S(2)}) collective-permute-start(bf16[512,512]{1,0:T(8,128)(2,1)S(1)} %out_product.2), channel_id=1, source_target_pairs={{0,1},{1,0},{2,3},{3,2},{4,5},{5,4},{6,7},{7,6},{8,9},{9,8},{10,11... | collective-permute-start | bytes 1572872 | tf_op jit(solution)/shard_map/ppermute | solution.py:445
  117.6 3.8 %collective-permute-start.2 = (bf16[512,512]{1,0:T(8,128)(2,1)S(1)}, bf16[512,512]{1,0:T(8,128)(2,1)S(1)}, u32[]{:S(2)}, u32[]{:S(2)}) collective-permute-start(bf16[512,512]{1,0:T(8,128)(2,1)S(1)} %bitcast.25), channel_id=1, source_target_pairs={{0,1},{1,0},{2,3},{3,2},{4,5},{5,4},{6,7},{7,6},{8,9},{9,8},{10,11... | collective-permute-start | bytes 1572872 | tf_op jit(solution)/shard_map/ppermute | solution.py:445
  121.4 17.5 %copy-start = (bf16[32,384,128]{2,1,0:T(8,128)(2,1)S(1)}, bf16[32,384,128]{2,1,0:T(8,128)(2,1)}, u32[]{:S(2)}) copy-start(bf16[32,384,128]{2,1,0:T(8,128)(2,1)} %all-gather.5.cloned.1.call-done.down_ref) | copy-start | bytes 9437188
  140.2 4.7 %collective-permute-start.3 = (bf16[128,2048]{1,0:T(8,128)(2,1)S(1)}, bf16[128,2048]{1,0:T(8,128)(2,1)S(1)}, u32[]{:S(2)}, u32[]{:S(2)}) collective-permute-start(bf16[128,2048]{1,0:T(8,128)(2,1)S(1)} %get-tuple-element.34), channel_id=1, source_target_pairs={{0,1},{1,0},{2,3},{3,2},{4,5},{5,4},{6,7},{7,6},{8,9},{9,8},{10,11... | collective-permute-start | bytes 1572872 | tf_op jit(solution)/shard_map/ppermute | solution.py:445
Sparse Core Ops, SparseCore 0:
  9.8 45.3 all-gather.2
  57.3 49.6 all-gather.4

commit v6 on v4

--- a/solution.py
+++ b/solution.py
@@ -361,13 +361,8 @@
 
 
 def times_down(hidden, down_ref):
-    return jnp.concatenate(
-        [
-            jnp.dot(hidden, down_ref[block], preferred_element_type=jnp.float32)
-            for block in range(down_ref.shape[0])
-        ],
-        axis=1,
-    )
+    blocks = jnp.concatenate([down_ref[block] for block in range(down_ref.shape[0])], axis=1)
+    return jnp.dot(hidden, blocks, preferred_element_type=jnp.float32)
 
 
 def hidden_kernel(half_ref, parts_ref, down_ref, hidden_ref, far_ref):

time: 175 us -> 175 us (level)
  no operation moved by 1% of the time
where the time goes in v6:
time: 175 us; the launch traced here: 174 us
  blocking collectives  103 us (59%)
  starting transfers between devices  27.1 us (15%)
  Pallas kernels  15.2 us (9%)
  between operations  14.2 us (8%)
  waiting for transfers between devices  10.7 us (6%)
  local copies, waits for them, and re-layouts  2.64 us (2%)
    all_to_all x1, blocking collectives, local(): lax.all_to_all(sent.reshape(x_size * ROWS, half * HEAD), ('x', 'z', 'c'),...  23.4 us
    all_to_all x1, blocking collectives, local(): parts = lax.all_to_all(parts, ('x', 'z', 'c'), 0, 0, tiled=True)  22.4 us
    all_to_all x1, blocking collectives, local(): parts = lax.all_to_all(parts, 'z', 0, 0, tiled=True)  21.1 us
    all_to_all x1, blocking collectives, local(): parts = lax.all_to_all(parts, ('z', 'c'), 0, 0, tiled=True)  20.3 us
    ppermute x4, starting transfers between devices, swap(): return lax.ppermute(value, 'c', [(0, 1), (1, 0)])  20.2 us
    all_to_all x1, blocking collectives, local(): gated = lax.all_to_all(gated, 'x', 0, 0, tiled=True)  15.9 us
    pallas_call x1, Pallas kernels, attention(): pl.pallas_call(functools.partial(attention_kernel, own_rows), grid_spec=p...  5.57 us
    ppermute x4, waiting for transfers between devices, swap(): return lax.ppermute(value, 'c', [(0, 1), (1, 0)])  4.56 us
  transfers between devices with their start and end apart: 8, of which 5 were waited for; matrix products, arithmetic and copies ran while one was open for 1% of the time, Pallas kernels for 5%

profile of v6, /device:TPU:1, one launch (start us, length us, event | category | flops | bytes accessed | tf_op | source)
XLA Modules:
  0.0 173.7 jit_solution(4977453715372082623)
XLA Ops:
  6.5 0.0 all-gather.3.cloned.1.call-start
  7.2 2.4 %pack.1 = (bf16[128,1024]{1,0:T(8,128)(2,1)}, bf16[272,1024]{1,0:T(8,128)(2,1)}, bf16[4,384,128]{2,1,0:T(8,128)(2,1)}, s32[4,128]{1,0:T(4,128)}) custom-call(s32[1,16]{1,0:T(1,128)} %lens_ref.1, s32[1]{0:T(128)S(6)} %copy.14.offset_ref, s32[12,1,16]{2,1,0:T(1,128)} %bitcast.38, s32[1,4]{1,0:T(1,128)} %shared_ref.1, bf16[256,128]{1,0:T(8,128)(2,1)} %out_ref.1, ...), custom_call_target="tpu_custom_call" | custom-call | tf_op jit(solution)/shard_map/pack/pallas_call | solution.py:246
  9.6 0.0 all-gather.3.cloned.1.call-update
  9.6 8.8 %collective-permute-start = (bf16[272,1024]{1,0:T(8,128)(2,1)}, bf16[272,1024]{1,0:T(8,128)(2,1)S(1)}, u32[]{:S(2)}, u32[]{:S(2)}) collective-permute-start(bf16[272,1024]{1,0:T(8,128)(2,1)} %get-tuple-element.20.own_key.own_value), channel_id=1, source_target_pairs={{0,1},{1,0},{2,3},{3,2},{4,5},{5,4},{6,7},{7,6},{8,9},{9,8},{10,11... | collective-permute-start | bytes 1671176 | tf_op jit(solution)/shard_map/ppermute | solution.py:440
  18.4 3.5 %all-to-all-start = ((bf16[4,384,128]{2,1,0:T(8,128)(2,1)}), bf16[4,384,128]{2,1,0:T(8,128)(2,1)S(1)}, u32[]{:S(2)}, u32[]{:S(2)}) async-start(bf16[4,384,128]{2,1,0:T(8,128)(2,1)} %get-tuple-element.22), calls=%async_computation | async-start | bytes 786432 | tf_op jit(solution)/shard_map/all_to_all | solution.py:478
  21.9 0.0 all-gather.5.cloned.1.call-start
  22.0 0.0 collective-permute-done.far_key.far_value
  22.0 0.0 copy-start.4
  22.0 0.8 copy-done.4
  22.8 5.6 %attention.1 = (bf16[8,272,128]{2,1,0:T(8,128)(2,1)}, f32[8,4096]{1,0:T(8,128)}) custom-call(s32[1]{0:T(128)} %bitcast.core_ref.place_ref.near_ref.half_ref, s32[1]{0:T(128)} %bitcast.1.mine_ref, s32[4,128]{1,0:T(4,128)} %get-tuple-element.19.limit_ref, bf16[1,128,4096]{2,1,0:T(8,128)(2,1)} %residual_ref.1, bf16[128,4096]{1,0:T(8,128)(2,1)} %bitcast.32, ...), custom_call_target="tpu_custom_call" | custom-call | tf_op jit(solution)/shard_map/attention/pallas_call | solution.py:141
  28.3 1.7 %all-to-all-done = bf16[4,384,128]{2,1,0:T(8,128)(2,1)S(1)} async-done(((bf16[4,384,128]{2,1,0:T(8,128)(2,1)}), bf16[4,384,128]{2,1,0:T(8,128)(2,1)S(1)}, u32[]{:S(2)}, u32[]{:S(2)}) %all-to-all-start) | async-done | bytes 393248 | tf_op jit(solution)/shard_map/all_to_all | solution.py:478
  30.1 0.0 copy-start.5
  30.1 0.7 copy-done.5
  30.8 0.0 all-gather.5.cloned.1.call-update
  30.9 21.1 %all_to_all.53.parts_ref = bf16[8,272,128]{2,1,0:T(8,128)(2,1)S(1)} all-to-all(bf16[8,272,128]{2,1,0:T(8,128)(2,1)} %get-tuple-element.23), channel_id=1, replica_groups=mesh['y'=8,'x'=4,'z'=8,'c'=2] {'z'}, dimensions={0} | all-to-all | bytes 1114112 | tf_op jit(solution)/shard_map/all_to_all | solution.py:484
  51.9 0.0 copy-start.2
  51.9 0.0 copy-start.3
  51.9 0.9 combine.1
  52.9 3.4 %all-to-all-start.2 = ((bf16[4,128,256]{2,1,0:T(8,128)(2,1)}), bf16[4,128,256]{2,1,0:T(8,128)(2,1)S(1)}, u32[]{:S(2)}, u32[]{:S(2)}) async-start(bf16[4,128,256]{2,1,0:T(8,128)(2,1)} %combine.1), calls=%async_computation.2 | async-start | bytes 524288 | tf_op jit(solution)/shard_map/all_to_all | solution.py:485
  56.3 0.0 all-gather.3.cloned.1.call-done.near_weights.far_weights
  56.3 1.1 slice.4.weights_ref
  57.4 0.0 copy-start.1
  57.4 4.4 %all-to-all-done.2 = bf16[4,128,256]{2,1,0:T(8,128)(2,1)S(1)} async-done(((bf16[4,128,256]{2,1,0:T(8,128)(2,1)}), bf16[4,128,256]{2,1,0:T(8,128)(2,1)S(1)}, u32[]{:S(2)}, u32[]{:S(2)}) %all-to-all-start.2) | async-done | bytes 262176 | tf_op jit(solution)/shard_map/all_to_all | solution.py:485
  61.8 1.0 out_product.2
  62.8 6.0 %collective-permute-start.1 = (bf16[512,512]{1,0:T(8,128)(2,1)S(1)}, bf16[512,512]{1,0:T(8,128)(2,1)S(1)}, u32[]{:S(2)}, u32[]{:S(2)}) collective-permute-start(bf16[512,512]{1,0:T(8,128)(2,1)S(1)} %out_product.2), channel_id=1, source_target_pairs={{0,1},{1,0},{2,3},{3,2},{4,5},{5,4},{6,7},{7,6},{8,9},{9,8},{10,11... | collective-permute-start | bytes 1572872 | tf_op jit(solution)/shard_map/ppermute | solution.py:440
  68.9 1.5 collective-permute-done.1.rest_0_
  70.4 1.2 out_product.3
  71.5 22.4 %all_to_all.54 = bf16[64,8,512]{2,1,0:T(8,128)(2,1)S(1)} all-to-all(bf16[64,8,512]{2,1,0:T(8,128)(2,1)S(1)} %bitcast.29), channel_id=1, replica_groups=mesh['y'=8,'x'=4,'z'=8,'c'=2] {'x','z','c'}, dimensions={0} | all-to-all | bytes 1048576 | tf_op jit(solution)/shard_map/all_to_all | solution.py:491
  94.0 0.0 copy-done.2
  94.0 0.0 copy-done.3
  94.0 0.2 add_and_norm.1
  94.2 23.4 %all_to_all.55 = bf16[64,8,512]{2,1,0:T(8,128)(2,1)S(1)} all-to-all(bf16[64,8,512]{2,1,0:T(8,128)(2,1)S(1)} %bitcast.30), channel_id=1, replica_groups=mesh['y'=8,'x'=4,'z'=8,'c'=2] {'x','z','c'}, dimensions={0} | all-to-all | bytes 1048576 | tf_op jit(solution)/shard_map/all_to_all | solution.py:494
  117.6 2.2 %collective-permute-start.2 = (bf16[512,512]{1,0:T(8,128)(2,1)S(1)}, bf16[512,512]{1,0:T(8,128)(2,1)S(1)}, u32[]{:S(2)}, u32[]{:S(2)}) collective-permute-start(bf16[512,512]{1,0:T(8,128)(2,1)S(1)} %bitcast.25), channel_id=1, source_target_pairs={{0,1},{1,0},{2,3},{3,2},{4,5},{5,4},{6,7},{7,6},{8,9},{9,8},{10,11... | collective-permute-start | bytes 1572872 | tf_op jit(solution)/shard_map/ppermute | solution.py:440
  119.8 0.0 all-gather.5.cloned.1.call-done.down_ref
  119.9 0.0 copy-start
  119.9 1.5 collective-permute-done.2.far_rows
  121.4 0.0 copy-done.1
  121.4 1.6 gate_product.1
  123.0 15.9 %all_to_all.56.parts_ref = bf16[4,128,768]{2,1,0:T(8,128)(2,1)S(1)} all-to-all(bf16[4,128,768]{2,1,0:T(8,128)(2,1)S(1)} %bitcast.22), channel_id=1, replica_groups=mesh['y'=8,'x'=4,'z'=8,'c'=2] {'x'}, dimensions={0} | all-to-all | bytes 1572864 | tf_op jit(solution)/shard_map/all_to_all | solution.py:500
  138.9 0.0 copy-done
  138.9 1.2 hidden_product.1
  140.1 3.2 %collective-permute-start.3 = (bf16[128,2048]{1,0:T(8,128)(2,1)S(1)}, bf16[128,2048]{1,0:T(8,128)(2,1)S(1)}, u32[]{:S(2)}, u32[]{:S(2)}) collective-permute-start(bf16[128,2048]{1,0:T(8,128)(2,1)S(1)} %get-tuple-element.32), channel_id=1, source_target_pairs={{0,1},{1,0},{2,3},{3,2},{4,5},{5,4},{6,7},{7,6},{8,9},{9,8},{10,11... | collective-permute-start | bytes 1572872 | tf_op jit(solution)/shard_map/ppermute | solution.py:440
  143.3 1.5 collective-permute-done.3.far_ref
  144.8 1.1 down_product.1
  145.9 20.3 %all_to_all.57 = bf16[16,8,2048]{2,1,0:T(8,128)(2,1)S(1)} all-to-all(bf16[16,8,2048]{2,1,0:T(8,128)(2,1)S(1)} %bitcast.27), channel_id=1, replica_groups=mesh['y'=8,'x'=4,'z'=8,'c'=2] {'z','c'}, dimensions={0} | all-to-all | bytes 1048576 | tf_op jit(solution)/shard_map/all_to_all | solution.py:504
  166.2 0.1 convert_reduce_fusion
  166.3 0.7 fusion
Async XLA Ops:
  6.5 49.8 %all-gather.3.cloned.1.call-start = ((), (), s32[]{:S(2)}) async-start(), calls=%async_computation.7 | async-start | bytes 2359296 | tf_op jit(solution)/shard_map/all_gather | solution.py:476
  9.6 12.3 %collective-permute-start = (bf16[272,1024]{1,0:T(8,128)(2,1)}, bf16[272,1024]{1,0:T(8,128)(2,1)S(1)}, u32[]{:S(2)}, u32[]{:S(2)}) collective-permute-start(bf16[272,1024]{1,0:T(8,128)(2,1)} %get-tuple-element.20.own_key.own_value), channel_id=1, source_target_pairs={{0,1},{1,0},{2,3},{3,2},{4,5},{5,4},{6,7},{7,6},{8,9},{9,8},{10,11... | collective-permute-start | bytes 1671176 | tf_op jit(solution)/shard_map/ppermute | solution.py:440
  18.4 11.7 %all-to-all-start = ((bf16[4,384,128]{2,1,0:T(8,128)(2,1)}), bf16[4,384,128]{2,1,0:T(8,128)(2,1)S(1)}, u32[]{:S(2)}, u32[]{:S(2)}) async-start(bf16[4,384,128]{2,1,0:T(8,128)(2,1)} %get-tuple-element.22), calls=%async_computation | async-start | bytes 786432 | tf_op jit(solution)/shard_map/all_to_all | solution.py:478
  21.9 97.9 %all-gather.5.cloned.1.call-start = ((), (), s32[]{:S(2)}) async-start(), calls=%async_computation.8 | async-start | bytes 3538944 | tf_op jit(solution)/shard_map/all_gather | solution.py:483
  22.0 0.8 copy-start.4
  30.1 0.7 copy-start.5
  51.9 42.0 %copy-start.2 = (f32[8,4096]{1,0:T(8,128)S(1)}, f32[8,4096]{1,0:T(8,128)}, u32[]{:S(2)}) copy-start(f32[8,4096]{1,0:T(8,128)} %get-tuple-element.25.residual_ref) | copy-start | bytes 393220
  51.9 42.0 %copy-start.3 = (f32[4096]{0:T(1024)S(1)}, f32[4096]{0:T(1024)}, u32[]{:S(2)}) copy-start(f32[4096]{0:T(1024)} %param.17) | copy-start | bytes 49156
  52.9 8.9 %all-to-all-start.2 = ((bf16[4,128,256]{2,1,0:T(8,128)(2,1)}), bf16[4,128,256]{2,1,0:T(8,128)(2,1)S(1)}, u32[]{:S(2)}, u32[]{:S(2)}) async-start(bf16[4,128,256]{2,1,0:T(8,128)(2,1)} %combine.1), calls=%async_computation.2 | async-start | bytes 524288 | tf_op jit(solution)/shard_map/all_to_all | solution.py:485
  57.4 64.0 %copy-start.1 = (bf16[1024,1024]{1,0:T(8,128)(2,1)S(1)}, bf16[1024,1024]{1,0:T(8,128)(2,1)}, u32[]{:S(2)}) copy-start(bf16[1024,1024]{1,0:T(8,128)(2,1)} %all-gather.3.cloned.1.call-done.near_weights.far_weights) | copy-start | bytes 6291460
  62.8 7.6 %collective-permute-start.1 = (bf16[512,512]{1,0:T(8,128)(2,1)S(1)}, bf16[512,512]{1,0:T(8,128)(2,1)S(1)}, u32[]{:S(2)}, u32[]{:S(2)}) collective-permute-start(bf16[512,512]{1,0:T(8,128)(2,1)S(1)} %out_product.2), channel_id=1, source_target_pairs={{0,1},{1,0},{2,3},{3,2},{4,5},{5,4},{6,7},{7,6},{8,9},{9,8},{10,11... | collective-permute-start | bytes 1572872 | tf_op jit(solution)/shard_map/ppermute | solution.py:440
  117.6 3.8 %collective-permute-start.2 = (bf16[512,512]{1,0:T(8,128)(2,1)S(1)}, bf16[512,512]{1,0:T(8,128)(2,1)S(1)}, u32[]{:S(2)}, u32[]{:S(2)}) collective-permute-start(bf16[512,512]{1,0:T(8,128)(2,1)S(1)} %bitcast.25), channel_id=1, source_target_pairs={{0,1},{1,0},{2,3},{3,2},{4,5},{5,4},{6,7},{7,6},{8,9},{9,8},{10,11... | collective-permute-start | bytes 1572872 | tf_op jit(solution)/shard_map/ppermute | solution.py:440
  119.9 19.1 %copy-start = (bf16[32,384,128]{2,1,0:T(8,128)(2,1)S(1)}, bf16[32,384,128]{2,1,0:T(8,128)(2,1)}, u32[]{:S(2)}) copy-start(bf16[32,384,128]{2,1,0:T(8,128)(2,1)} %all-gather.5.cloned.1.call-done.down_ref) | copy-start | bytes 9437188
  140.1 4.7 %collective-permute-start.3 = (bf16[128,2048]{1,0:T(8,128)(2,1)S(1)}, bf16[128,2048]{1,0:T(8,128)(2,1)S(1)}, u32[]{:S(2)}, u32[]{:S(2)}) collective-permute-start(bf16[128,2048]{1,0:T(8,128)(2,1)S(1)} %get-tuple-element.32), channel_id=1, source_target_pairs={{0,1},{1,0},{2,3},{3,2},{4,5},{5,4},{6,7},{7,6},{8,9},{9,8},{10,11... | collective-permute-start | bytes 1572872 | tf_op jit(solution)/shard_map/ppermute | solution.py:440
Sparse Core Ops, SparseCore 0:
  9.7 45.3 all-gather.2
  57.3 49.6 all-gather.4

commit v7 on v5

--- a/solution.py
+++ b/solution.py
@@ -390,7 +390,7 @@
 
 def hidden_product(half, parts, down):
     units = down.shape[1]
-    steps = 4 if down.shape[0] % 8 == 0 else 1
+    steps = 2 if down.shape[0] % 8 == 0 else 1
     width = down.shape[0] // 2 * HEAD
     return pl.pallas_call(
         hidden_kernel,
@@ -421,7 +421,7 @@
 
 
 def down_product(half, hidden, down, far):
-    steps = 4 if down.shape[0] % 8 == 0 else 1
+    steps = 2 if down.shape[0] % 8 == 0 else 1
     column = pl.BlockSpec((ROWS, far.shape[1] // steps), lambda i, half: (0, i))
     return pl.pallas_call(
         down_kernel,

time: 175 us -> 174 us (level)
  no operation moved by 1% of the time
where the time goes in v7:
time: 174 us; the launch traced here: 173 us
  blocking collectives  104 us (60%)
  starting transfers between devices  27.3 us (16%)
  Pallas kernels  14.7 us (8%)
  between operations  14.2 us (8%)
  waiting for transfers between devices  10.8 us (6%)
  local copies, waits for them, and re-layouts  1.91 us (1%)
    all_to_all x1, blocking collectives, local(): lax.all_to_all(sent.reshape(x_size * ROWS, half * HEAD), ('x', 'z', 'c'),...  23.4 us
    all_to_all x1, blocking collectives, local(): parts = lax.all_to_all(parts, ('x', 'z', 'c'), 0, 0, tiled=True)  23.1 us
    all_to_all x1, blocking collectives, local(): parts = lax.all_to_all(parts, 'z', 0, 0, tiled=True)  21.1 us
    all_to_all x1, blocking collectives, local(): parts = lax.all_to_all(parts, ('z', 'c'), 0, 0, tiled=True)  20.3 us
    ppermute x4, starting transfers between devices, swap(): return lax.ppermute(value, 'c', [(0, 1), (1, 0)])  20.2 us
    all_to_all x1, blocking collectives, local(): gated = lax.all_to_all(gated, 'x', 0, 0, tiled=True)  15.9 us
    pallas_call x1, Pallas kernels, attention(): pl.pallas_call(functools.partial(attention_kernel, own_rows), grid_spec=p...  5.57 us
    ppermute x4, waiting for transfers between devices, swap(): return lax.ppermute(value, 'c', [(0, 1), (1, 0)])  4.6 us
  transfers between devices with their start and end apart: 8, of which 5 were waited for; matrix products, arithmetic and copies ran while one was open for 1% of the time, Pallas kernels for 5%

profile of v7, /device:TPU:1, one launch (start us, length us, event | category | flops | bytes accessed | tf_op | source)
XLA Modules:
  0.0 173.3 jit_solution(11292896211467129654)
XLA Ops:
  6.5 0.0 all-gather.3.cloned.1.call-start
  7.2 2.4 %pack.1 = (bf16[128,1024]{1,0:T(8,128)(2,1)}, bf16[272,1024]{1,0:T(8,128)(2,1)}, bf16[4,384,128]{2,1,0:T(8,128)(2,1)}, s32[4,128]{1,0:T(4,128)}) custom-call(s32[1,16]{1,0:T(1,128)} %lens_ref.1, s32[1]{0:T(128)S(6)} %copy.14.offset_ref, s32[12,1,16]{2,1,0:T(1,128)} %bitcast.38, s32[1,4]{1,0:T(1,128)} %shared_ref.1, bf16[256,128]{1,0:T(8,128)(2,1)} %out_ref.1, ...), custom_call_target="tpu_custom_call" | custom-call | tf_op jit(solution)/shard_map/pack/pallas_call | solution.py:246
  9.6 0.0 all-gather.3.cloned.1.call-update
  9.6 8.8 %collective-permute-start = (bf16[272,1024]{1,0:T(8,128)(2,1)}, bf16[272,1024]{1,0:T(8,128)(2,1)S(1)}, u32[]{:S(2)}, u32[]{:S(2)}) collective-permute-start(bf16[272,1024]{1,0:T(8,128)(2,1)} %get-tuple-element.21.own_key.own_value), channel_id=1, source_target_pairs={{0,1},{1,0},{2,3},{3,2},{4,5},{5,4},{6,7},{7,6},{8,9},{9,8},{10,11... | collective-permute-start | bytes 1671176 | tf_op jit(solution)/shard_map/ppermute | solution.py:445
  18.4 3.5 %all-to-all-start = ((bf16[4,384,128]{2,1,0:T(8,128)(2,1)}), bf16[4,384,128]{2,1,0:T(8,128)(2,1)S(1)}, u32[]{:S(2)}, u32[]{:S(2)}) async-start(bf16[4,384,128]{2,1,0:T(8,128)(2,1)} %get-tuple-element.23), calls=%async_computation | async-start | bytes 786432 | tf_op jit(solution)/shard_map/all_to_all | solution.py:483
  21.9 0.0 all-gather.5.cloned.1.call-start
  22.0 0.0 collective-permute-done.far_key.far_value
  22.0 0.0 copy-start.4
  22.0 0.8 copy-done.4
  22.8 5.6 %attention.1 = (bf16[8,272,128]{2,1,0:T(8,128)(2,1)}, f32[8,4096]{1,0:T(8,128)}) custom-call(s32[1]{0:T(128)} %bitcast.core_ref.place_ref.near_ref.half_ref, s32[1]{0:T(128)} %bitcast.1.mine_ref, s32[4,128]{1,0:T(4,128)} %get-tuple-element.20.limit_ref, bf16[1,128,4096]{2,1,0:T(8,128)(2,1)} %residual_ref.1, bf16[128,4096]{1,0:T(8,128)(2,1)} %bitcast.32, ...), custom_call_target="tpu_custom_call" | custom-call | tf_op jit(solution)/shard_map/attention/pallas_call | solution.py:141
  28.4 1.7 all-to-all-done
  30.1 0.0 copy-start.5
  30.1 21.1 %all_to_all.53.parts_ref = bf16[8,272,128]{2,1,0:T(8,128)(2,1)S(1)} all-to-all(bf16[8,272,128]{2,1,0:T(8,128)(2,1)} %get-tuple-element.24), channel_id=1, replica_groups=mesh['y'=8,'x'=4,'z'=8,'c'=2] {'z'}, dimensions={0} | all-to-all | bytes 1114112 | tf_op jit(solution)/shard_map/all_to_all | solution.py:488
  51.2 0.9 combine.1
  52.1 0.0 copy-start.2
  52.1 0.0 copy-start.3
  52.1 0.0 copy-done.5
  52.1 0.0 all-gather.5.cloned.1.call-update
  52.1 3.5 %all-to-all-start.2 = ((bf16[4,128,256]{2,1,0:T(8,128)(2,1)}), bf16[4,128,256]{2,1,0:T(8,128)(2,1)S(1)}, u32[]{:S(2)}, u32[]{:S(2)}) async-start(bf16[4,128,256]{2,1,0:T(8,128)(2,1)} %combine.1), calls=%async_computation.2 | async-start | bytes 524288 | tf_op jit(solution)/shard_map/all_to_all | solution.py:492
  55.7 0.0 all-gather.3.cloned.1.call-done.near_weights.far_weights
  55.7 1.1 slice.4.weights_ref
  56.8 0.0 copy-start.1
  56.8 4.4 %all-to-all-done.2 = bf16[4,128,256]{2,1,0:T(8,128)(2,1)S(1)} async-done(((bf16[4,128,256]{2,1,0:T(8,128)(2,1)}), bf16[4,128,256]{2,1,0:T(8,128)(2,1)S(1)}, u32[]{:S(2)}, u32[]{:S(2)}) %all-to-all-start.2) | async-done | bytes 262176 | tf_op jit(solution)/shard_map/all_to_all | solution.py:492
  61.2 1.0 out_product.2
  62.2 6.1 %collective-permute-start.1 = (bf16[512,512]{1,0:T(8,128)(2,1)S(1)}, bf16[512,512]{1,0:T(8,128)(2,1)S(1)}, u32[]{:S(2)}, u32[]{:S(2)}) collective-permute-start(bf16[512,512]{1,0:T(8,128)(2,1)S(1)} %out_product.2), channel_id=1, source_target_pairs={{0,1},{1,0},{2,3},{3,2},{4,5},{5,4},{6,7},{7,6},{8,9},{9,8},{10,11... | collective-permute-start | bytes 1572872 | tf_op jit(solution)/shard_map/ppermute | solution.py:445
  68.3 1.5 collective-permute-done.1.rest_0_
  69.8 1.2 out_product.3
  70.9 23.1 %all_to_all.54 = bf16[64,8,512]{2,1,0:T(8,128)(2,1)S(1)} all-to-all(bf16[64,8,512]{2,1,0:T(8,128)(2,1)S(1)} %bitcast.29), channel_id=1, replica_groups=mesh['y'=8,'x'=4,'z'=8,'c'=2] {'x','z','c'}, dimensions={0} | all-to-all | bytes 1048576 | tf_op jit(solution)/shard_map/all_to_all | solution.py:498
  94.0 0.0 copy-done.2
  94.0 0.0 copy-done.3
  94.0 0.2 add_and_norm.1
  94.2 23.4 %all_to_all.55 = bf16[64,8,512]{2,1,0:T(8,128)(2,1)S(1)} all-to-all(bf16[64,8,512]{2,1,0:T(8,128)(2,1)S(1)} %bitcast.30), channel_id=1, replica_groups=mesh['y'=8,'x'=4,'z'=8,'c'=2] {'x','z','c'}, dimensions={0} | all-to-all | bytes 1048576 | tf_op jit(solution)/shard_map/all_to_all | solution.py:501
  117.6 2.2 %collective-permute-start.2 = (bf16[512,512]{1,0:T(8,128)(2,1)S(1)}, bf16[512,512]{1,0:T(8,128)(2,1)S(1)}, u32[]{:S(2)}, u32[]{:S(2)}) collective-permute-start(bf16[512,512]{1,0:T(8,128)(2,1)S(1)} %bitcast.25), channel_id=1, source_target_pairs={{0,1},{1,0},{2,3},{3,2},{4,5},{5,4},{6,7},{7,6},{8,9},{9,8},{10,11... | collective-permute-start | bytes 1572872 | tf_op jit(solution)/shard_map/ppermute | solution.py:445
  119.8 1.6 collective-permute-done.2.far_rows
  121.4 0.0 all-gather.5.cloned.1.call-done.down_ref
  121.4 0.0 copy-done.1
  121.4 0.0 copy-start
  121.4 1.6 gate_product.1
  123.1 15.9 %all_to_all.56.parts_ref = bf16[4,128,768]{2,1,0:T(8,128)(2,1)S(1)} all-to-all(bf16[4,128,768]{2,1,0:T(8,128)(2,1)S(1)} %bitcast.22), channel_id=1, replica_groups=mesh['y'=8,'x'=4,'z'=8,'c'=2] {'x'}, dimensions={0} | all-to-all | bytes 1572864 | tf_op jit(solution)/shard_map/all_to_all | solution.py:507
  138.9 0.0 copy-done
  138.9 0.9 hidden_product.1
  139.9 3.2 %collective-permute-start.3 = (bf16[128,2048]{1,0:T(8,128)(2,1)S(1)}, bf16[128,2048]{1,0:T(8,128)(2,1)S(1)}, u32[]{:S(2)}, u32[]{:S(2)}) collective-permute-start(bf16[128,2048]{1,0:T(8,128)(2,1)S(1)} %get-tuple-element.34), channel_id=1, source_target_pairs={{0,1},{1,0},{2,3},{3,2},{4,5},{5,4},{6,7},{7,6},{8,9},{9,8},{10,11... | collective-permute-start | bytes 1572872 | tf_op jit(solution)/shard_map/ppermute | solution.py:445
  143.1 1.5 collective-permute-done.3.far_ref
  144.6 0.9 down_product.1
  145.5 20.3 %all_to_all.57 = bf16[16,8,2048]{2,1,0:T(8,128)(2,1)S(1)} all-to-all(bf16[16,8,2048]{2,1,0:T(8,128)(2,1)S(1)} %bitcast.27), channel_id=1, replica_groups=mesh['y'=8,'x'=4,'z'=8,'c'=2] {'z','c'}, dimensions={0} | all-to-all | bytes 1048576 | tf_op jit(solution)/shard_map/all_to_all | solution.py:511
  165.8 0.1 convert_reduce_fusion
  165.8 0.7 fusion
Async XLA Ops:
  6.5 49.2 %all-gather.3.cloned.1.call-start = ((), (), s32[]{:S(2)}) async-start(), calls=%async_computation.7 | async-start | bytes 2359296 | tf_op jit(solution)/shard_map/all_gather | solution.py:481
  9.6 12.3 %collective-permute-start = (bf16[272,1024]{1,0:T(8,128)(2,1)}, bf16[272,1024]{1,0:T(8,128)(2,1)S(1)}, u32[]{:S(2)}, u32[]{:S(2)}) collective-permute-start(bf16[272,1024]{1,0:T(8,128)(2,1)} %get-tuple-element.21.own_key.own_value), channel_id=1, source_target_pairs={{0,1},{1,0},{2,3},{3,2},{4,5},{5,4},{6,7},{7,6},{8,9},{9,8},{10,11... | collective-permute-start | bytes 1671176 | tf_op jit(solution)/shard_map/ppermute | solution.py:445
  18.4 11.7 %all-to-all-start = ((bf16[4,384,128]{2,1,0:T(8,128)(2,1)}), bf16[4,384,128]{2,1,0:T(8,128)(2,1)S(1)}, u32[]{:S(2)}, u32[]{:S(2)}) async-start(bf16[4,384,128]{2,1,0:T(8,128)(2,1)} %get-tuple-element.23), calls=%async_computation | async-start | bytes 786432 | tf_op jit(solution)/shard_map/all_to_all | solution.py:483
  21.9 99.5 %all-gather.5.cloned.1.call-start = ((), (), s32[]{:S(2)}) async-start(), calls=%async_computation.8 | async-start | bytes 3538944 | tf_op jit(solution)/shard_map/all_gather | solution.py:491
  22.0 0.8 copy-start.4
  30.1 22.0 %copy-start.5 = (bf16[4,384,128]{2,1,0:T(8,128)(2,1)}, bf16[4,384,128]{2,1,0:T(8,128)(2,1)S(1)}, u32[]{:S(2)}) copy-start(bf16[4,384,128]{2,1,0:T(8,128)(2,1)S(1)} %all-to-all-done) | copy-start | bytes 1179652
  52.1 41.9 %copy-start.2 = (f32[8,4096]{1,0:T(8,128)S(1)}, f32[8,4096]{1,0:T(8,128)}, u32[]{:S(2)}) copy-start(f32[8,4096]{1,0:T(8,128)} %get-tuple-element.26.residual_ref) | copy-start | bytes 393220
  52.1 41.9 %copy-start.3 = (f32[4096]{0:T(1024)S(1)}, f32[4096]{0:T(1024)}, u32[]{:S(2)}) copy-start(f32[4096]{0:T(1024)} %param.17) | copy-start | bytes 49156
  52.1 9.0 %all-to-all-start.2 = ((bf16[4,128,256]{2,1,0:T(8,128)(2,1)}), bf16[4,128,256]{2,1,0:T(8,128)(2,1)S(1)}, u32[]{:S(2)}, u32[]{:S(2)}) async-start(bf16[4,128,256]{2,1,0:T(8,128)(2,1)} %combine.1), calls=%async_computation.2 | async-start | bytes 524288 | tf_op jit(solution)/shard_map/all_to_all | solution.py:492
  56.8 64.6 %copy-start.1 = (bf16[1024,1024]{1,0:T(8,128)(2,1)S(1)}, bf16[1024,1024]{1,0:T(8,128)(2,1)}, u32[]{:S(2)}) copy-start(bf16[1024,1024]{1,0:T(8,128)(2,1)} %all-gather.3.cloned.1.call-done.near_weights.far_weights) | copy-start | bytes 6291460
  62.2 7.6 %collective-permute-start.1 = (bf16[512,512]{1,0:T(8,128)(2,1)S(1)}, bf16[512,512]{1,0:T(8,128)(2,1)S(1)}, u32[]{:S(2)}, u32[]{:S(2)}) collective-permute-start(bf16[512,512]{1,0:T(8,128)(2,1)S(1)} %out_product.2), channel_id=1, source_target_pairs={{0,1},{1,0},{2,3},{3,2},{4,5},{5,4},{6,7},{7,6},{8,9},{9,8},{10,11... | collective-permute-start | bytes 1572872 | tf_op jit(solution)/shard_map/ppermute | solution.py:445
  117.6 3.8 %collective-permute-start.2 = (bf16[512,512]{1,0:T(8,128)(2,1)S(1)}, bf16[512,512]{1,0:T(8,128)(2,1)S(1)}, u32[]{:S(2)}, u32[]{:S(2)}) collective-permute-start(bf16[512,512]{1,0:T(8,128)(2,1)S(1)} %bitcast.25), channel_id=1, source_target_pairs={{0,1},{1,0},{2,3},{3,2},{4,5},{5,4},{6,7},{7,6},{8,9},{9,8},{10,11... | collective-permute-start | bytes 1572872 | tf_op jit(solution)/shard_map/ppermute | solution.py:445
  121.4 17.5 %copy-start = (bf16[32,384,128]{2,1,0:T(8,128)(2,1)S(1)}, bf16[32,384,128]{2,1,0:T(8,128)(2,1)}, u32[]{:S(2)}) copy-start(bf16[32,384,128]{2,1,0:T(8,128)(2,1)} %all-gather.5.cloned.1.call-done.down_ref) | copy-start | bytes 9437188
  139.9 4.7 %collective-permute-start.3 = (bf16[128,2048]{1,0:T(8,128)(2,1)S(1)}, bf16[128,2048]{1,0:T(8,128)(2,1)S(1)}, u32[]{:S(2)}, u32[]{:S(2)}) collective-permute-start(bf16[128,2048]{1,0:T(8,128)(2,1)S(1)} %get-tuple-element.34), channel_id=1, source_target_pairs={{0,1},{1,0},{2,3},{3,2},{4,5},{5,4},{6,7},{7,6},{8,9},{9,8},{10,11... | collective-permute-start | bytes 1572872 | tf_op jit(solution)/shard_map/ppermute | solution.py:445
Sparse Core Ops, SparseCore 0:
  9.8 45.3 all-gather.2
  57.3 49.6 all-gather.4
